TPU v7x, 32 devices: a whole 2x2x4 slice. The times are simulated.
32 devices in a mesh: zonal: 4 (over y, x), deg: 8 (over z, core).
Axes of the slice: x: 2, y: 2, z: 4, core: 2. Of those that a mesh axis runs over, the one named last changes fastest.
Arguments:
- spectral: bfloat16 [128, 2560, 128], P('zonal', 'deg'), may hold values from -6 to 6
- wavenumbers: int32 [128], P('zonal'), may hold values from 0 to 2559, as said below
- compress: bfloat16 [128, 2560, 128], P('zonal', 'deg'), may hold values from -0.3125 to 0.3125
- section_own: bfloat16 [2, 128, 8, 128, 128], P(None, 'zonal', 'deg'), may hold values from -0.375 to 0.375
- section_peer: bfloat16 [2, 128, 8, 128, 128], P(None, 'zonal', 'deg'), may hold values from -0.375 to 0.375
- expand: bfloat16 [128, 8, 640, 128], P('zonal', 'deg'), may hold values from -0.5 to 0.5
- block_ranks: int32 [3, 8], replicated, may hold values from 64 to 128, as said below
Outputs:
- fourier_rows: bfloat16 [128, 8, 4, 80, 128], P(None, 'deg', 'zonal')
Inputs may be any that keep to these rules, and one draw needn't show every extreme that they name: Distinct wavenumbers, sorted and dealt to the 4 groups of 32 slots in rounds of 8: one slot to each group going forward through the groups, then one to each going backward; 0 and 2559 always appear. block_ranks[s, g] is the live rank of block g after section s; in each section some block has rank 128.
All inputs are finite; a program needn't handle non-finite values.
Results may differ from a plain program's by a relative error of at most 0.008.
Values may be sent and summed in bfloat16 or wider, within the bound.
No kernel may reach another device: no remote copies, remote signals or barrier semaphores. Data moves between devices by JAX's collectives and lax.ppermute only.
A program may use at most 128 MiB of HBM per device.

v0:
```python
import jax
import jax.numpy as jnp
from jax import lax
from jax.sharding import PartitionSpec as P

SECTIONS = 2


def from_partner(array, axis, bit):
    return lax.ppermute(array, axis, [(i, i ^ 1 << bit) for i in range(lax.axis_size(axis))])


def split_halves(holding, which_dim, my_bit):
    first_half = lax.index_in_dim(holding, 0, which_dim, keepdims=False)
    second_half = lax.index_in_dim(holding, 1, which_dim, keepdims=False)
    kept_half = jnp.where(my_bit == 0, first_half, second_half)
    given_half = jnp.where(my_bit == 0, second_half, first_half)
    return (kept_half, given_half)


def body(spectral, wavenumbers, compress, section_own, section_peer, expand, block_ranks):
    deg_count = lax.axis_size("deg")
    deg_index = lax.axis_index("deg")
    levels_total = deg_count.bit_length() - 1
    low_bits = levels_total - SECTIONS
    block_size = spectral.shape[1]
    rank_width = compress.shape[2]
    column_count = spectral.shape[2]
    degree_ids = deg_index * block_size + jnp.arange(block_size, dtype=jnp.int32)
    live_mask = degree_ids[None, :] >= wavenumbers[:, None]
    masked_rows = jnp.where(live_mask[:, :, None], spectral, jnp.zeros_like(spectral))
    rank_depths = jnp.arange(rank_width, dtype=jnp.int32)

    def rank_keep(section_ordinal):
        return (rank_depths < block_ranks[section_ordinal, deg_index]).astype(jnp.float32)[
            None, :, None
        ]

    merged_result = jnp.einsum(
        "mnk,mnc->mkc", compress, masked_rows, preferred_element_type=jnp.float32
    )
    vector = (merged_result * rank_keep(0)).astype(jnp.bfloat16)
    for section_ordinal in range(1, SECTIONS + 1):
        counterpart = from_partner(vector, "deg", levels_total - section_ordinal)
        merged_result = jnp.einsum(
            "mkl,mlc->mkc",
            section_own[section_ordinal - 1, :, 0],
            vector,
            preferred_element_type=jnp.float32,
        )
        merged_result = merged_result + jnp.einsum(
            "mkl,mlc->mkc",
            section_peer[section_ordinal - 1, :, 0],
            counterpart,
            preferred_element_type=jnp.float32,
        )
        vector = (merged_result * rank_keep(section_ordinal)).astype(jnp.bfloat16)
    expansion = expand[:, 0]
    slot_count = expansion.shape[0]
    quarter_rows = expansion.shape[1]
    band_size = quarter_rows >> low_bits
    bit_order = list(range(low_bits - 1, -1, -1))
    remaining = list(range(low_bits - 1, -1, -1))
    holding = jnp.einsum("mrk,mkc->mrc", expansion, vector, preferred_element_type=jnp.float32)
    holding = holding.reshape((slot_count,) + (2,) * low_bits + (band_size, column_count))
    for bit_number in bit_order:
        which_dim = 1 + len([other for other in remaining if other > bit_number])
        my_bit = deg_index >> bit_number & 1
        kept_half, given_half = split_halves(holding, which_dim, my_bit)
        holding = kept_half + from_partner(given_half, "deg", bit_number)
        remaining = [other for other in remaining if other != bit_number]
    rounded = holding.astype(jnp.bfloat16)
    gathered = lax.all_to_all(rounded, "zonal", split_axis=1, concat_axis=0, tiled=True)
    return gathered.reshape(gathered.shape[0], 1, 1, gathered.shape[1], gathered.shape[2])


def solution(mesh):
    in_specs = (
        P("zonal", "deg", None),
        P("zonal"),
        P("zonal", "deg", None),
        P(None, "zonal", "deg", None, None),
        P(None, "zonal", "deg", None, None),
        P("zonal", "deg", None, None),
        P(),
    )
    out_specs = P(None, "deg", "zonal", None, None)
    return jax.shard_map(body, mesh=mesh, in_specs=in_specs, out_specs=out_specs, check_vma=False)
```

profile of v0, /device:TPU:0, one launch (start us, length us, event | category | flops | bytes accessed | tf_op | source)
XLA Modules:
  0.0 165.0 jit_solution(12686229388814999584)
XLA Ops:
  0.0 0.0 copy-start
  0.0 1.5 constant_dynamic-slice_fusion
  1.5 0.6 compare_convert_fusion.2
  2.1 0.7 broadcast_compare_fusion
  2.8 0.0 copy-done
  2.8 0.0 copy-start.3
  2.9 4.8 %multiply_convert_fusion.2 = bf16[32,128,128]{2,1,0:T(8,128)(2,1)S(1)} fusion(bf16[32,320,128]{2,1,0:T(8,128)(2,1)S(1)} %copy-done, bf16[32,320,128]{2,1,0:T(8,128)(2,1)} %param.7, pred[32,320]{1,0:T(8,128)(4,1)S(1)} %broadcast_compare_fusion, f32[128]{0:T(128)S(1)} %compare_convert_fusion.2), kind=kOutput, calls=%fused_computation.11 | convolution fusion | flops 337903616 | bytes 6302208 | tf_op jit(solution)/shard_map/mnk,mnc->mkc/dot_general | solution.py:39
  7.6 0.0 copy-start.2
  7.7 4.1 %collective-permute-start = (bf16[32,128,128]{1,2,0:T(8,128)(2,1)S(1)}, bf16[32,128,128]{1,2,0:T(8,128)(2,1)S(1)}, u32[]{:S(2)}, u32[]{:S(2)}) collective-permute-start(bf16[32,128,128]{1,2,0:T(8,128)(2,1)S(1)} %bitcast.54), channel_id=1, source_target_pairs={{0,4},{1,5},{2,6},{3,7},{4,0},{5,1},{6,2},{7,3},{8,12},{9,13},{10,... | collective-permute-start | bytes 3145736 | tf_op jit(solution)/shard_map/ppermute | solution.py:10
  11.8 0.7 compare_convert_fusion.1
  12.4 0.0 copy-done.3
  12.5 0.8 fusion.13
  13.3 44.1 %collective-permute-done = bf16[32,128,128]{1,2,0:T(8,128)(2,1)S(1)} collective-permute-done((bf16[32,128,128]{1,2,0:T(8,128)(2,1)S(1)}, bf16[32,128,128]{1,2,0:T(8,128)(2,1)S(1)}, u32[]{:S(2)}, u32[]{:S(2)}) %collective-permute-start) | collective-permute-done | bytes 1048608 | tf_op jit(solution)/shard_map/ppermute | solution.py:10
  57.4 0.0 copy-done.2
  57.4 1.8 %multiply_convert_fusion.1 = bf16[32,128,128]{2,1,0:T(8,128)(2,1)} fusion(f32[32,128,128]{2,1,0:T(8,128)S(1)} %fusion.13, bf16[32,128,128]{1,2,0:T(8,128)(2,1)S(1)} %collective-permute-done, bf16[2,32,1,128,128]{4,3,1,2,0:T(8,128)(2,1)S(1)} %bitcast.51, f32[128]{0:T(128)S(1)} %compare_convert_fusion.1), kind=kOutput, calls=%fused_computation.10 | convolution fusion | flops 135790592 | bytes 5243392 | tf_op jit(solution)/shard_map/mkl,mlc->mkc/dot_general | solution.py:51
  59.2 0.7 collective-permute-start.1
  59.9 0.6 compare_convert_fusion
  60.6 3.7 %fusion.12 = f32[32,128,128]{2,1,0:T(8,128)} fusion(bf16[32,128,128]{2,1,0:T(8,128)(2,1)} %multiply_convert_fusion.1, bf16[2,32,1,128,128]{4,3,1,2,0:T(8,128)(2,1)} %bitcast.52), kind=kOutput, calls=%fused_computation.15 | convolution fusion | flops 134217728 | bytes 4194304 | tf_op jit(solution)/shard_map/mkl,mlc->mkc/dot_general | solution.py:45
  64.3 19.6 %collective-permute-done.1 = bf16[32,128,128]{1,2,0:T(8,128)(2,1)} collective-permute-done((bf16[32,128,128]{1,2,0:T(8,128)(2,1)}, bf16[32,128,128]{1,2,0:T(8,128)(2,1)}, u32[]{:S(2)}, u32[]{:S(2)}) %collective-permute-start.1) | collective-permute-done | bytes 1048608 | tf_op jit(solution)/shard_map/ppermute | solution.py:10
  83.9 10.4 %fusion.3 = f32[32,640,128]{1,2,0:T(8,128)} fusion(bf16[32,1,640,128]{3,2,1,0:T(8,128)(2,1)} %param.12, f32[32,128,128]{2,1,0:T(8,128)} %fusion.12, bf16[32,128,128]{1,2,0:T(8,128)(2,1)} %collective-permute-done.1, bf16[2,32,1,128,128]{4,3,1,2,0:T(8,128)(2,1)} %bitcast.50, f32[128]{0:T(128)S(1)} %compare_convert_fusion), kind=kOutput, calls=%fused_computation.5 | convolution fusion | flops 806879232 | bytes 19923456 | tf_op jit(solution)/shard_map/mrk,mkc->mrc/dot_general | solution.py:64
  94.3 11.2 %copy.29 = f32[32,640,128]{2,1,0:T(8,128)} copy(f32[32,640,128]{1,2,0:T(8,128)} %fusion.3) | data formatting | bytes 20971520 | tf_op jit(solution)/shard_map/mrk,mkc->mrc/dot_general | solution.py:64
  105.5 0.0 copy-start.1
  105.5 4.8 %select_bitcast_fusion = f32[32,320,128]{2,1,0:T(8,128)S(1)} fusion(f32[32,2,320,128]{3,2,1,0:T(8,128)} %bitcast.47, pred[]{:T(512)S(6)} %eq.4), kind=kLoop, calls=%fused_computation.4 | loop fusion | flops 1310720 | bytes 15728641 | tf_op jit(solution)/shard_map/jit(_where)/select_n | solution.py:17
  110.3 0.1 collective-permute-start.2
  110.4 8.8 %collective-permute-done.2 = f32[32,320,128]{2,1,0:T(8,128)} collective-permute-done((f32[32,320,128]{2,1,0:T(8,128)S(1)}, f32[32,320,128]{2,1,0:T(8,128)}, u32[]{:S(2)}, u32[]{:S(2)}) %collective-permute-start.2) | collective-permute-done | bytes 5242912 | tf_op jit(solution)/shard_map/ppermute | solution.py:10
  119.1 0.0 copy-done.1
  119.1 5.4 %fusion = bf16[32,320,128]{2,1,0:T(8,128)(2,1)} fusion(f32[32,320,128]{2,1,0:T(8,128)} %collective-permute-done.2, f32[32,2,320,128]{3,2,1,0:T(8,128)S(1)} %bitcast.48, pred[]{:T(512)S(6)} %eq.4), kind=kLoop, calls=%fused_computation.1 | loop fusion | flops 3932160 | bytes 18350080 | tf_op jit(solution)/shard_map/convert_element_type | solution.py:72
  124.5 3.4 %copy.30 = bf16[32,320,128]{2,0,1:T(8,128)(2,1)S(1)} copy(bf16[32,320,128]{2,1,0:T(8,128)(2,1)} %fusion) | data formatting | bytes 5242880 | tf_op jit(solution)/shard_map/convert_element_type | solution.py:72
  127.9 34.6 %all_to_all.15 = bf16[32,320,128]{2,0,1:T(8,128)(2,1)S(1)} all-to-all(bf16[32,320,128]{2,0,1:T(8,128)(2,1)S(1)} %copy.30), channel_id=1, replica_groups=mesh['zonal'=4,'deg'=8] {'zonal'}, dimensions={1} | all-to-all | bytes 5242880 | tf_op jit(solution)/shard_map/all_to_all | solution.py:73
  162.5 2.5 %copy.32 = bf16[4,32,80,128]{3,2,1,0:T(8,128)(2,1)} copy(bf16[4,32,80,128]{3,1,2,0:T(8,128)(2,1)S(1)} %bitcast.49) | data formatting | bytes 5242880 | tf_op jit(solution)/shard_map/all_to_all | solution.py:73
  (1 shorter events, 0.0 us)
Async XLA Ops:
  0.0 2.8 %copy-start = (bf16[32,320,128]{2,1,0:T(8,128)(2,1)S(1)}, bf16[32,320,128]{2,1,0:T(8,128)(2,1)}, u32[]{:S(2)}) copy-start(bf16[32,320,128]{2,1,0:T(8,128)(2,1)} %param.9) | copy-start | bytes 7864324
  2.8 9.6 %copy-start.3 = (bf16[2,32,1,128,128]{4,3,2,1,0:T(8,128)(2,1)S(1)}, bf16[2,32,1,128,128]{4,3,2,1,0:T(8,128)(2,1)}, u32[]{:S(2)}) copy-start(bf16[2,32,1,128,128]{4,3,2,1,0:T(8,128)(2,1)} %param.10) | copy-start | bytes 6291460
  7.6 49.7 %copy-start.2 = (bf16[2,32,1,128,128]{4,3,2,1,0:T(8,128)(2,1)S(1)}, bf16[2,32,1,128,128]{4,3,2,1,0:T(8,128)(2,1)}, u32[]{:S(2)}) copy-start(bf16[2,32,1,128,128]{4,3,2,1,0:T(8,128)(2,1)} %param.11) | copy-start | bytes 6291460
  7.7 49.7 %collective-permute-start = (bf16[32,128,128]{1,2,0:T(8,128)(2,1)S(1)}, bf16[32,128,128]{1,2,0:T(8,128)(2,1)S(1)}, u32[]{:S(2)}, u32[]{:S(2)}) collective-permute-start(bf16[32,128,128]{1,2,0:T(8,128)(2,1)S(1)} %bitcast.54), channel_id=1, source_target_pairs={{0,4},{1,5},{2,6},{3,7},{4,0},{5,1},{6,2},{7,3},{8,12},{9,13},{10,... | collective-permute-start | bytes 3145736 | tf_op jit(solution)/shard_map/ppermute | solution.py:10
  59.2 24.7 %collective-permute-start.1 = (bf16[32,128,128]{1,2,0:T(8,128)(2,1)}, bf16[32,128,128]{1,2,0:T(8,128)(2,1)}, u32[]{:S(2)}, u32[]{:S(2)}) collective-permute-start(bf16[32,128,128]{1,2,0:T(8,128)(2,1)} %bitcast.9), channel_id=1, source_target_pairs={{0,2},{1,3},{2,0},{3,1},{4,6},{5,7},{6,4},{7,5},{8,10},{9,11},{10,... | collective-permute-start | bytes 3145736 | tf_op jit(solution)/shard_map/ppermute | solution.py:10
  105.5 13.7 %copy-start.1 = (f32[32,640,128]{2,1,0:T(8,128)S(1)}, f32[32,640,128]{2,1,0:T(8,128)}, u32[]{:S(2)}) copy-start(f32[32,640,128]{2,1,0:T(8,128)} %copy.29) | copy-start | bytes 31457284
  110.3 8.9 %collective-permute-start.2 = (f32[32,320,128]{2,1,0:T(8,128)S(1)}, f32[32,320,128]{2,1,0:T(8,128)}, u32[]{:S(2)}, u32[]{:S(2)}) collective-permute-start(f32[32,320,128]{2,1,0:T(8,128)S(1)} %select_bitcast_fusion), channel_id=1, source_target_pairs={{0,1},{1,0},{2,3},{3,2},{4,5},{5,4},{6,7},{7,6},{8,9},{9,8},{10,11... | collective-permute-start | bytes 15728648 | tf_op jit(solution)/shard_map/ppermute | solution.py:10
where the time goes:
time: 166 us; the launch traced here: 165 us
  waiting for transfers between devices  72.4 us (44%)
  blocking collectives  34.6 us (21%)
  matrix products  21.5 us (13%)
  local copies, waits for them, and re-layouts  18.7 us (11%)
  other arithmetic  12.8 us (8%)
  starting transfers between devices  4.9 us (3%)
    ppermute x3, waiting for transfers between devices, from_partner(): lax.ppermute(array, axis, [(i, i ^ 1 << bit) for i in range(lax.axis_size...  72.4 us
    all_to_all x1, blocking collectives, body(): lax.all_to_all(rounded, 'zonal', split_axis=1, concat_axis=0, tiled=True)  34.6 us
    dot_general x1, local copies, waits for them, and re-layouts, body(): jnp.einsum('mrk,mkc->mrc', expansion, vector, preferred_element_type=jnp....  11.2 us
    dot_general x1, matrix products, body(): jnp.einsum('mrk,mkc->mrc', expansion, vector, preferred_element_type=jnp....  10.4 us
    convert_element_type x1, other arithmetic, body(): rounded = holding.astype(jnp.bfloat16)  5.37 us
    ppermute x3, starting transfers between devices, from_partner(): lax.ppermute(array, axis, [(i, i ^ 1 << bit) for i in range(lax.axis_size...  4.9 us
    select_n x1, other arithmetic, split_halves(): given_half = jnp.where(my_bit == 0, second_half, first_half)  4.81 us
    dot_general x1, matrix products, body(): jnp.einsum('mnk,mnc->mkc', compress, masked_rows, preferred_element_type=...  4.78 us
  transfers between devices with their start and end apart: 3, of which 3 were waited for; matrix products, arithmetic and copies ran while one was open for 4% of the time, Pallas kernels for 0%

commit v1 on v0

v1 whole, which is shorter than its diff:
```python
import functools

import jax
import jax.numpy as jnp
from jax import lax
from jax.experimental import pallas as pl
from jax.experimental.pallas import tpu as pltpu
from jax.sharding import PartitionSpec as P

SECTIONS = 2
CHUNKS = (8, 8, 8, 4, 4)
VMEM_LIMIT = 32 * 2**20


def from_partner(array, axis, offset):
    pairs = [(i, i ^ offset) for i in range(lax.axis_size(axis))]
    return lax.ppermute(array, axis, pairs)


def dot(a, b, contract_a=1):
    return lax.dot_general(
        a, b, (((contract_a,), (0,)), ((), ())), preferred_element_type=jnp.float32
    )


def call(kernel, name, scalars, operands, in_specs, out_specs, out_shape, steps, flops):
    outs = out_shape if isinstance(out_shape, (list, tuple)) else [out_shape]
    moved = sum(o.size * o.dtype.itemsize for o in outs) + flops // 128
    return pl.pallas_call(
        kernel,
        out_shape=out_shape,
        grid_spec=pltpu.PrefetchScalarGridSpec(
            num_scalar_prefetch=len(scalars),
            grid=(steps,),
            in_specs=in_specs,
            out_specs=out_specs,
        ),
        compiler_params=pltpu.CompilerParams(vmem_limit_bytes=VMEM_LIMIT),
        cost_estimate=pl.CostEstimate(flops=flops, bytes_accessed=moved, transcendentals=0),
        name=name,
    )(*scalars, *operands)


def group(count):
    return max(b for b in (4, 2, 1) if count % b == 0)


def compress_kernel(first, b, waves, ranks, x_ref, a_ref, o_ref):
    block = lax.axis_index("deg")
    step = pl.program_id(0)
    nb, cols = x_ref.shape[1:]
    width = a_ref.shape[2]
    degree = lax.broadcasted_iota(jnp.int32, (nb, cols), 0) + block * nb
    keep = lax.broadcasted_iota(jnp.int32, (width, cols), 0) < ranks[0, block]
    for j in range(b):
        live = jnp.where(degree >= waves[first + step * b + j], x_ref[j], 0).astype(x_ref.dtype)
        total = dot(a_ref[j], live, 0)
        o_ref[j] = jnp.where(keep, total, 0.0).astype(o_ref.dtype)


def compress_slots(first, count, waves, ranks, spectral, compress):
    b = group(count)
    nb, cols = spectral.shape[1:]
    width = compress.shape[2]
    start = first // b
    return call(
        functools.partial(compress_kernel, first, b),
        "compress_slots",
        (waves, ranks),
        (spectral, compress),
        [
            pl.BlockSpec((b, nb, cols), lambda i, *_: (start + i, 0, 0)),
            pl.BlockSpec((b, nb, width), lambda i, *_: (start + i, 0, 0)),
        ],
        pl.BlockSpec((b, width, cols), lambda i, *_: (i, 0, 0)),
        jax.ShapeDtypeStruct((count, width, cols), jnp.bfloat16),
        count // b,
        2 * count * nb * width * cols,
    )


def section_kernel(section, b, ranks, own_ref, peer_ref, v_ref, u_ref, o_ref):
    block = lax.axis_index("deg")
    width, cols = v_ref.shape[1:]
    keep = lax.broadcasted_iota(jnp.int32, (width, cols), 0) < ranks[section, block]
    for j in range(b):
        total = dot(own_ref[j], v_ref[j]) + dot(peer_ref[j], u_ref[j])
        o_ref[j] = jnp.where(keep, total, 0.0).astype(o_ref.dtype)


def section_slots(section, first, ranks, own, peer, vector, partner):
    count, width, cols = vector.shape
    b = group(count)
    start = first // b
    weight = pl.BlockSpec(
        (None, b, None, width, width), lambda i, *_: (section - 1, start + i, 0, 0, 0)
    )
    part = pl.BlockSpec((b, width, cols), lambda i, *_: (i, 0, 0))
    return call(
        functools.partial(section_kernel, section, b),
        f"section_{section}_slots",
        (ranks,),
        (own, peer, vector, partner),
        [weight, weight, part, part],
        part,
        jax.ShapeDtypeStruct(vector.shape, jnp.bfloat16),
        count // b,
        4 * count * width * width * cols,
    )


def expand_kernel(b, pieces, place, kept_ref, got_ref, v_ref, u_ref, *refs):
    outs, rows_ref = refs[:-1], refs[-1]
    piece = outs[0].shape[1]
    zone = lax.axis_index("zonal")
    for j in range(b):
        total = dot(kept_ref[j], v_ref[j]) + dot(got_ref[j], u_ref[j])
        rows_ref[...] = total
        for offset in range(pieces):
            at = pl.multiple_of((zone ^ offset) * piece, piece)
            outs[offset][j] = rows_ref[pl.ds(at, piece), :].astype(outs[offset].dtype)


def expand_pieces(first, place, expand, got, vector, partner, pieces):
    count, width, cols = vector.shape
    rows = got.shape[1]
    piece = rows // pieces
    b = group(count)
    start = first // b
    part = pl.BlockSpec((b, width, cols), lambda i, *_: (i, 0, 0))
    moved = pl.BlockSpec((b, piece, cols), lambda i, *_: (i, 0, 0))
    flops = 4 * count * rows * width * cols
    return pl.pallas_call(
        functools.partial(expand_kernel, b, pieces),
        out_shape=[jax.ShapeDtypeStruct((count, piece, cols), jnp.bfloat16)] * pieces,
        grid_spec=pltpu.PrefetchScalarGridSpec(
            num_scalar_prefetch=1,
            grid=(count // b,),
            in_specs=[
                pl.BlockSpec((b, None, rows, width), lambda i, p: (start + i, 0, p[0], 0)),
                pl.BlockSpec((b, rows, width), lambda i, p: (start + i, 0, 0)),
                part,
                part,
            ],
            out_specs=[moved] * pieces,
            scratch_shapes=[pltpu.VMEM((rows, cols), jnp.float32)],
        ),
        compiler_params=pltpu.CompilerParams(vmem_limit_bytes=VMEM_LIMIT),
        cost_estimate=pl.CostEstimate(
            flops=flops, bytes_accessed=flops // 128, transcendentals=0
        ),
        name="expand_pieces",
    )(place, expand, got, vector, partner)


def split_halves(holding, which_dim, my_bit):
    first_half = lax.index_in_dim(holding, 0, which_dim, keepdims=False)
    second_half = lax.index_in_dim(holding, 1, which_dim, keepdims=False)
    kept_half = jnp.where(my_bit == 0, first_half, second_half)
    given_half = jnp.where(my_bit == 0, second_half, first_half)
    return (kept_half, given_half)


def reduce_bands(expansion, vector, low_bits, deg_index):
    slots, rows = expansion.shape[:2]
    holding = jnp.einsum("mrk,mkc->mrc", expansion, vector, preferred_element_type=jnp.float32)
    holding = holding.reshape((slots,) + (2,) * low_bits + (rows >> low_bits, vector.shape[2]))
    for bit in range(low_bits - 1, -1, -1):
        kept_half, given_half = split_halves(holding, 1, deg_index >> bit & 1)
        holding = kept_half + from_partner(given_half, "deg", 1 << bit)
    return holding.astype(jnp.bfloat16)


def body(spectral, wavenumbers, compress, section_own, section_peer, expand, block_ranks):
    deg_count = lax.axis_size("deg")
    zones = lax.axis_size("zonal")
    deg_index = lax.axis_index("deg")
    zone = lax.axis_index("zonal")
    levels_total = deg_count.bit_length() - 1
    low_bits = levels_total - SECTIONS
    slots = spectral.shape[0]
    cols = spectral.shape[2]
    rows = expand.shape[2]
    band = rows >> low_bits
    piece = band // zones
    pairwise = low_bits == 1 and zones <= 4 and piece % 16 == 0

    chunks = []
    first = 0
    for count in CHUNKS:
        chunks.append((first, count))
        first += count
    assert first == slots

    if pairwise:
        place = (deg_index & 1).astype(jnp.int32)[None]
        given = lax.dynamic_slice_in_dim(expand[:, 0], (1 - place[0]) * band, band, axis=1)
        got = from_partner(given, "deg", 1)
        out = jnp.zeros((zones * slots, piece, cols), jnp.bfloat16)
    else:
        out = []

    for first, count in chunks:
        vector = compress_slots(first, count, wavenumbers, block_ranks, spectral, compress)
        for section in range(1, SECTIONS + 1):
            partner = from_partner(vector, "deg", deg_count >> section)
            vector = section_slots(
                section, first, block_ranks, section_own, section_peer, vector, partner
            )
        if pairwise:
            partner = from_partner(vector, "deg", 1)
            parts = expand_pieces(first, place, expand, got, vector, partner, zones)
            for offset, part in enumerate(parts):
                if offset:
                    part = from_partner(part, "zonal", offset)
                out = lax.dynamic_update_slice(
                    out, part, ((zone ^ offset) * slots + first, 0, 0)
                )
        else:
            part = reduce_bands(expand[first : first + count, 0], vector, low_bits, deg_index)
            part = lax.all_to_all(part, "zonal", split_axis=1, concat_axis=0, tiled=True)
            out.append(part.reshape(zones, count, piece, cols))
    if not pairwise:
        out = jnp.concatenate(out, axis=1)
    return out.reshape(zones * slots, 1, 1, piece, cols)


def solution(mesh):
    in_specs = (
        P("zonal", "deg", None),
        P("zonal"),
        P("zonal", "deg", None),
        P(None, "zonal", "deg", None, None),
        P(None, "zonal", "deg", None, None),
        P("zonal", "deg", None, None),
        P(),
    )
    out_specs = P(None, "deg", "zonal", None, None)
    return jax.shard_map(body, mesh=mesh, in_specs=in_specs, out_specs=out_specs, check_vma=False)
```

time: 166 us -> 115 us (0.69)
  blocking collectives: 34.6 us -> 0 us
  starting transfers between devices: 4.9 us -> 36.7 us
  waiting for transfers between devices: 72.4 us -> 45.8 us
  Pallas kernels: 0 us -> 22.2 us
  matrix products: 21.5 us -> 0 us
  other arithmetic: 12.8 us -> 0 us
  local copies, waits for them, and re-layouts: 18.7 us -> 9.8 us
    all_to_all x1 -> x0, blocking collectives: 34.6 us -> none  [body(): lax.all_to_all(rounded, 'zonal', split_axis=1, concat_axis=0, tiled=True)]
    ppermute x3 -> x31, starting transfers between devices: 4.9 us -> 36.7 us  [from_partner(): return lax.ppermute(array, axis, pairs)]
    ppermute x3 -> x31, waiting for transfers between devices: 72.4 us -> 45.8 us  [from_partner(): return lax.ppermute(array, axis, pairs)]
    pallas_call x0 -> x20, Pallas kernels: none -> 22.2 us  [the longest x15 15.5 us: call(): pl.pallas_call(kernel, out_shape=out_shape, grid_spec=pltpu.PrefetchScala...]
    dot_general x5 -> x0, matrix products: 21.5 us -> none  [the longest x1 10.4 us: body(): jnp.einsum('mrk,mkc->mrc', expansion, vector, preferred_element_type=jnp....]
    dot_general x1 -> x0, local copies, waits for them, and re-layouts: 11.2 us -> none  [body(): jnp.einsum('mrk,mkc->mrc', expansion, vector, preferred_element_type=jnp....]
    convert_element_type x4 -> x0, other arithmetic: 7.25 us -> none  [the longest x1 5.37 us: body(): rounded = holding.astype(jnp.bfloat16)]
    unnamed x8 -> x20, local copies, waits for them, and re-layouts: 0.02 us -> 4.85 us
  transfers between devices with their start and end apart: 3 -> 31, of which waited for: 3 -> 15; matrix products, arithmetic and copies ran while one was open for 4% -> 1% of each run, Pallas kernels for 0% -> 19%
where the time goes in v1:
time: 115 us
  waiting for transfers between devices  45.8 us (40%)
  starting transfers between devices  36.7 us (32%)
  Pallas kernels  22.2 us (19%)
  local copies, waits for them, and re-layouts  9.8 us (9%)
    ppermute x31, waiting for transfers between devices, from_partner(): return lax.ppermute(array, axis, pairs)  45.8 us
    ppermute x31, starting transfers between devices, from_partner(): return lax.ppermute(array, axis, pairs)  36.7 us
    pallas_call x15, Pallas kernels, call(): pl.pallas_call(kernel, out_shape=out_shape, grid_spec=pltpu.PrefetchScala...  15.5 us
    pallas_call x5, Pallas kernels, expand_pieces(): pl.pallas_call(functools.partial(expand_kernel, b, pieces), out_shape=[ja...  6.74 us
    unnamed x20, local copies, waits for them, and re-layouts  4.85 us
    dynamic_slice x1, local copies, waits for them, and re-layouts, body(): lax.dynamic_slice_in_dim(expand[:, 0], (1 - place[0]) * band, band, axis=1)  3.56 us
  transfers between devices with their start and end apart: 31, of which 15 were waited for; matrix products, arithmetic and copies ran while one was open for 1% of the time, Pallas kernels for 19%

profile of v1, /device:TPU:0, one launch (start us, length us, event | category | flops | bytes accessed | tf_op | source)
XLA Modules:
  0.0 114.9 jit_solution(216052944463503422)
XLA Ops:
  0.0 3.6 %dynamic-slice_bitcast_fusion = bf16[32,320,128]{2,1,0:T(8,128)(2,1)} fusion(bf16[32,1,640,128]{3,2,1,0:T(8,128)(2,1)} %kept_ref.9, s32[]{:T(128)S(6)} %select_n.63), kind=kLoop, calls=%fused_computation | loop fusion | bytes 5242884 | tf_op jit(solution)/shard_map/dynamic_slice | solution.py:197
  5.9 4.0 %collective-permute-start.1 = (bf16[8,128,128]{2,1,0:T(8,128)(2,1)S(1)}, bf16[8,128,128]{2,1,0:T(8,128)(2,1)S(1)}, u32[]{:S(2)}, u32[]{:S(2)}) collective-permute-start(bf16[8,128,128]{2,1,0:T(8,128)(2,1)S(1)} %compress_slots.5.v_ref), channel_id=1, source_target_pairs={{0,4},{1,5},{2,6},{3,7},{4,0},{5,1},{6,2},{7,3},{8,12},{9,13},{10,... | collective-permute-start | bytes 786440 | tf_op jit(solution)/shard_map/ppermute | solution.py:17
  12.5 3.0 %collective-permute-start.13 = (bf16[8,128,128]{2,1,0:T(8,128)(2,1)S(1)}, bf16[8,128,128]{2,1,0:T(8,128)(2,1)S(1)}, u32[]{:S(2)}, u32[]{:S(2)}) collective-permute-start(bf16[8,128,128]{2,1,0:T(8,128)(2,1)S(1)} %compress_slots.7.v_ref), channel_id=1, source_target_pairs={{0,4},{1,5},{2,6},{3,7},{4,0},{5,1},{6,2},{7,3},{8,12},{9,13},{10,... | collective-permute-start | bytes 786440 | tf_op jit(solution)/shard_map/ppermute | solution.py:17
  15.4 18.4 %collective-permute-done.1.u_ref = bf16[8,128,128]{2,1,0:T(8,128)(2,1)S(1)} collective-permute-done((bf16[8,128,128]{2,1,0:T(8,128)(2,1)S(1)}, bf16[8,128,128]{2,1,0:T(8,128)(2,1)S(1)}, u32[]{:S(2)}, u32[]{:S(2)}) %collective-permute-start.1) | collective-permute-done | bytes 262176 | tf_op jit(solution)/shard_map/ppermute | solution.py:17
  36.2 3.4 %collective-permute-start.19 = (bf16[4,128,128]{2,1,0:T(8,128)(2,1)S(1)}, bf16[4,128,128]{2,1,0:T(8,128)(2,1)S(1)}, u32[]{:S(2)}, u32[]{:S(2)}) collective-permute-start(bf16[4,128,128]{2,1,0:T(8,128)(2,1)S(1)} %compress_slots.8.v_ref), channel_id=1, source_target_pairs={{0,4},{1,5},{2,6},{3,7},{4,0},{5,1},{6,2},{7,3},{8,12},{9,13},{10,... | collective-permute-start | bytes 393224 | tf_op jit(solution)/shard_map/ppermute | solution.py:17
  41.0 6.8 %collective-permute-done.13.u_ref = bf16[8,128,128]{2,1,0:T(8,128)(2,1)S(1)} collective-permute-done((bf16[8,128,128]{2,1,0:T(8,128)(2,1)S(1)}, bf16[8,128,128]{2,1,0:T(8,128)(2,1)S(1)}, u32[]{:S(2)}, u32[]{:S(2)}) %collective-permute-start.13) | collective-permute-done | bytes 262176 | tf_op jit(solution)/shard_map/ppermute | solution.py:17
  50.4 3.5 %collective-permute-start.25 = (bf16[4,128,128]{2,1,0:T(8,128)(2,1)S(1)}, bf16[4,128,128]{2,1,0:T(8,128)(2,1)S(1)}, u32[]{:S(2)}, u32[]{:S(2)}) collective-permute-start(bf16[4,128,128]{2,1,0:T(8,128)(2,1)S(1)} %compress_slots.9.v_ref), channel_id=1, source_target_pairs={{0,4},{1,5},{2,6},{3,7},{4,0},{5,1},{6,2},{7,3},{8,12},{9,13},{10,... | collective-permute-start | bytes 393224 | tf_op jit(solution)/shard_map/ppermute | solution.py:17
  56.5 2.5 %collective-permute-done.25.u_ref = bf16[4,128,128]{2,1,0:T(8,128)(2,1)S(1)} collective-permute-done((bf16[4,128,128]{2,1,0:T(8,128)(2,1)S(1)}, bf16[4,128,128]{2,1,0:T(8,128)(2,1)S(1)}, u32[]{:S(2)}, u32[]{:S(2)}) %collective-permute-start.25) | collective-permute-done | bytes 131104 | tf_op jit(solution)/shard_map/ppermute | solution.py:17
  59.8 1.8 %collective-permute-done.8.u_ref = bf16[8,128,128]{2,1,0:T(8,128)(2,1)S(1)} collective-permute-done((bf16[8,128,128]{2,1,0:T(8,128)(2,1)S(1)}, bf16[8,128,128]{2,1,0:T(8,128)(2,1)S(1)}, u32[]{:S(2)}, u32[]{:S(2)}) %collective-permute-start.8) | collective-permute-done | bytes 262176 | tf_op jit(solution)/shard_map/ppermute | solution.py:17
  61.6 2.1 %collective-permute-start.26 = (bf16[4,128,128]{2,1,0:T(8,128)(2,1)S(1)}, bf16[4,128,128]{2,1,0:T(8,128)(2,1)S(1)}, u32[]{:S(2)}, u32[]{:S(2)}) collective-permute-start(bf16[4,128,128]{2,1,0:T(8,128)(2,1)S(1)} %section_1_slots.9.v_ref), channel_id=1, source_target_pairs={{0,2},{1,3},{2,0},{3,1},{4,6},{5,7},{6,4},{7,5},{8,10},{9,11},{10,... | collective-permute-start | bytes 393224 | tf_op jit(solution)/shard_map/ppermute | solution.py:17
  64.8 2.4 %collective-permute-done.14.u_ref = bf16[8,128,128]{2,1,0:T(8,128)(2,1)S(1)} collective-permute-done((bf16[8,128,128]{2,1,0:T(8,128)(2,1)S(1)}, bf16[8,128,128]{2,1,0:T(8,128)(2,1)S(1)}, u32[]{:S(2)}, u32[]{:S(2)}) %collective-permute-start.14) | collective-permute-done | bytes 262176 | tf_op jit(solution)/shard_map/ppermute | solution.py:17
  68.3 1.7 %collective-permute-done.20.u_ref = bf16[4,128,128]{2,1,0:T(8,128)(2,1)S(1)} collective-permute-done((bf16[4,128,128]{2,1,0:T(8,128)(2,1)S(1)}, bf16[4,128,128]{2,1,0:T(8,128)(2,1)S(1)}, u32[]{:S(2)}, u32[]{:S(2)}) %collective-permute-start.20) | collective-permute-done | bytes 131104 | tf_op jit(solution)/shard_map/ppermute | solution.py:17
  70.0 1.4 %section_2_slots.8.v_ref = bf16[4,128,128]{2,1,0:T(8,128)(2,1)} custom-call(s32[3,8]{1,0:T(4,128)S(1)} %copy-done.5, bf16[2,32,1,128,128]{4,3,2,1,0:T(8,128)(2,1)S(1)} %copy-done, bf16[2,32,1,128,128]{4,3,2,1,0:T(8,128)(2,1)S(1)} %copy-done.1, bf16[4,128,128]{2,1,0:T(8,128)(2,1)S(1)} %section_1_slots.8.v_ref, ...), custom_call_target="tpu_custom_call" | custom-call | flops 33554432 | bytes 393216 | tf_op jit(solution)/shard_map/section_2_slots/pallas_call | solution.py:29
  74.8 2.5 %copy-done.2 = bf16[32,1,640,128]{3,2,1,0:T(8,128)(2,1)S(1)} copy-done((bf16[32,1,640,128]{3,2,1,0:T(8,128)(2,1)S(1)}, bf16[32,1,640,128]{3,2,1,0:T(8,128)(2,1)}, u32[]{:S(2)}) %copy-start.2) | copy-done | bytes 5242904
  79.0 1.6 %collective-permute-start.4 = (bf16[8,80,128]{2,1,0:T(8,128)(2,1)S(1)}, bf16[8,80,128]{2,1,0:T(8,128)(2,1)S(1)}, u32[]{:S(2)}, u32[]{:S(2)}) collective-permute-start(bf16[8,80,128]{2,1,0:T(8,128)(2,1)S(1)} %get-tuple-element.26), channel_id=1, source_target_pairs={{0,8},{8,0},{16,24},{24,16},{1,9},{9,1},{17,25},{25,17},{2,10},{10... | collective-permute-start | bytes 491528 | tf_op jit(solution)/shard_map/ppermute | solution.py:17
  80.6 1.5 %collective-permute-start.5 = (bf16[8,80,128]{2,1,0:T(8,128)(2,1)S(1)}, bf16[8,80,128]{2,1,0:T(8,128)(2,1)S(1)}, u32[]{:S(2)}, u32[]{:S(2)}) collective-permute-start(bf16[8,80,128]{2,1,0:T(8,128)(2,1)S(1)} %get-tuple-element.27), channel_id=1, source_target_pairs={{0,16},{8,24},{16,0},{24,8},{1,17},{9,25},{17,1},{25,9},{2,18},{10... | collective-permute-start | bytes 491528 | tf_op jit(solution)/shard_map/ppermute | solution.py:17
  82.2 1.3 %expand_pieces.8 = (bf16[4,80,128]{2,1,0:T(8,128)(2,1)S(1)}, bf16[4,80,128]{2,1,0:T(8,128)(2,1)S(1)}, bf16[4,80,128]{2,1,0:T(8,128)(2,1)S(1)}, bf16[4,80,128]{2,1,0:T(8,128)(2,1)S(1)}) custom-call(s32[1]{0:T(128)} %bitcast.place, bf16[32,1,640,128]{3,2,1,0:T(8,128)(2,1)S(1)} %copy-done.2, bf16[32,320,128]{2,1,0:T(8,128)(2,1)S(1)} %collective-permute-done.got_ref, ...), custom_call_target="tpu_custom_call" | custom-call | flops 83886080 | bytes 655360 | tf_op jit(solution)/shard_map/expand_pieces/pallas_call | solution.py:133
  84.0 1.7 %expand_pieces.6 = (bf16[8,80,128]{2,1,0:T(8,128)(2,1)S(1)}, bf16[8,80,128]{2,1,0:T(8,128)(2,1)S(1)}, bf16[8,80,128]{2,1,0:T(8,128)(2,1)S(1)}, bf16[8,80,128]{2,1,0:T(8,128)(2,1)S(1)}) custom-call(s32[1]{0:T(128)} %bitcast.place, bf16[32,1,640,128]{3,2,1,0:T(8,128)(2,1)S(1)} %copy-done.2, bf16[32,320,128]{2,1,0:T(8,128)(2,1)S(1)} %collective-permute-done.got_ref, ...), custom_call_target="tpu_custom_call" | custom-call | flops 167772160 | bytes 1310720 | tf_op jit(solution)/shard_map/expand_pieces/pallas_call | solution.py:133
  85.7 1.6 %collective-permute-start.10 = (bf16[8,80,128]{2,1,0:T(8,128)(2,1)S(1)}, bf16[8,80,128]{2,1,0:T(8,128)(2,1)S(1)}, u32[]{:S(2)}, u32[]{:S(2)}) collective-permute-start(bf16[8,80,128]{2,1,0:T(8,128)(2,1)S(1)} %get-tuple-element.30), channel_id=1, source_target_pairs={{0,8},{8,0},{16,24},{24,16},{1,9},{9,1},{17,25},{25,17},{2,10},{10... | collective-permute-start | bytes 491528 | tf_op jit(solution)/shard_map/ppermute | solution.py:17
  87.3 1.7 %expand_pieces.7 = (bf16[8,80,128]{2,1,0:T(8,128)(2,1)S(1)}, bf16[8,80,128]{2,1,0:T(8,128)(2,1)S(1)}, bf16[8,80,128]{2,1,0:T(8,128)(2,1)S(1)}, bf16[8,80,128]{2,1,0:T(8,128)(2,1)S(1)}) custom-call(s32[1]{0:T(128)} %bitcast.place, bf16[32,1,640,128]{3,2,1,0:T(8,128)(2,1)S(1)} %copy-done.2, bf16[32,320,128]{2,1,0:T(8,128)(2,1)S(1)} %collective-permute-done.got_ref, ...), custom_call_target="tpu_custom_call" | custom-call | flops 167772160 | bytes 1310720 | tf_op jit(solution)/shard_map/expand_pieces/pallas_call | solution.py:133
  89.0 1.6 %collective-permute-start.11 = (bf16[8,80,128]{2,1,0:T(8,128)(2,1)S(1)}, bf16[8,80,128]{2,1,0:T(8,128)(2,1)S(1)}, u32[]{:S(2)}, u32[]{:S(2)}) collective-permute-start(bf16[8,80,128]{2,1,0:T(8,128)(2,1)S(1)} %get-tuple-element.31), channel_id=1, source_target_pairs={{0,16},{8,24},{16,0},{24,8},{1,17},{9,25},{17,1},{25,9},{2,18},{10... | collective-permute-start | bytes 491528 | tf_op jit(solution)/shard_map/ppermute | solution.py:17
  90.6 1.3 %expand_pieces.9 = (bf16[4,80,128]{2,1,0:T(8,128)(2,1)S(1)}, bf16[4,80,128]{2,1,0:T(8,128)(2,1)S(1)}, bf16[4,80,128]{2,1,0:T(8,128)(2,1)S(1)}, bf16[4,80,128]{2,1,0:T(8,128)(2,1)S(1)}) custom-call(s32[1]{0:T(128)} %bitcast.place, bf16[32,1,640,128]{3,2,1,0:T(8,128)(2,1)S(1)} %copy-done.2, bf16[32,320,128]{2,1,0:T(8,128)(2,1)S(1)} %collective-permute-done.got_ref, ...), custom_call_target="tpu_custom_call" | custom-call | flops 83886080 | bytes 655360 | tf_op jit(solution)/shard_map/expand_pieces/pallas_call | solution.py:133
  92.8 1.6 %collective-permute-start.16 = (bf16[8,80,128]{2,1,0:T(8,128)(2,1)S(1)}, bf16[8,80,128]{2,1,0:T(8,128)(2,1)S(1)}, u32[]{:S(2)}, u32[]{:S(2)}) collective-permute-start(bf16[8,80,128]{2,1,0:T(8,128)(2,1)S(1)} %get-tuple-element.34), channel_id=1, source_target_pairs={{0,8},{8,0},{16,24},{24,16},{1,9},{9,1},{17,25},{25,17},{2,10},{10... | collective-permute-start | bytes 491528 | tf_op jit(solution)/shard_map/ppermute | solution.py:17
  94.4 1.6 %collective-permute-start.17 = (bf16[8,80,128]{2,1,0:T(8,128)(2,1)S(1)}, bf16[8,80,128]{2,1,0:T(8,128)(2,1)S(1)}, u32[]{:S(2)}, u32[]{:S(2)}) collective-permute-start(bf16[8,80,128]{2,1,0:T(8,128)(2,1)S(1)} %get-tuple-element.35), channel_id=1, source_target_pairs={{0,16},{8,24},{16,0},{24,8},{1,17},{9,25},{17,1},{25,9},{2,18},{10... | collective-permute-start | bytes 491528 | tf_op jit(solution)/shard_map/ppermute | solution.py:17
  96.7 1.6 %collective-permute-start.22 = (bf16[4,80,128]{2,1,0:T(8,128)(2,1)S(1)}, bf16[4,80,128]{2,1,0:T(8,128)(2,1)S(1)}, u32[]{:S(2)}, u32[]{:S(2)}) collective-permute-start(bf16[4,80,128]{2,1,0:T(8,128)(2,1)S(1)} %get-tuple-element.38), channel_id=1, source_target_pairs={{0,8},{8,0},{16,24},{24,16},{1,9},{9,1},{17,25},{25,17},{2,10},{10... | collective-permute-start | bytes 245768 | tf_op jit(solution)/shard_map/ppermute | solution.py:17
  98.2 2.2 %collective-permute-done.12 = bf16[8,80,128]{2,1,0:T(8,128)(2,1)S(1)} collective-permute-done((bf16[8,80,128]{2,1,0:T(8,128)(2,1)S(1)}, bf16[8,80,128]{2,1,0:T(8,128)(2,1)S(1)}, u32[]{:S(2)}, u32[]{:S(2)}) %collective-permute-start.12) | collective-permute-done | bytes 163872 | tf_op jit(solution)/shard_map/ppermute | solution.py:17
  101.0 1.9 %collective-permute-done.16 = bf16[8,80,128]{2,1,0:T(8,128)(2,1)S(1)} collective-permute-done((bf16[8,80,128]{2,1,0:T(8,128)(2,1)S(1)}, bf16[8,80,128]{2,1,0:T(8,128)(2,1)S(1)}, u32[]{:S(2)}, u32[]{:S(2)}) %collective-permute-start.16) | collective-permute-done | bytes 163872 | tf_op jit(solution)/shard_map/ppermute | solution.py:17
  103.0 1.5 %collective-permute-start.24 = (bf16[4,80,128]{2,1,0:T(8,128)(2,1)S(1)}, bf16[4,80,128]{2,1,0:T(8,128)(2,1)S(1)}, u32[]{:S(2)}, u32[]{:S(2)}) collective-permute-start(bf16[4,80,128]{2,1,0:T(8,128)(2,1)S(1)} %get-tuple-element.40), channel_id=1, source_target_pairs={{0,24},{8,16},{16,8},{24,0},{1,25},{9,17},{17,9},{25,1},{2,26},{10... | collective-permute-start | bytes 245768 | tf_op jit(solution)/shard_map/ppermute | solution.py:17
  106.1 1.4 %collective-permute-done.18 = bf16[8,80,128]{2,1,0:T(8,128)(2,1)S(1)} collective-permute-done((bf16[8,80,128]{2,1,0:T(8,128)(2,1)S(1)}, bf16[8,80,128]{2,1,0:T(8,128)(2,1)S(1)}, u32[]{:S(2)}, u32[]{:S(2)}) %collective-permute-start.18) | collective-permute-done | bytes 163872 | tf_op jit(solution)/shard_map/ppermute | solution.py:17
  107.5 1.3 %collective-permute-start.29 = (bf16[4,80,128]{2,1,0:T(8,128)(2,1)S(1)}, bf16[4,80,128]{2,1,0:T(8,128)(2,1)S(1)}, u32[]{:S(2)}, u32[]{:S(2)}) collective-permute-start(bf16[4,80,128]{2,1,0:T(8,128)(2,1)S(1)} %get-tuple-element.43), channel_id=1, source_target_pairs={{0,16},{8,24},{16,0},{24,8},{1,17},{9,25},{17,1},{25,9},{2,18},{10... | collective-permute-start | bytes 245768 | tf_op jit(solution)/shard_map/ppermute | solution.py:17
  110.5 1.5 %collective-permute-done.29 = bf16[4,80,128]{2,1,0:T(8,128)(2,1)S(1)} collective-permute-done((bf16[4,80,128]{2,1,0:T(8,128)(2,1)S(1)}, bf16[4,80,128]{2,1,0:T(8,128)(2,1)S(1)}, u32[]{:S(2)}, u32[]{:S(2)}) %collective-permute-start.29) | collective-permute-done | bytes 81952 | tf_op jit(solution)/shard_map/ppermute | solution.py:17
  112.0 2.3 %collective-permute-done.30 = bf16[4,80,128]{2,1,0:T(8,128)(2,1)S(1)} collective-permute-done((bf16[4,80,128]{2,1,0:T(8,128)(2,1)S(1)}, bf16[4,80,128]{2,1,0:T(8,128)(2,1)S(1)}, u32[]{:S(2)}, u32[]{:S(2)}) %collective-permute-start.30) | collective-permute-done | bytes 81952 | tf_op jit(solution)/shard_map/ppermute | solution.py:17
  (92 shorter events, 28.0 us)
Async XLA Ops:
  3.6 71.2 %collective-permute-start = (bf16[32,320,128]{2,1,0:T(8,128)(2,1)}, bf16[32,320,128]{2,1,0:T(8,128)(2,1)S(1)}, u32[]{:S(2)}, u32[]{:S(2)}) collective-permute-start(bf16[32,320,128]{2,1,0:T(8,128)(2,1)} %dynamic-slice_bitcast_fusion), channel_id=1, source_target_pairs={{0,1},{1,0},{2,3},{3,2},{4,5},{5,4},{6,7},{7,6},{8,9},{9,8},{10,11... | collective-permute-start | bytes 7864328 | tf_op jit(solution)/shard_map/ppermute | solution.py:17
  5.9 27.9 %collective-permute-start.1 = (bf16[8,128,128]{2,1,0:T(8,128)(2,1)S(1)}, bf16[8,128,128]{2,1,0:T(8,128)(2,1)S(1)}, u32[]{:S(2)}, u32[]{:S(2)}) collective-permute-start(bf16[8,128,128]{2,1,0:T(8,128)(2,1)S(1)} %compress_slots.5.v_ref), channel_id=1, source_target_pairs={{0,4},{1,5},{2,6},{3,7},{4,0},{5,1},{6,2},{7,3},{8,12},{9,13},{10,... | collective-permute-start | bytes 786440 | tf_op jit(solution)/shard_map/ppermute | solution.py:17
  11.1 22.7 %copy-start = (bf16[2,32,1,128,128]{4,3,2,1,0:T(8,128)(2,1)S(1)}, bf16[2,32,1,128,128]{4,3,2,1,0:T(8,128)(2,1)}, u32[]{:S(2)}) copy-start(bf16[2,32,1,128,128]{4,3,2,1,0:T(8,128)(2,1)} %own_ref.19) | copy-start | bytes 6291460
  11.2 28.5 %collective-permute-start.7 = (bf16[8,128,128]{2,1,0:T(8,128)(2,1)S(1)}, bf16[8,128,128]{2,1,0:T(8,128)(2,1)S(1)}, u32[]{:S(2)}, u32[]{:S(2)}) collective-permute-start(bf16[8,128,128]{2,1,0:T(8,128)(2,1)S(1)} %compress_slots.6.v_ref), channel_id=1, source_target_pairs={{0,4},{1,5},{2,6},{3,7},{4,0},{5,1},{6,2},{7,3},{8,12},{9,13},{10,... | collective-permute-start | bytes 786440 | tf_op jit(solution)/shard_map/ppermute | solution.py:17
  12.5 35.3 %collective-permute-start.13 = (bf16[8,128,128]{2,1,0:T(8,128)(2,1)S(1)}, bf16[8,128,128]{2,1,0:T(8,128)(2,1)S(1)}, u32[]{:S(2)}, u32[]{:S(2)}) collective-permute-start(bf16[8,128,128]{2,1,0:T(8,128)(2,1)S(1)} %compress_slots.7.v_ref), channel_id=1, source_target_pairs={{0,4},{1,5},{2,6},{3,7},{4,0},{5,1},{6,2},{7,3},{8,12},{9,13},{10,... | collective-permute-start | bytes 786440 | tf_op jit(solution)/shard_map/ppermute | solution.py:17
  34.9 19.7 %collective-permute-start.2 = (bf16[8,128,128]{2,1,0:T(8,128)(2,1)S(1)}, bf16[8,128,128]{2,1,0:T(8,128)(2,1)S(1)}, u32[]{:S(2)}, u32[]{:S(2)}) collective-permute-start(bf16[8,128,128]{2,1,0:T(8,128)(2,1)S(1)} %section_1_slots.5.v_ref), channel_id=1, source_target_pairs={{0,2},{1,3},{2,0},{3,1},{4,6},{5,7},{6,4},{7,5},{8,10},{9,11},{10,... | collective-permute-start | bytes 786440 | tf_op jit(solution)/shard_map/ppermute | solution.py:17
  36.2 14.2 %collective-permute-start.19 = (bf16[4,128,128]{2,1,0:T(8,128)(2,1)S(1)}, bf16[4,128,128]{2,1,0:T(8,128)(2,1)S(1)}, u32[]{:S(2)}, u32[]{:S(2)}) collective-permute-start(bf16[4,128,128]{2,1,0:T(8,128)(2,1)S(1)} %compress_slots.8.v_ref), channel_id=1, source_target_pairs={{0,4},{1,5},{2,6},{3,7},{4,0},{5,1},{6,2},{7,3},{8,12},{9,13},{10,... | collective-permute-start | bytes 393224 | tf_op jit(solution)/shard_map/ppermute | solution.py:17
  40.7 20.9 %collective-permute-start.8 = (bf16[8,128,128]{2,1,0:T(8,128)(2,1)S(1)}, bf16[8,128,128]{2,1,0:T(8,128)(2,1)S(1)}, u32[]{:S(2)}, u32[]{:S(2)}) collective-permute-start(bf16[8,128,128]{2,1,0:T(8,128)(2,1)S(1)} %section_1_slots.6.v_ref), channel_id=1, source_target_pairs={{0,2},{1,3},{2,0},{3,1},{4,6},{5,7},{6,4},{7,5},{8,10},{9,11},{10,... | collective-permute-start | bytes 786440 | tf_op jit(solution)/shard_map/ppermute | solution.py:17
  48.9 18.3 %collective-permute-start.14 = (bf16[8,128,128]{2,1,0:T(8,128)(2,1)S(1)}, bf16[8,128,128]{2,1,0:T(8,128)(2,1)S(1)}, u32[]{:S(2)}, u32[]{:S(2)}) collective-permute-start(bf16[8,128,128]{2,1,0:T(8,128)(2,1)S(1)} %section_1_slots.7.v_ref), channel_id=1, source_target_pairs={{0,2},{1,3},{2,0},{3,1},{4,6},{5,7},{6,4},{7,5},{8,10},{9,11},{10,... | collective-permute-start | bytes 786440 | tf_op jit(solution)/shard_map/ppermute | solution.py:17
  50.4 8.6 %collective-permute-start.25 = (bf16[4,128,128]{2,1,0:T(8,128)(2,1)S(1)}, bf16[4,128,128]{2,1,0:T(8,128)(2,1)S(1)}, u32[]{:S(2)}, u32[]{:S(2)}) collective-permute-start(bf16[4,128,128]{2,1,0:T(8,128)(2,1)S(1)} %compress_slots.9.v_ref), channel_id=1, source_target_pairs={{0,4},{1,5},{2,6},{3,7},{4,0},{5,1},{6,2},{7,3},{8,12},{9,13},{10,... | collective-permute-start | bytes 393224 | tf_op jit(solution)/shard_map/ppermute | solution.py:17
  54.7 15.3 %collective-permute-start.20 = (bf16[4,128,128]{2,1,0:T(8,128)(2,1)S(1)}, bf16[4,128,128]{2,1,0:T(8,128)(2,1)S(1)}, u32[]{:S(2)}, u32[]{:S(2)}) collective-permute-start(bf16[4,128,128]{2,1,0:T(8,128)(2,1)S(1)} %section_1_slots.8.v_ref), channel_id=1, source_target_pairs={{0,2},{1,3},{2,0},{3,1},{4,6},{5,7},{6,4},{7,5},{8,10},{9,11},{10,... | collective-permute-start | bytes 393224 | tf_op jit(solution)/shard_map/ppermute | solution.py:17
  59.0 14.6 %collective-permute-start.3 = (bf16[8,128,128]{2,1,0:T(8,128)(2,1)S(1)}, bf16[8,128,128]{2,1,0:T(8,128)(2,1)S(1)}, u32[]{:S(2)}, u32[]{:S(2)}) collective-permute-start(bf16[8,128,128]{2,1,0:T(8,128)(2,1)S(1)} %section_2_slots.5.v_ref), channel_id=1, source_target_pairs={{0,1},{1,0},{2,3},{3,2},{4,5},{5,4},{6,7},{7,6},{8,9},{9,8},{10,11... | collective-permute-start | bytes 786440 | tf_op jit(solution)/shard_map/ppermute | solution.py:17
  61.6 11.1 %collective-permute-start.26 = (bf16[4,128,128]{2,1,0:T(8,128)(2,1)S(1)}, bf16[4,128,128]{2,1,0:T(8,128)(2,1)S(1)}, u32[]{:S(2)}, u32[]{:S(2)}) collective-permute-start(bf16[4,128,128]{2,1,0:T(8,128)(2,1)S(1)} %section_1_slots.9.v_ref), channel_id=1, source_target_pairs={{0,2},{1,3},{2,0},{3,1},{4,6},{5,7},{6,4},{7,5},{8,10},{9,11},{10,... | collective-permute-start | bytes 393224 | tf_op jit(solution)/shard_map/ppermute | solution.py:17
  67.2 16.3 %collective-permute-start.9 = (bf16[8,128,128]{2,1,0:T(8,128)(2,1)S(1)}, bf16[8,128,128]{2,1,0:T(8,128)(2,1)}, u32[]{:S(2)}, u32[]{:S(2)}) collective-permute-start(bf16[8,128,128]{2,1,0:T(8,128)(2,1)S(1)} %section_2_slots.6.v_ref), channel_id=1, source_target_pairs={{0,1},{1,0},{2,3},{3,2},{4,5},{5,4},{6,7},{7,6},{8,9},{9,8},{10,11... | collective-permute-start | bytes 786440 | tf_op jit(solution)/shard_map/ppermute | solution.py:17
  70.0 15.7 %collective-permute-start.15 = (bf16[8,128,128]{2,1,0:T(8,128)(2,1)S(1)}, bf16[8,128,128]{2,1,0:T(8,128)(2,1)}, u32[]{:S(2)}, u32[]{:S(2)}) collective-permute-start(bf16[8,128,128]{2,1,0:T(8,128)(2,1)S(1)} %section_2_slots.7.v_ref), channel_id=1, source_target_pairs={{0,1},{1,0},{2,3},{3,2},{4,5},{5,4},{6,7},{7,6},{8,9},{9,8},{10,11... | collective-permute-start | bytes 786440 | tf_op jit(solution)/shard_map/ppermute | solution.py:17
  72.7 7.9 %collective-permute-start.21 = (bf16[4,128,128]{2,1,0:T(8,128)(2,1)}, bf16[4,128,128]{2,1,0:T(8,128)(2,1)}, u32[]{:S(2)}, u32[]{:S(2)}) collective-permute-start(bf16[4,128,128]{2,1,0:T(8,128)(2,1)} %section_2_slots.8.v_ref), channel_id=1, source_target_pairs={{0,1},{1,0},{2,3},{3,2},{4,5},{5,4},{6,7},{7,6},{8,9},{9,8},{10,11... | collective-permute-start | bytes 393224 | tf_op jit(solution)/shard_map/ppermute | solution.py:17
  74.3 14.7 %collective-permute-start.27 = (bf16[4,128,128]{2,1,0:T(8,128)(2,1)S(1)}, bf16[4,128,128]{2,1,0:T(8,128)(2,1)}, u32[]{:S(2)}, u32[]{:S(2)}) collective-permute-start(bf16[4,128,128]{2,1,0:T(8,128)(2,1)S(1)} %section_2_slots.9.v_ref), channel_id=1, source_target_pairs={{0,1},{1,0},{2,3},{3,2},{4,5},{5,4},{6,7},{7,6},{8,9},{9,8},{10,11... | collective-permute-start | bytes 393224 | tf_op jit(solution)/shard_map/ppermute | solution.py:17
  79.0 13.2 %collective-permute-start.4 = (bf16[8,80,128]{2,1,0:T(8,128)(2,1)S(1)}, bf16[8,80,128]{2,1,0:T(8,128)(2,1)S(1)}, u32[]{:S(2)}, u32[]{:S(2)}) collective-permute-start(bf16[8,80,128]{2,1,0:T(8,128)(2,1)S(1)} %get-tuple-element.26), channel_id=1, source_target_pairs={{0,8},{8,0},{16,24},{24,16},{1,9},{9,1},{17,25},{25,17},{2,10},{10... | collective-permute-start | bytes 491528 | tf_op jit(solution)/shard_map/ppermute | solution.py:17
  80.6 12.1 %collective-permute-start.5 = (bf16[8,80,128]{2,1,0:T(8,128)(2,1)S(1)}, bf16[8,80,128]{2,1,0:T(8,128)(2,1)S(1)}, u32[]{:S(2)}, u32[]{:S(2)}) collective-permute-start(bf16[8,80,128]{2,1,0:T(8,128)(2,1)S(1)} %get-tuple-element.27), channel_id=1, source_target_pairs={{0,16},{8,24},{16,0},{24,8},{1,17},{9,25},{17,1},{25,9},{2,18},{10... | collective-permute-start | bytes 491528 | tf_op jit(solution)/shard_map/ppermute | solution.py:17
  83.5 10.9 %collective-permute-start.6 = (bf16[8,80,128]{2,1,0:T(8,128)(2,1)S(1)}, bf16[8,80,128]{2,1,0:T(8,128)(2,1)S(1)}, u32[]{:S(2)}, u32[]{:S(2)}) collective-permute-start(bf16[8,80,128]{2,1,0:T(8,128)(2,1)S(1)} %get-tuple-element.28), channel_id=1, source_target_pairs={{0,24},{8,16},{16,8},{24,0},{1,25},{9,17},{17,9},{25,1},{2,26},{10... | collective-permute-start | bytes 491528 | tf_op jit(solution)/shard_map/ppermute | solution.py:17
  85.7 10.4 %collective-permute-start.10 = (bf16[8,80,128]{2,1,0:T(8,128)(2,1)S(1)}, bf16[8,80,128]{2,1,0:T(8,128)(2,1)S(1)}, u32[]{:S(2)}, u32[]{:S(2)}) collective-permute-start(bf16[8,80,128]{2,1,0:T(8,128)(2,1)S(1)} %get-tuple-element.30), channel_id=1, source_target_pairs={{0,8},{8,0},{16,24},{24,16},{1,9},{9,1},{17,25},{25,17},{2,10},{10... | collective-permute-start | bytes 491528 | tf_op jit(solution)/shard_map/ppermute | solution.py:17
  89.0 7.7 %collective-permute-start.11 = (bf16[8,80,128]{2,1,0:T(8,128)(2,1)S(1)}, bf16[8,80,128]{2,1,0:T(8,128)(2,1)S(1)}, u32[]{:S(2)}, u32[]{:S(2)}) collective-permute-start(bf16[8,80,128]{2,1,0:T(8,128)(2,1)S(1)} %get-tuple-element.31), channel_id=1, source_target_pairs={{0,16},{8,24},{16,0},{24,8},{1,17},{9,25},{17,1},{25,9},{2,18},{10... | collective-permute-start | bytes 491528 | tf_op jit(solution)/shard_map/ppermute | solution.py:17
  92.3 8.2 %collective-permute-start.12 = (bf16[8,80,128]{2,1,0:T(8,128)(2,1)S(1)}, bf16[8,80,128]{2,1,0:T(8,128)(2,1)S(1)}, u32[]{:S(2)}, u32[]{:S(2)}) collective-permute-start(bf16[8,80,128]{2,1,0:T(8,128)(2,1)S(1)} %get-tuple-element.32), channel_id=1, source_target_pairs={{0,24},{8,16},{16,8},{24,0},{1,25},{9,17},{17,9},{25,1},{2,26},{10... | collective-permute-start | bytes 491528 | tf_op jit(solution)/shard_map/ppermute | solution.py:17
  92.8 10.2 %collective-permute-start.16 = (bf16[8,80,128]{2,1,0:T(8,128)(2,1)S(1)}, bf16[8,80,128]{2,1,0:T(8,128)(2,1)S(1)}, u32[]{:S(2)}, u32[]{:S(2)}) collective-permute-start(bf16[8,80,128]{2,1,0:T(8,128)(2,1)S(1)} %get-tuple-element.34), channel_id=1, source_target_pairs={{0,8},{8,0},{16,24},{24,16},{1,9},{9,1},{17,25},{25,17},{2,10},{10... | collective-permute-start | bytes 491528 | tf_op jit(solution)/shard_map/ppermute | solution.py:17
  94.4 10.9 %collective-permute-start.17 = (bf16[8,80,128]{2,1,0:T(8,128)(2,1)S(1)}, bf16[8,80,128]{2,1,0:T(8,128)(2,1)S(1)}, u32[]{:S(2)}, u32[]{:S(2)}) collective-permute-start(bf16[8,80,128]{2,1,0:T(8,128)(2,1)S(1)} %get-tuple-element.35), channel_id=1, source_target_pairs={{0,16},{8,24},{16,0},{24,8},{1,17},{9,25},{17,1},{25,9},{2,18},{10... | collective-permute-start | bytes 491528 | tf_op jit(solution)/shard_map/ppermute | solution.py:17
  96.1 11.4 %collective-permute-start.18 = (bf16[8,80,128]{2,1,0:T(8,128)(2,1)S(1)}, bf16[8,80,128]{2,1,0:T(8,128)(2,1)S(1)}, u32[]{:S(2)}, u32[]{:S(2)}) collective-permute-start(bf16[8,80,128]{2,1,0:T(8,128)(2,1)S(1)} %get-tuple-element.36), channel_id=1, source_target_pairs={{0,24},{8,16},{16,8},{24,0},{1,25},{9,17},{17,9},{25,1},{2,26},{10... | collective-permute-start | bytes 491528 | tf_op jit(solution)/shard_map/ppermute | solution.py:17
  96.7 12.2 %collective-permute-start.22 = (bf16[4,80,128]{2,1,0:T(8,128)(2,1)S(1)}, bf16[4,80,128]{2,1,0:T(8,128)(2,1)S(1)}, u32[]{:S(2)}, u32[]{:S(2)}) collective-permute-start(bf16[4,80,128]{2,1,0:T(8,128)(2,1)S(1)} %get-tuple-element.38), channel_id=1, source_target_pairs={{0,8},{8,0},{16,24},{24,16},{1,9},{9,1},{17,25},{25,17},{2,10},{10... | collective-permute-start | bytes 245768 | tf_op jit(solution)/shard_map/ppermute | solution.py:17
  100.5 9.4 %collective-permute-start.23 = (bf16[4,80,128]{2,1,0:T(8,128)(2,1)S(1)}, bf16[4,80,128]{2,1,0:T(8,128)(2,1)S(1)}, u32[]{:S(2)}, u32[]{:S(2)}) collective-permute-start(bf16[4,80,128]{2,1,0:T(8,128)(2,1)S(1)} %get-tuple-element.39), channel_id=1, source_target_pairs={{0,16},{8,24},{16,0},{24,8},{1,17},{9,25},{17,1},{25,9},{2,18},{10... | collective-permute-start | bytes 245768 | tf_op jit(solution)/shard_map/ppermute | solution.py:17
  103.0 7.4 %collective-permute-start.24 = (bf16[4,80,128]{2,1,0:T(8,128)(2,1)S(1)}, bf16[4,80,128]{2,1,0:T(8,128)(2,1)S(1)}, u32[]{:S(2)}, u32[]{:S(2)}) collective-permute-start(bf16[4,80,128]{2,1,0:T(8,128)(2,1)S(1)} %get-tuple-element.40), channel_id=1, source_target_pairs={{0,24},{8,16},{16,8},{24,0},{1,25},{9,17},{17,9},{25,1},{2,26},{10... | collective-permute-start | bytes 245768 | tf_op jit(solution)/shard_map/ppermute | solution.py:17
  105.3 5.1 %collective-permute-start.28 = (bf16[4,80,128]{2,1,0:T(8,128)(2,1)S(1)}, bf16[4,80,128]{2,1,0:T(8,128)(2,1)S(1)}, u32[]{:S(2)}, u32[]{:S(2)}) collective-permute-start(bf16[4,80,128]{2,1,0:T(8,128)(2,1)S(1)} %get-tuple-element.42), channel_id=1, source_target_pairs={{0,8},{8,0},{16,24},{24,16},{1,9},{9,1},{17,25},{25,17},{2,10},{10... | collective-permute-start | bytes 245768 | tf_op jit(solution)/shard_map/ppermute | solution.py:17
  107.5 4.4 %collective-permute-start.29 = (bf16[4,80,128]{2,1,0:T(8,128)(2,1)S(1)}, bf16[4,80,128]{2,1,0:T(8,128)(2,1)S(1)}, u32[]{:S(2)}, u32[]{:S(2)}) collective-permute-start(bf16[4,80,128]{2,1,0:T(8,128)(2,1)S(1)} %get-tuple-element.43), channel_id=1, source_target_pairs={{0,16},{8,24},{16,0},{24,8},{1,17},{9,25},{17,1},{25,9},{2,18},{10... | collective-permute-start | bytes 245768 | tf_op jit(solution)/shard_map/ppermute | solution.py:17
  108.9 5.4 %collective-permute-start.30 = (bf16[4,80,128]{2,1,0:T(8,128)(2,1)S(1)}, bf16[4,80,128]{2,1,0:T(8,128)(2,1)S(1)}, u32[]{:S(2)}, u32[]{:S(2)}) collective-permute-start(bf16[4,80,128]{2,1,0:T(8,128)(2,1)S(1)} %get-tuple-element.44), channel_id=1, source_target_pairs={{0,24},{8,16},{16,8},{24,0},{1,25},{9,17},{17,9},{25,1},{2,26},{10... | collective-permute-start | bytes 245768 | tf_op jit(solution)/shard_map/ppermute | solution.py:17
  (9 other events, 42.0 us)

commit v2 on v1

v2 whole, which is shorter than its diff:
```python
import functools
import math

import jax
import jax.numpy as jnp
from jax import lax
from jax.experimental import pallas as pl
from jax.experimental.pallas import tpu as pltpu
from jax.sharding import PartitionSpec as P

SECTIONS = 2
CHUNKS = (8, 8, 8, 8)
ORDER = (
    "C0",
    "C123",
    "G0",
    "10",
    "11",
    "20",
    "E0",
    "12",
    "21",
    "E1",
    "13",
    "22",
    "E2<P4_0",
    "23",
    "E3<P4_1",
)
COSTS = {}
VMEM_LIMIT = 52 * 2**20
EXPAND_LIMIT = 52 * 2**20
SECTION_LIMIT = 52 * 2**20
HBM = pl.BlockSpec(memory_space=pltpu.HBM)
ANY = pl.BlockSpec(memory_space=pl.ANY)


def from_partner(array, axis, offset, scope):
    pairs = [(i, i ^ offset) for i in range(lax.axis_size(axis))]
    with jax.named_scope(scope):
        return lax.ppermute(array, axis, pairs)


def dot(a, b, contract_a=1):
    return lax.dot_general(
        a, b, (((contract_a,), (0,)), ((), ())), preferred_element_type=jnp.float32
    )


def dot_pair(a, b, v, u):
    return dot(jnp.concatenate([a, b], axis=1), jnp.concatenate([v, u], axis=0))


def ordered(kernel, used, late):
    def run(*refs):
        kernel(*refs[:used], *refs[used + late :])

    return run


def call(kernel, name, scalars, operands, in_specs, out_specs, out_shape, steps, flops, late, scratch=(), limit=VMEM_LIMIT):
    return pl.pallas_call(
        ordered(kernel, len(scalars) + len(operands), len(late)),
        out_shape=out_shape,
        grid_spec=pltpu.PrefetchScalarGridSpec(
            num_scalar_prefetch=len(scalars),
            grid=(steps,),
            in_specs=[*in_specs] + [ANY] * len(late),
            out_specs=out_specs,
            scratch_shapes=scratch,
        ),
        compiler_params=pltpu.CompilerParams(vmem_limit_bytes=limit),
        cost_estimate=pl.CostEstimate(flops=flops, bytes_accessed=0, transcendentals=0),
        name=name,
    )(*scalars, *operands, *late)


def group(count, most=4):
    return max(b for b in range(1, most + 1) if count % b == 0)


def compress_kernel(first, b, waves, ranks, x_hbm, a_hbm, *refs):
    outs, (x_ref, a_ref, sems) = refs[:-3], refs[-3:]
    block = lax.axis_index("deg")
    nb, cols = x_ref.shape[1:]
    width = a_ref.shape[2]

    def copies(g):
        here, there = pl.ds(g * b, b), pl.ds(first + g * b, b)
        return (
            pltpu.make_async_copy(x_hbm.at[there], x_ref.at[here], sems.at[0, g]),
            pltpu.make_async_copy(a_hbm.at[there], a_ref.at[here], sems.at[1, g]),
        )

    for g in range(x_ref.shape[0] // b):
        for copy in copies(g):
            copy.start()
    degree = lax.broadcasted_iota(jnp.int32, (nb, cols), 0) + block * nb
    keep = lax.broadcasted_iota(jnp.int32, (width, cols), 0) < ranks[0, block]
    start = 0
    for out in outs:

        def some(g, carry, out=out, start=start):
            for copy in copies(start // b + g):
                copy.wait()
            for j in range(b):
                slot = g * b + j
                wave = waves[first + start + slot]
                live = jnp.where(degree >= wave, x_ref[start + slot], 0).astype(x_ref.dtype)
                total = dot(a_ref[start + slot], live, 0)
                out[slot] = jnp.where(keep, total, 0.0).astype(out.dtype)
            return carry

        lax.fori_loop(0, out.shape[0] // b, some, 0)
        start += out.shape[0]


def compress_slots(first, counts, waves, ranks, spectral, compress, late):
    b = min(group(count) for count in (first, *counts) if count)
    nb, cols = spectral.shape[1:]
    width = compress.shape[2]
    count = sum(counts)
    shapes = [(n, width, cols) for n in counts]
    return call(
        functools.partial(compress_kernel, first, b),
        "compress_slots",
        (waves, ranks),
        (spectral, compress),
        [HBM, HBM],
        [pl.BlockSpec(s, lambda i, *_: (0, 0, 0)) for s in shapes],
        [jax.ShapeDtypeStruct(s, jnp.bfloat16) for s in shapes],
        1,
        0 * count * nb * width * cols,
        late,
        [
            pltpu.VMEM((count, nb, cols), spectral.dtype),
            pltpu.VMEM((count, nb, width), compress.dtype),
            pltpu.SemaphoreType.DMA((2, count // b)),
        ],
    )


def section_kernel(section, b, ranks, own_ref, peer_ref, v_ref, u_ref, o_ref):
    block = lax.axis_index("deg")
    width, cols = v_ref.shape[1:]
    keep = lax.broadcasted_iota(jnp.int32, (width, cols), 0) < ranks[section, block]
    for j in range(b):
        total = dot_pair(own_ref[j], peer_ref[j], v_ref[j], u_ref[j])
        o_ref[j] = jnp.where(keep, total, 0.0).astype(o_ref.dtype)


def section_slots(section, first, ranks, own, peer, vector, partner, late, cost=0):
    count, width, cols = vector.shape
    b = group(math.gcd(first, count), 10)
    start = first // b
    weight = pl.BlockSpec(
        (None, b, None, width, width), lambda i, *_: (section - 1, start + i, 0, 0, 0)
    )
    part = pl.BlockSpec((b, width, cols), lambda i, *_: (i, 0, 0))
    return call(
        functools.partial(section_kernel, section, b),
        f"section_{section}_slots",
        (ranks,),
        (own, peer, vector, partner),
        [weight, weight, part, part],
        part,
        jax.ShapeDtypeStruct(vector.shape, jnp.bfloat16),
        count // b,
        cost or 4 * count * width * width * cols,
        late,
        (),
        SECTION_LIMIT,
    )


def expand_kernel(b, place, kept_ref, got_ref, both_ref, *refs):
    outs, rows_ref = refs[:-1], refs[-1]
    piece = outs[0].shape[1]
    zone = lax.axis_index("zonal")
    mine = place[0]
    for j in range(b):
        rows_ref[...] = dot_pair(kept_ref[j], got_ref[j], both_ref[mine, j], both_ref[1 - mine, j])
        for offset, out in enumerate(outs):
            at = pl.multiple_of((zone ^ offset) * piece, piece)
            out[j] = rows_ref[pl.ds(at, piece), :].astype(out.dtype)


def expand_pieces(first, place, expand, got, both, pieces, late):
    count, width, cols = both.shape[1:]
    rows = expand.shape[2] // 2
    piece = rows // pieces
    b = group(math.gcd(first, count), 4)
    start = first // b
    weight = pl.BlockSpec((b, None, rows, width), lambda i, p: (start + i, 0, p[0], 0))
    return call(
        functools.partial(expand_kernel, b),
        "expand_pieces",
        (place,),
        (expand, got, both),
        [weight, weight, pl.BlockSpec((2, b, width, cols), lambda i, *_: (0, i, 0, 0))],
        [pl.BlockSpec((b, piece, cols), lambda i, *_: (i, 0, 0))] * pieces,
        [jax.ShapeDtypeStruct((count, piece, cols), jnp.bfloat16)] * pieces,
        count // b,
        4 * count * rows * width * cols,
        late,
        [pltpu.VMEM((rows, cols), jnp.float32)],
        EXPAND_LIMIT,
    )


def split_halves(holding, which_dim, my_bit):
    first_half = lax.index_in_dim(holding, 0, which_dim, keepdims=False)
    second_half = lax.index_in_dim(holding, 1, which_dim, keepdims=False)
    kept_half = jnp.where(my_bit == 0, first_half, second_half)
    given_half = jnp.where(my_bit == 0, second_half, first_half)
    return (kept_half, given_half)


def reduce_bands(expansion, vector, low_bits, deg_index):
    slots, rows = expansion.shape[:2]
    holding = jnp.einsum("mrk,mkc->mrc", expansion, vector, preferred_element_type=jnp.float32)
    holding = holding.reshape((slots,) + (2,) * low_bits + (rows >> low_bits, vector.shape[2]))
    for bit in range(low_bits - 1, -1, -1):
        kept_half, given_half = split_halves(holding, 1, deg_index >> bit & 1)
        holding = kept_half + from_partner(given_half, "deg", 1 << bit, "band_halves")
    return holding.astype(jnp.bfloat16)


def body(spectral, wavenumbers, compress, section_own, section_peer, expand, block_ranks):
    deg_count = lax.axis_size("deg")
    zones = lax.axis_size("zonal")
    deg_index = lax.axis_index("deg")
    zone = lax.axis_index("zonal")
    levels_total = deg_count.bit_length() - 1
    low_bits = levels_total - SECTIONS
    slots = spectral.shape[0]
    cols = spectral.shape[2]
    rows = expand.shape[2]
    band = rows >> low_bits
    piece = band // zones
    pairwise = low_bits == 1 and zones == 4 and piece % 16 == 0

    firsts = [sum(CHUNKS[:k]) for k in range(len(CHUNKS))]
    assert sum(CHUNKS) == slots
    late, sent, state = [], {}, {}

    def gate(waits):
        return late[-1:] + [array for w in waits for array in sent[w]]

    def send(name, array, axis, offset):
        sent[name] = [from_partner(array, axis, offset, name)]
        return sent[name][0]

    def run(step, ks, waits):
        k = ks[0]
        first, count = firsts[k], CHUNKS[k]
        if step == "C":
            counts = [CHUNKS[k] for k in ks]
            outs = compress_slots(
                first, counts, wavenumbers, block_ranks, spectral, compress, gate(waits)
            )
            late.append(outs[-1])
            for k, out in zip(ks, outs):
                state[k] = out
                send(f"P1_{k}", out, "deg", deg_count >> 1)
        elif step in "12":
            section = int(step)
            out = section_slots(
                section, first, block_ranks, section_own, section_peer,
                state[k], sent[f"P{step}_{k}"][0], gate(waits), COSTS.get(f"{step}{k}", 0),
            )
            late.append(out)
            state[k] = out
            if section < SECTIONS:
                send(f"P{section + 1}_{k}", out, "deg", deg_count >> section + 1)
            elif pairwise:
                groups = [[i, i + 1] for i in range(0, deg_count, 2)]
                state[k] = lax.all_gather(out, "deg", axis_index_groups=groups)
        elif step == "G" and pairwise:
            send("PG_0", expand, "deg", 1)
        elif step == "E" and pairwise:
            parts = expand_pieces(
                first, place, expand, sent["PG_0"][0], state[k], zones, gate(waits)
            )
            late.append(parts[0])
            state[k] = parts
            sent[f"P4_{k}"] = [
                send(f"P4{offset}_{k}", part, "zonal", offset)
                for offset, part in enumerate(parts) if offset
            ]
        elif step == "E":
            part = reduce_bands(expand[first : first + count, 0], state[k], low_bits, deg_index)
            part = lax.all_to_all(part, "zonal", split_axis=1, concat_axis=0, tiled=True)
            state[k] = part.reshape(zones, count, piece, cols)

    if pairwise:
        place = (deg_index & 1).astype(jnp.int32)[None]
    for item in ORDER:
        step, _, waits = item.partition("<")
        with jax.named_scope("K" + step):
            run(step[0], [int(k) for k in step[1:]], waits.split(",") if waits and pairwise else [])

    if not pairwise:
        out = jnp.concatenate([state[k] for k in range(len(CHUNKS))], axis=1)
        return out.reshape(zones * slots, 1, 1, piece, cols)
    out = jnp.zeros((zones * slots, piece, cols), jnp.bfloat16)
    last = len(CHUNKS) - 1
    for k in [last, *range(last)]:
        at = zone * slots + firsts[k]
        out = lax.dynamic_update_slice(out, state[k][0], (at, 0, 0))
    for k in range(last + 1):
        for offset, part in enumerate(sent[f"P4_{k}"], 1):
            at = (zone ^ offset) * slots + firsts[k]
            out = lax.dynamic_update_slice(out, part, (at, 0, 0))
    return out.reshape(zones * slots, 1, 1, piece, cols)


def solution(mesh):
    in_specs = (
        P("zonal", "deg", None),
        P("zonal"),
        P("zonal", "deg", None),
        P(None, "zonal", "deg", None, None),
        P(None, "zonal", "deg", None, None),
        P("zonal", "deg", None, None),
        P(),
    )
    out_specs = P(None, "deg", "zonal", None, None)
    return jax.shard_map(body, mesh=mesh, in_specs=in_specs, out_specs=out_specs, check_vma=False)
```

time: 115 us -> 96.3 us (0.84)
  waiting for transfers between devices: 45.8 us -> 27.3 us
  blocking collectives: 0 us -> 8.71 us
  starting transfers between devices: 36.7 us -> 28.3 us
  local copies, waits for them, and re-layouts: 9.8 us -> 2.77 us
  Pallas kernels: 22.2 us -> 28.4 us
    ppermute x31 -> x21, waiting for transfers between devices: 45.8 us -> 27.3 us  [from_partner(): return lax.ppermute(array, axis, pairs)]
    all_gather x0 -> x4, blocking collectives: none -> 8.71 us  [run(): state[k] = lax.all_gather(out, 'deg', axis_index_groups=groups)]
    ppermute x31 -> x21, starting transfers between devices: 36.7 us -> 28.3 us  [from_partner(): return lax.ppermute(array, axis, pairs)]
    pallas_call x20 -> x14, Pallas kernels: 22.2 us -> 28.4 us  [call(): pl.pallas_call(ordered(kernel, len(scalars) + len(operands), len(late)),...]
    dynamic_slice x1 -> x0, local copies, waits for them, and re-layouts: 3.56 us -> none  [body(): lax.dynamic_slice_in_dim(expand[:, 0], (1 - place[0]) * band, band, axis=1)]
    unnamed x20 -> x8, local copies, waits for them, and re-layouts: 4.85 us -> 1.35 us
  transfers between devices with their start and end apart: 31 -> 21, of which waited for: 15 -> 6; matrix products, arithmetic and copies ran while one was open for 1% -> 1% of each run, Pallas kernels for 19% -> 30%
where the time goes in v2:
time: 96.3 us; the launch traced here: 95.8 us
  Pallas kernels  28.4 us (29%)
  starting transfers between devices  28.3 us (29%)
  waiting for transfers between devices  27.3 us (28%)
  blocking collectives  8.71 us (9%)
  local copies, waits for them, and re-layouts  2.77 us (3%)
    pallas_call x14, Pallas kernels, call(): pl.pallas_call(ordered(kernel, len(scalars) + len(operands), len(late)),...  28.4 us
    ppermute x21, starting transfers between devices, from_partner(): return lax.ppermute(array, axis, pairs)  28.3 us
    ppermute x21, waiting for transfers between devices, from_partner(): return lax.ppermute(array, axis, pairs)  27.3 us
    all_gather x4, blocking collectives, run(): state[k] = lax.all_gather(out, 'deg', axis_index_groups=groups)  8.71 us
  transfers between devices with their start and end apart: 21, of which 6 were waited for; matrix products, arithmetic and copies ran while one was open for 1% of the time, Pallas kernels for 30%

profile of v2, /device:TPU:0, one launch (start us, length us, event | category | flops | bytes accessed | tf_op | source)
XLA Modules:
  0.0 95.8 jit_solution(4682241064810316120)
XLA Ops:
  1.8 2.3 %compress_slots.2.refs_4_.refs_3_ = bf16[8,128,128]{2,1,0:T(8,128)(2,1)S(1)} custom-call(s32[32]{0:T(128)S(1)} %copy-done.2, s32[3,8]{1,0:T(4,128)S(1)} %copy-done, bf16[32,320,128]{2,1,0:T(8,128)(2,1)} %refs_2_.11, bf16[32,320,128]{2,1,0:T(8,128)(2,1)} %refs_3_.3), custom_call_target="tpu_custom_call" | custom-call | tf_op jit(solution)/shard_map/KC0/compress_slots/pallas_call | solution.py:62
  4.1 3.7 %collective-permute-start.3 = (bf16[8,128,128]{2,1,0:T(8,128)(2,1)S(1)}, bf16[8,128,128]{2,1,0:T(8,128)(2,1)S(1)}, u32[]{:S(2)}, u32[]{:S(2)}) collective-permute-start(bf16[8,128,128]{2,1,0:T(8,128)(2,1)S(1)} %compress_slots.2.refs_4_.refs_3_), channel_id=1, source_target_pairs={{0,4},{1,5},{2,6},{3,7},{4,0},{5,1},{6,2},{7,3},{8,12},{9,13},{10,... | collective-permute-start | bytes 786440 | tf_op jit(solution)/shard_map/KC0/P1_0/ppermute | solution.py:41
  7.7 3.6 %compress_slots.3 = (bf16[8,128,128]{2,1,0:T(8,128)(2,1)S(1)}, bf16[8,128,128]{2,1,0:T(8,128)(2,1)S(1)}, bf16[8,128,128]{2,1,0:T(8,128)(2,1)S(1)}) custom-call(s32[32]{0:T(128)S(1)} %copy-done.2, s32[3,8]{1,0:T(4,128)S(1)} %copy-done, bf16[32,320,128]{2,1,0:T(8,128)(2,1)} %refs_2_.11, bf16[32,320,128]{2,1,0:T(8,128)(2,1)} %refs_3_.3, ...), custom_call_target="tpu_custom_call" | custom-call | tf_op jit(solution)/shard_map/KC123/compress_slots/pallas_call | solution.py:62
  11.4 14.7 %collective-permute-done.3.refs_4_ = bf16[8,128,128]{2,1,0:T(8,128)(2,1)S(1)} collective-permute-done((bf16[8,128,128]{2,1,0:T(8,128)(2,1)S(1)}, bf16[8,128,128]{2,1,0:T(8,128)(2,1)S(1)}, u32[]{:S(2)}, u32[]{:S(2)}) %collective-permute-start.3) | collective-permute-done | bytes 262176 | tf_op jit(solution)/shard_map/KC0/P1_0/ppermute | solution.py:41
  26.1 1.9 %section_1_slots.4.refs_5_.refs_3_ = bf16[8,128,128]{2,1,0:T(8,128)(2,1)S(1)} custom-call(s32[3,8]{1,0:T(4,128)S(1)} %copy-done.1, bf16[2,32,1,128,128]{4,3,2,1,0:T(8,128)(2,1)} %refs_1_.26, bf16[2,32,1,128,128]{4,3,2,1,0:T(8,128)(2,1)} %refs_2_.19, bf16[8,128,128]{2,1,0:T(8,128)(2,1)S(1)} %compress_slots.2.refs_4_.refs_3_, ...), custom_call_target="tpu_custom_call" | custom-call | flops 67108864 | tf_op jit(solution)/shard_map/K10/section_1_slots/pallas_call | solution.py:62
  28.7 3.4 %collective-permute-start.5 = (bf16[8,128,128]{2,1,0:T(8,128)(2,1)S(1)}, bf16[8,128,128]{2,1,0:T(8,128)(2,1)S(1)}, u32[]{:S(2)}, u32[]{:S(2)}) collective-permute-start(bf16[8,128,128]{2,1,0:T(8,128)(2,1)S(1)} %get-tuple-element.26.refs_3_), channel_id=1, source_target_pairs={{0,4},{1,5},{2,6},{3,7},{4,0},{5,1},{6,2},{7,3},{8,12},{9,13},{10,... | collective-permute-start | bytes 786440 | tf_op jit(solution)/shard_map/KC123/P1_2/ppermute | solution.py:41
  32.1 1.9 %section_1_slots.5.refs_5_.refs_3_ = bf16[8,128,128]{2,1,0:T(8,128)(2,1)S(1)} custom-call(s32[3,8]{1,0:T(4,128)S(1)} %copy-done.1, bf16[2,32,1,128,128]{4,3,2,1,0:T(8,128)(2,1)} %refs_1_.26, bf16[2,32,1,128,128]{4,3,2,1,0:T(8,128)(2,1)} %refs_2_.19, bf16[8,128,128]{2,1,0:T(8,128)(2,1)S(1)} %get-tuple-element.25.refs_3_, ...), custom_call_target="tpu_custom_call" | custom-call | flops 67108864 | tf_op jit(solution)/shard_map/K11/section_1_slots/pallas_call | solution.py:62
  34.3 3.5 %collective-permute-start.1 = (bf16[8,128,128]{2,1,0:T(8,128)(2,1)S(1)}, bf16[8,128,128]{2,1,0:T(8,128)(2,1)S(1)}, u32[]{:S(2)}, u32[]{:S(2)}) collective-permute-start(bf16[8,128,128]{2,1,0:T(8,128)(2,1)S(1)} %get-tuple-element.24.refs_5_.refs_3_), channel_id=1, source_target_pairs={{0,4},{1,5},{2,6},{3,7},{4,0},{5,1},{6,2},{7,3},{8,12},{9,13},{10,... | collective-permute-start | bytes 786440 | tf_op jit(solution)/shard_map/KC123/P1_3/ppermute | solution.py:41
  37.7 4.9 %collective-permute-done.6.refs_4_ = bf16[8,128,128]{2,1,0:T(8,128)(2,1)S(1)} collective-permute-done((bf16[8,128,128]{2,1,0:T(8,128)(2,1)S(1)}, bf16[8,128,128]{2,1,0:T(8,128)(2,1)S(1)}, u32[]{:S(2)}, u32[]{:S(2)}) %collective-permute-start.6) | collective-permute-done | bytes 262176 | tf_op jit(solution)/shard_map/K10/P2_0/ppermute | solution.py:41
  42.7 1.9 %section_2_slots.4.refs_4_ = bf16[8,128,128]{2,1,0:T(8,128)(2,1)S(1)} custom-call(s32[3,8]{1,0:T(4,128)S(1)} %copy-done.1, bf16[2,32,1,128,128]{4,3,2,1,0:T(8,128)(2,1)} %refs_1_.26, bf16[2,32,1,128,128]{4,3,2,1,0:T(8,128)(2,1)} %refs_2_.19, bf16[8,128,128]{2,1,0:T(8,128)(2,1)S(1)} %section_1_slots.4.refs_5_.refs_3_, ...), custom_call_target="tpu_custom_call" | custom-call | flops 67108864 | tf_op jit(solution)/shard_map/K20/section_2_slots/pallas_call | solution.py:62
  44.6 2.2 %all-gather = bf16[16,128,128]{2,1,0:T(8,128)(2,1)S(1)} all-gather(bf16[8,128,128]{2,1,0:T(8,128)(2,1)S(1)} %section_2_slots.4.refs_4_), channel_id=2, replica_groups={{0,1},{2,3},{4,5},{6,7},{8,9},{10,11},{12,13},{14,15},{16,17},{18,19},{..., dimensions={0}, use_global_device_ids=true | all-gather | bytes 786432 | tf_op jit(solution)/shard_map/K20/all_gather | solution.py:278
  46.7 1.9 %expand_pieces.4 = (bf16[8,80,128]{2,1,0:T(8,128)(2,1)S(1)}, bf16[8,80,128]{2,1,0:T(8,128)(2,1)S(1)}, bf16[8,80,128]{2,1,0:T(8,128)(2,1)S(1)}, bf16[8,80,128]{2,1,0:T(8,128)(2,1)S(1)}) custom-call(s32[1]{0:T(128)} %bitcast.refs_0_, bf16[32,1,640,128]{3,2,1,0:T(8,128)(2,1)} %refs_1_.27, bf16[32,1,640,128]{3,2,1,0:T(8,128)(2,1)} %collective-permute-done.refs_2_, ...), custom_call_target="tpu_custom_call" | custom-call | flops 167772160 | tf_op jit(solution)/shard_map/KE0/expand_pieces/pallas_call | solution.py:62
  48.6 1.9 %section_1_slots.6.refs_5_.refs_3_ = bf16[8,128,128]{2,1,0:T(8,128)(2,1)S(1)} custom-call(s32[3,8]{1,0:T(4,128)S(1)} %copy-done.1, bf16[2,32,1,128,128]{4,3,2,1,0:T(8,128)(2,1)} %refs_1_.26, bf16[2,32,1,128,128]{4,3,2,1,0:T(8,128)(2,1)} %refs_2_.19, bf16[8,128,128]{2,1,0:T(8,128)(2,1)S(1)} %get-tuple-element.26.refs_3_, ...), custom_call_target="tpu_custom_call" | custom-call | flops 67108864 | tf_op jit(solution)/shard_map/K12/section_1_slots/pallas_call | solution.py:62
  50.6 1.8 %collective-permute-start.10 = (bf16[8,80,128]{2,1,0:T(8,128)(2,1)S(1)}, bf16[8,80,128]{2,1,0:T(8,128)(2,1)S(1)}, u32[]{:S(2)}, u32[]{:S(2)}) collective-permute-start(bf16[8,80,128]{2,1,0:T(8,128)(2,1)S(1)} %get-tuple-element.30), channel_id=1, source_target_pairs={{0,16},{8,24},{16,0},{24,8},{1,17},{9,25},{17,1},{25,9},{2,18},{10... | collective-permute-start | bytes 491528 | tf_op jit(solution)/shard_map/KE0/P42_0/ppermute | solution.py:41
  53.9 1.9 %section_2_slots.5.refs_4_ = bf16[8,128,128]{2,1,0:T(8,128)(2,1)S(1)} custom-call(s32[3,8]{1,0:T(4,128)S(1)} %copy-done.1, bf16[2,32,1,128,128]{4,3,2,1,0:T(8,128)(2,1)} %refs_1_.26, bf16[2,32,1,128,128]{4,3,2,1,0:T(8,128)(2,1)} %refs_2_.19, bf16[8,128,128]{2,1,0:T(8,128)(2,1)S(1)} %section_1_slots.5.refs_5_.refs_3_, ...), custom_call_target="tpu_custom_call" | custom-call | flops 67108864 | tf_op jit(solution)/shard_map/K21/section_2_slots/pallas_call | solution.py:62
  55.8 2.2 %all-gather.1 = bf16[16,128,128]{2,1,0:T(8,128)(2,1)S(1)} all-gather(bf16[8,128,128]{2,1,0:T(8,128)(2,1)S(1)} %section_2_slots.5.refs_4_), channel_id=3, replica_groups={{0,1},{2,3},{4,5},{6,7},{8,9},{10,11},{12,13},{14,15},{16,17},{18,19},{..., dimensions={0}, use_global_device_ids=true | all-gather | bytes 786432 | tf_op jit(solution)/shard_map/K21/all_gather | solution.py:278
  58.0 1.9 %expand_pieces.5 = (bf16[8,80,128]{2,1,0:T(8,128)(2,1)S(1)}, bf16[8,80,128]{2,1,0:T(8,128)(2,1)S(1)}, bf16[8,80,128]{2,1,0:T(8,128)(2,1)S(1)}, bf16[8,80,128]{2,1,0:T(8,128)(2,1)S(1)}) custom-call(s32[1]{0:T(128)} %bitcast.refs_0_, bf16[32,1,640,128]{3,2,1,0:T(8,128)(2,1)} %refs_1_.27, bf16[32,1,640,128]{3,2,1,0:T(8,128)(2,1)} %collective-permute-done.refs_2_, ...), custom_call_target="tpu_custom_call" | custom-call | flops 167772160 | tf_op jit(solution)/shard_map/KE1/expand_pieces/pallas_call | solution.py:62
  59.9 1.9 %section_1_slots.7.refs_5_.refs_3_ = bf16[8,128,128]{2,1,0:T(8,128)(2,1)S(1)} custom-call(s32[3,8]{1,0:T(4,128)S(1)} %copy-done.1, bf16[2,32,1,128,128]{4,3,2,1,0:T(8,128)(2,1)} %refs_1_.26, bf16[2,32,1,128,128]{4,3,2,1,0:T(8,128)(2,1)} %refs_2_.19, bf16[8,128,128]{2,1,0:T(8,128)(2,1)S(1)} %get-tuple-element.24.refs_5_.refs_3_, ...), custom_call_target="tpu_custom_call" | custom-call | flops 67108864 | tf_op jit(solution)/shard_map/K13/section_1_slots/pallas_call | solution.py:62
  61.8 2.0 %collective-permute-start.7 = (bf16[8,128,128]{2,1,0:T(8,128)(2,1)S(1)}, bf16[8,128,128]{2,1,0:T(8,128)(2,1)S(1)}, u32[]{:S(2)}, u32[]{:S(2)}) collective-permute-start(bf16[8,128,128]{2,1,0:T(8,128)(2,1)S(1)} %section_1_slots.7.refs_5_.refs_3_), channel_id=1, source_target_pairs={{0,2},{1,3},{2,0},{3,1},{4,6},{5,7},{6,4},{7,5},{8,10},{9,11},{10,... | collective-permute-start | bytes 786440 | tf_op jit(solution)/shard_map/K13/P2_3/ppermute | solution.py:41
  64.0 1.7 %collective-permute-start.12 = (bf16[8,80,128]{2,1,0:T(8,128)(2,1)S(1)}, bf16[8,80,128]{2,1,0:T(8,128)(2,1)S(1)}, u32[]{:S(2)}, u32[]{:S(2)}) collective-permute-start(bf16[8,80,128]{2,1,0:T(8,128)(2,1)S(1)} %get-tuple-element.33), channel_id=1, source_target_pairs={{0,8},{8,0},{16,24},{24,16},{1,9},{9,1},{17,25},{25,17},{2,10},{10... | collective-permute-start | bytes 491528 | tf_op jit(solution)/shard_map/KE1/P41_1/ppermute | solution.py:41
  65.8 1.9 %section_2_slots.6.refs_4_ = bf16[8,128,128]{2,1,0:T(8,128)(2,1)S(1)} custom-call(s32[3,8]{1,0:T(4,128)S(1)} %copy-done.1, bf16[2,32,1,128,128]{4,3,2,1,0:T(8,128)(2,1)} %refs_1_.26, bf16[2,32,1,128,128]{4,3,2,1,0:T(8,128)(2,1)} %refs_2_.19, bf16[8,128,128]{2,1,0:T(8,128)(2,1)S(1)} %section_1_slots.6.refs_5_.refs_3_, ...), custom_call_target="tpu_custom_call" | custom-call | flops 67108864 | tf_op jit(solution)/shard_map/K22/section_2_slots/pallas_call | solution.py:62
  67.7 1.6 %collective-permute-start.13 = (bf16[8,80,128]{2,1,0:T(8,128)(2,1)S(1)}, bf16[8,80,128]{2,1,0:T(8,128)(2,1)S(1)}, u32[]{:S(2)}, u32[]{:S(2)}) collective-permute-start(bf16[8,80,128]{2,1,0:T(8,128)(2,1)S(1)} %get-tuple-element.34), channel_id=1, source_target_pairs={{0,16},{8,24},{16,0},{24,8},{1,17},{9,25},{17,1},{25,9},{2,18},{10... | collective-permute-start | bytes 491528 | tf_op jit(solution)/shard_map/KE1/P42_1/ppermute | solution.py:41
  69.5 2.2 %all-gather.2 = bf16[16,128,128]{2,1,0:T(8,128)(2,1)S(1)} all-gather(bf16[8,128,128]{2,1,0:T(8,128)(2,1)S(1)} %section_2_slots.6.refs_4_), channel_id=4, replica_groups={{0,1},{2,3},{4,5},{6,7},{8,9},{10,11},{12,13},{14,15},{16,17},{18,19},{..., dimensions={0}, use_global_device_ids=true | all-gather | bytes 786432 | tf_op jit(solution)/shard_map/K22/all_gather | solution.py:278
  71.7 1.9 %expand_pieces.6 = (bf16[8,80,128]{2,1,0:T(8,128)(2,1)S(1)}, bf16[8,80,128]{2,1,0:T(8,128)(2,1)S(1)}, bf16[8,80,128]{2,1,0:T(8,128)(2,1)S(1)}, bf16[8,80,128]{2,1,0:T(8,128)(2,1)S(1)}) custom-call(s32[1]{0:T(128)} %bitcast.refs_0_, bf16[32,1,640,128]{3,2,1,0:T(8,128)(2,1)} %refs_1_.27, bf16[32,1,640,128]{3,2,1,0:T(8,128)(2,1)} %collective-permute-done.refs_2_, ...), custom_call_target="tpu_custom_call" | custom-call | flops 167772160 | tf_op jit(solution)/shard_map/KE2/expand_pieces/pallas_call | solution.py:62
  73.5 1.8 %collective-permute-start.15 = (bf16[8,80,128]{2,1,0:T(8,128)(2,1)S(1)}, bf16[8,80,128]{2,1,0:T(8,128)(2,1)S(1)}, u32[]{:S(2)}, u32[]{:S(2)}) collective-permute-start(bf16[8,80,128]{2,1,0:T(8,128)(2,1)S(1)} %get-tuple-element.37), channel_id=1, source_target_pairs={{0,8},{8,0},{16,24},{24,16},{1,9},{9,1},{17,25},{25,17},{2,10},{10... | collective-permute-start | bytes 491528 | tf_op jit(solution)/shard_map/KE2/P41_2/ppermute | solution.py:41
  76.9 1.9 %section_2_slots.7.refs_4_ = bf16[8,128,128]{2,1,0:T(8,128)(2,1)S(1)} custom-call(s32[3,8]{1,0:T(4,128)S(1)} %copy-done.1, bf16[2,32,1,128,128]{4,3,2,1,0:T(8,128)(2,1)} %refs_1_.26, bf16[2,32,1,128,128]{4,3,2,1,0:T(8,128)(2,1)} %refs_2_.19, bf16[8,128,128]{2,1,0:T(8,128)(2,1)S(1)} %section_1_slots.7.refs_5_.refs_3_, ...), custom_call_target="tpu_custom_call" | custom-call | flops 67108864 | tf_op jit(solution)/shard_map/K23/section_2_slots/pallas_call | solution.py:62
  78.8 2.2 %all-gather.3 = bf16[16,128,128]{2,1,0:T(8,128)(2,1)S(1)} all-gather(bf16[8,128,128]{2,1,0:T(8,128)(2,1)S(1)} %section_2_slots.7.refs_4_), channel_id=5, replica_groups={{0,1},{2,3},{4,5},{6,7},{8,9},{10,11},{12,13},{14,15},{16,17},{18,19},{..., dimensions={0}, use_global_device_ids=true | all-gather | bytes 786432 | tf_op jit(solution)/shard_map/K23/all_gather | solution.py:278
  81.2 1.9 %expand_pieces.7 = (bf16[8,80,128]{2,1,0:T(8,128)(2,1)S(1)}, bf16[8,80,128]{2,1,0:T(8,128)(2,1)S(1)}, bf16[8,80,128]{2,1,0:T(8,128)(2,1)S(1)}, bf16[8,80,128]{2,1,0:T(8,128)(2,1)S(1)}) custom-call(s32[1]{0:T(128)} %bitcast.refs_0_, bf16[32,1,640,128]{3,2,1,0:T(8,128)(2,1)} %refs_1_.27, bf16[32,1,640,128]{3,2,1,0:T(8,128)(2,1)} %collective-permute-done.refs_2_, ...), custom_call_target="tpu_custom_call" | custom-call | flops 167772160 | tf_op jit(solution)/shard_map/KE3/expand_pieces/pallas_call | solution.py:62
  83.1 1.8 %collective-permute-start.18 = (bf16[8,80,128]{2,1,0:T(8,128)(2,1)S(1)}, bf16[8,80,128]{2,1,0:T(8,128)(2,1)S(1)}, u32[]{:S(2)}, u32[]{:S(2)}) collective-permute-start(bf16[8,80,128]{2,1,0:T(8,128)(2,1)S(1)} %get-tuple-element.40), channel_id=1, source_target_pairs={{0,8},{8,0},{16,24},{24,16},{1,9},{9,1},{17,25},{25,17},{2,10},{10... | collective-permute-start | bytes 491528 | tf_op jit(solution)/shard_map/KE3/P41_3/ppermute | solution.py:41
  84.9 1.6 %collective-permute-start.19 = (bf16[8,80,128]{2,1,0:T(8,128)(2,1)S(1)}, bf16[8,80,128]{2,1,0:T(8,128)(2,1)S(1)}, u32[]{:S(2)}, u32[]{:S(2)}) collective-permute-start(bf16[8,80,128]{2,1,0:T(8,128)(2,1)S(1)} %get-tuple-element.41), channel_id=1, source_target_pairs={{0,16},{8,24},{16,0},{24,8},{1,17},{9,25},{17,1},{25,9},{2,18},{10... | collective-permute-start | bytes 491528 | tf_op jit(solution)/shard_map/KE3/P42_3/ppermute | solution.py:41
  89.0 2.5 %collective-permute-done.18 = bf16[8,80,128]{2,1,0:T(8,128)(2,1)S(1)} collective-permute-done((bf16[8,80,128]{2,1,0:T(8,128)(2,1)S(1)}, bf16[8,80,128]{2,1,0:T(8,128)(2,1)S(1)}, u32[]{:S(2)}, u32[]{:S(2)}) %collective-permute-start.18) | collective-permute-done | bytes 163872 | tf_op jit(solution)/shard_map/KE3/P41_3/ppermute | solution.py:41
  91.5 2.1 %collective-permute-done.19 = bf16[8,80,128]{2,1,0:T(8,128)(2,1)S(1)} collective-permute-done((bf16[8,80,128]{2,1,0:T(8,128)(2,1)S(1)}, bf16[8,80,128]{2,1,0:T(8,128)(2,1)S(1)}, u32[]{:S(2)}, u32[]{:S(2)}) %collective-permute-start.19) | collective-permute-done | bytes 163872 | tf_op jit(solution)/shard_map/KE3/P42_3/ppermute | solution.py:41
  (53 shorter events, 11.2 us)
Async XLA Ops:
  0.0 46.7 %collective-permute-start = (bf16[32,1,640,128]{3,2,1,0:T(8,128)(2,1)}, bf16[32,1,640,128]{3,2,1,0:T(8,128)(2,1)}, u32[]{:S(2)}, u32[]{:S(2)}) collective-permute-start(bf16[32,1,640,128]{3,2,1,0:T(8,128)(2,1)} %refs_1_.27), channel_id=1, source_target_pairs={{0,1},{1,0},{2,3},{3,2},{4,5},{5,4},{6,7},{7,6},{8,9},{9,8},{10,11... | collective-permute-start | bytes 15728648 | tf_op jit(solution)/shard_map/KG0/PG_0/ppermute | solution.py:41
  0.5 0.7 copy-start
  1.1 0.7 copy-start.2
  4.1 22.1 %copy-start.1 = (s32[3,8]{1,0:T(4,128)S(1)}, s32[3,8]{1,0:T(4,128)}, u32[]{:S(2)}) copy-start(s32[3,8]{1,0:T(4,128)} %refs_0_.19) | copy-start | bytes 292
  4.1 22.0 %collective-permute-start.3 = (bf16[8,128,128]{2,1,0:T(8,128)(2,1)S(1)}, bf16[8,128,128]{2,1,0:T(8,128)(2,1)S(1)}, u32[]{:S(2)}, u32[]{:S(2)}) collective-permute-start(bf16[8,128,128]{2,1,0:T(8,128)(2,1)S(1)} %compress_slots.2.refs_4_.refs_3_), channel_id=1, source_target_pairs={{0,4},{1,5},{2,6},{3,7},{4,0},{5,1},{6,2},{7,3},{8,12},{9,13},{10,... | collective-permute-start | bytes 786440 | tf_op jit(solution)/shard_map/KC0/P1_0/ppermute | solution.py:41
  11.3 20.8 %collective-permute-start.2 = (bf16[8,128,128]{2,1,0:T(8,128)(2,1)S(1)}, bf16[8,128,128]{2,1,0:T(8,128)(2,1)S(1)}, u32[]{:S(2)}, u32[]{:S(2)}) collective-permute-start(bf16[8,128,128]{2,1,0:T(8,128)(2,1)S(1)} %get-tuple-element.25.refs_3_), channel_id=1, source_target_pairs={{0,4},{1,5},{2,6},{3,7},{4,0},{5,1},{6,2},{7,3},{8,12},{9,13},{10,... | collective-permute-start | bytes 786440 | tf_op jit(solution)/shard_map/KC123/P1_1/ppermute | solution.py:41
  28.0 14.6 %collective-permute-start.6 = (bf16[8,128,128]{2,1,0:T(8,128)(2,1)S(1)}, bf16[8,128,128]{2,1,0:T(8,128)(2,1)S(1)}, u32[]{:S(2)}, u32[]{:S(2)}) collective-permute-start(bf16[8,128,128]{2,1,0:T(8,128)(2,1)S(1)} %section_1_slots.4.refs_5_.refs_3_), channel_id=1, source_target_pairs={{0,2},{1,3},{2,0},{3,1},{4,6},{5,7},{6,4},{7,5},{8,10},{9,11},{10,... | collective-permute-start | bytes 786440 | tf_op jit(solution)/shard_map/K10/P2_0/ppermute | solution.py:41
  28.7 19.9 %collective-permute-start.5 = (bf16[8,128,128]{2,1,0:T(8,128)(2,1)S(1)}, bf16[8,128,128]{2,1,0:T(8,128)(2,1)S(1)}, u32[]{:S(2)}, u32[]{:S(2)}) collective-permute-start(bf16[8,128,128]{2,1,0:T(8,128)(2,1)S(1)} %get-tuple-element.26.refs_3_), channel_id=1, source_target_pairs={{0,4},{1,5},{2,6},{3,7},{4,0},{5,1},{6,2},{7,3},{8,12},{9,13},{10,... | collective-permute-start | bytes 786440 | tf_op jit(solution)/shard_map/KC123/P1_2/ppermute | solution.py:41
  34.0 19.9 %collective-permute-start.4 = (bf16[8,128,128]{2,1,0:T(8,128)(2,1)S(1)}, bf16[8,128,128]{2,1,0:T(8,128)(2,1)S(1)}, u32[]{:S(2)}, u32[]{:S(2)}) collective-permute-start(bf16[8,128,128]{2,1,0:T(8,128)(2,1)S(1)} %section_1_slots.5.refs_5_.refs_3_), channel_id=1, source_target_pairs={{0,2},{1,3},{2,0},{3,1},{4,6},{5,7},{6,4},{7,5},{8,10},{9,11},{10,... | collective-permute-start | bytes 786440 | tf_op jit(solution)/shard_map/K11/P2_1/ppermute | solution.py:41
  34.3 25.6 %collective-permute-start.1 = (bf16[8,128,128]{2,1,0:T(8,128)(2,1)S(1)}, bf16[8,128,128]{2,1,0:T(8,128)(2,1)S(1)}, u32[]{:S(2)}, u32[]{:S(2)}) collective-permute-start(bf16[8,128,128]{2,1,0:T(8,128)(2,1)S(1)} %get-tuple-element.24.refs_5_.refs_3_), channel_id=1, source_target_pairs={{0,4},{1,5},{2,6},{3,7},{4,0},{5,1},{6,2},{7,3},{8,12},{9,13},{10,... | collective-permute-start | bytes 786440 | tf_op jit(solution)/shard_map/KC123/P1_3/ppermute | solution.py:41
  50.5 13.5 %collective-permute-start.8 = (bf16[8,128,128]{2,1,0:T(8,128)(2,1)S(1)}, bf16[8,128,128]{2,1,0:T(8,128)(2,1)S(1)}, u32[]{:S(2)}, u32[]{:S(2)}) collective-permute-start(bf16[8,128,128]{2,1,0:T(8,128)(2,1)S(1)} %section_1_slots.6.refs_5_.refs_3_), channel_id=1, source_target_pairs={{0,2},{1,3},{2,0},{3,1},{4,6},{5,7},{6,4},{7,5},{8,10},{9,11},{10,... | collective-permute-start | bytes 786440 | tf_op jit(solution)/shard_map/K12/P2_2/ppermute | solution.py:41
  50.6 17.1 %collective-permute-start.10 = (bf16[8,80,128]{2,1,0:T(8,128)(2,1)S(1)}, bf16[8,80,128]{2,1,0:T(8,128)(2,1)S(1)}, u32[]{:S(2)}, u32[]{:S(2)}) collective-permute-start(bf16[8,80,128]{2,1,0:T(8,128)(2,1)S(1)} %get-tuple-element.30), channel_id=1, source_target_pairs={{0,16},{8,24},{16,0},{24,8},{1,17},{9,25},{17,1},{25,9},{2,18},{10... | collective-permute-start | bytes 491528 | tf_op jit(solution)/shard_map/KE0/P42_0/ppermute | solution.py:41
  52.4 16.8 %collective-permute-start.11 = (bf16[8,80,128]{2,1,0:T(8,128)(2,1)S(1)}, bf16[8,80,128]{2,1,0:T(8,128)(2,1)S(1)}, u32[]{:S(2)}, u32[]{:S(2)}) collective-permute-start(bf16[8,80,128]{2,1,0:T(8,128)(2,1)S(1)} %get-tuple-element.31), channel_id=1, source_target_pairs={{0,24},{8,16},{16,8},{24,0},{1,25},{9,17},{17,9},{25,1},{2,26},{10... | collective-permute-start | bytes 491528 | tf_op jit(solution)/shard_map/KE0/P43_0/ppermute | solution.py:41
  61.8 13.6 %collective-permute-start.7 = (bf16[8,128,128]{2,1,0:T(8,128)(2,1)S(1)}, bf16[8,128,128]{2,1,0:T(8,128)(2,1)S(1)}, u32[]{:S(2)}, u32[]{:S(2)}) collective-permute-start(bf16[8,128,128]{2,1,0:T(8,128)(2,1)S(1)} %section_1_slots.7.refs_5_.refs_3_), channel_id=1, source_target_pairs={{0,2},{1,3},{2,0},{3,1},{4,6},{5,7},{6,4},{7,5},{8,10},{9,11},{10,... | collective-permute-start | bytes 786440 | tf_op jit(solution)/shard_map/K13/P2_3/ppermute | solution.py:41
  63.7 7.9 %collective-permute-start.9 = (bf16[8,80,128]{2,1,0:T(8,128)(2,1)S(1)}, bf16[8,80,128]{2,1,0:T(8,128)(2,1)S(1)}, u32[]{:S(2)}, u32[]{:S(2)}) collective-permute-start(bf16[8,80,128]{2,1,0:T(8,128)(2,1)S(1)} %get-tuple-element.29), channel_id=1, source_target_pairs={{0,8},{8,0},{16,24},{24,16},{1,9},{9,1},{17,25},{25,17},{2,10},{10... | collective-permute-start | bytes 491528 | tf_op jit(solution)/shard_map/KE0/P41_0/ppermute | solution.py:41
  64.0 17.0 %collective-permute-start.12 = (bf16[8,80,128]{2,1,0:T(8,128)(2,1)S(1)}, bf16[8,80,128]{2,1,0:T(8,128)(2,1)S(1)}, u32[]{:S(2)}, u32[]{:S(2)}) collective-permute-start(bf16[8,80,128]{2,1,0:T(8,128)(2,1)S(1)} %get-tuple-element.33), channel_id=1, source_target_pairs={{0,8},{8,0},{16,24},{24,16},{1,9},{9,1},{17,25},{25,17},{2,10},{10... | collective-permute-start | bytes 491528 | tf_op jit(solution)/shard_map/KE1/P41_1/ppermute | solution.py:41
  67.7 13.5 %collective-permute-start.13 = (bf16[8,80,128]{2,1,0:T(8,128)(2,1)S(1)}, bf16[8,80,128]{2,1,0:T(8,128)(2,1)S(1)}, u32[]{:S(2)}, u32[]{:S(2)}) collective-permute-start(bf16[8,80,128]{2,1,0:T(8,128)(2,1)S(1)} %get-tuple-element.34), channel_id=1, source_target_pairs={{0,16},{8,24},{16,0},{24,8},{1,17},{9,25},{17,1},{25,9},{2,18},{10... | collective-permute-start | bytes 491528 | tf_op jit(solution)/shard_map/KE1/P42_1/ppermute | solution.py:41
  69.3 11.9 %collective-permute-start.14 = (bf16[8,80,128]{2,1,0:T(8,128)(2,1)S(1)}, bf16[8,80,128]{2,1,0:T(8,128)(2,1)S(1)}, u32[]{:S(2)}, u32[]{:S(2)}) collective-permute-start(bf16[8,80,128]{2,1,0:T(8,128)(2,1)S(1)} %get-tuple-element.35), channel_id=1, source_target_pairs={{0,24},{8,16},{16,8},{24,0},{1,25},{9,17},{17,9},{25,1},{2,26},{10... | collective-permute-start | bytes 491528 | tf_op jit(solution)/shard_map/KE1/P43_1/ppermute | solution.py:41
  73.5 13.6 %collective-permute-start.15 = (bf16[8,80,128]{2,1,0:T(8,128)(2,1)S(1)}, bf16[8,80,128]{2,1,0:T(8,128)(2,1)S(1)}, u32[]{:S(2)}, u32[]{:S(2)}) collective-permute-start(bf16[8,80,128]{2,1,0:T(8,128)(2,1)S(1)} %get-tuple-element.37), channel_id=1, source_target_pairs={{0,8},{8,0},{16,24},{24,16},{1,9},{9,1},{17,25},{25,17},{2,10},{10... | collective-permute-start | bytes 491528 | tf_op jit(solution)/shard_map/KE2/P41_2/ppermute | solution.py:41
  75.3 12.1 %collective-permute-start.16 = (bf16[8,80,128]{2,1,0:T(8,128)(2,1)S(1)}, bf16[8,80,128]{2,1,0:T(8,128)(2,1)S(1)}, u32[]{:S(2)}, u32[]{:S(2)}) collective-permute-start(bf16[8,80,128]{2,1,0:T(8,128)(2,1)S(1)} %get-tuple-element.38), channel_id=1, source_target_pairs={{0,16},{8,24},{16,0},{24,8},{1,17},{9,25},{17,1},{25,9},{2,18},{10... | collective-permute-start | bytes 491528 | tf_op jit(solution)/shard_map/KE2/P42_2/ppermute | solution.py:41
  81.0 7.9 %collective-permute-start.17 = (bf16[8,80,128]{2,1,0:T(8,128)(2,1)S(1)}, bf16[8,80,128]{2,1,0:T(8,128)(2,1)S(1)}, u32[]{:S(2)}, u32[]{:S(2)}) collective-permute-start(bf16[8,80,128]{2,1,0:T(8,128)(2,1)S(1)} %get-tuple-element.39), channel_id=1, source_target_pairs={{0,24},{8,16},{16,8},{24,0},{1,25},{9,17},{17,9},{25,1},{2,26},{10... | collective-permute-start | bytes 491528 | tf_op jit(solution)/shard_map/KE2/P43_2/ppermute | solution.py:41
  83.1 8.4 %collective-permute-start.18 = (bf16[8,80,128]{2,1,0:T(8,128)(2,1)S(1)}, bf16[8,80,128]{2,1,0:T(8,128)(2,1)S(1)}, u32[]{:S(2)}, u32[]{:S(2)}) collective-permute-start(bf16[8,80,128]{2,1,0:T(8,128)(2,1)S(1)} %get-tuple-element.40), channel_id=1, source_target_pairs={{0,8},{8,0},{16,24},{24,16},{1,9},{9,1},{17,25},{25,17},{2,10},{10... | collective-permute-start | bytes 491528 | tf_op jit(solution)/shard_map/KE3/P41_3/ppermute | solution.py:41
  84.9 8.7 %collective-permute-start.19 = (bf16[8,80,128]{2,1,0:T(8,128)(2,1)S(1)}, bf16[8,80,128]{2,1,0:T(8,128)(2,1)S(1)}, u32[]{:S(2)}, u32[]{:S(2)}) collective-permute-start(bf16[8,80,128]{2,1,0:T(8,128)(2,1)S(1)} %get-tuple-element.41), channel_id=1, source_target_pairs={{0,16},{8,24},{16,0},{24,8},{1,17},{9,25},{17,1},{25,9},{2,18},{10... | collective-permute-start | bytes 491528 | tf_op jit(solution)/shard_map/KE3/P42_3/ppermute | solution.py:41
  87.2 8.0 %collective-permute-start.20 = (bf16[8,80,128]{2,1,0:T(8,128)(2,1)S(1)}, bf16[8,80,128]{2,1,0:T(8,128)(2,1)S(1)}, u32[]{:S(2)}, u32[]{:S(2)}) collective-permute-start(bf16[8,80,128]{2,1,0:T(8,128)(2,1)S(1)} %get-tuple-element.42), channel_id=1, source_target_pairs={{0,24},{8,16},{16,8},{24,0},{1,25},{9,17},{17,9},{25,1},{2,26},{10... | collective-permute-start | bytes 491528 | tf_op jit(solution)/shard_map/KE3/P43_3/ppermute | solution.py:41
  93.6 1.5 %copy-start.3 = (bf16[128,1,1,80,128]{4,3,2,1,0:T(8,128)(2,1)}, bf16[128,1,1,80,128]{4,3,2,1,0:T(8,128)(2,1)S(1)}, u32[]{:S(2)}) copy-start(bf16[128,1,1,80,128]{4,3,2,1,0:T(8,128)(2,1)S(1)} %bitcast_dynamic-update-slice_fusion.1) | copy-start | bytes 7864324

commit v3 on v2

v3 whole, which is shorter than its diff:
```python
import functools
import math

import jax
import jax.numpy as jnp
from jax import lax
from jax.experimental import pallas as pl
from jax.experimental.pallas import tpu as pltpu
from jax.sharding import PartitionSpec as P

SECTIONS = 2
CHUNKS = (8, 8, 8, 8)
ORDER = (
    "C0",
    "C2",
    "G0",
    "C3<PG_0",
    "C1",
    "10",
    "11",
    "20",
    "E0+12",
    "21",
    "E1+13",
    "22",
    "E2+23<P4_0",
    "E3<P4_1",
)
COSTS = {}
VMEM_LIMIT = 832 * 2**16
HBM = pl.BlockSpec(memory_space=pltpu.HBM)
SMEM = pl.BlockSpec(memory_space=pltpu.SMEM)
ANY = pl.BlockSpec(memory_space=pl.ANY)


def from_partner(array, axis, offset, scope):
    pairs = [(i, i ^ offset) for i in range(lax.axis_size(axis))]
    with jax.named_scope(scope):
        return lax.ppermute(array, axis, pairs)


def dot(a, b, contract_a=1):
    return lax.dot_general(
        a, b, (((contract_a,), (0,)), ((), ())), preferred_element_type=jnp.float32
    )


def dot_pair(a, b, v, u):
    return dot(jnp.concatenate([a, b], axis=1), jnp.concatenate([v, u], axis=0))


def ordered(kernel, used, late):
    def run(*refs):
        kernel(*refs[:used], *refs[used + late :])

    return run


def group(count, most=4):
    return max(b for b in range(1, most + 1) if count % b == 0)


def compress_kernel(first, b, waves, ranks, x_hbm, a_hbm, *refs):
    outs, (x_ref, a_ref, sems) = refs[:-3], refs[-3:]
    block = lax.axis_index("deg")
    nb, cols = x_ref.shape[1:]
    width = a_ref.shape[2]

    def copies(g):
        here, there = pl.ds(g * b, b), pl.ds(first + g * b, b)
        return (
            pltpu.make_async_copy(x_hbm.at[there], x_ref.at[here], sems.at[0, g]),
            pltpu.make_async_copy(a_hbm.at[there], a_ref.at[here], sems.at[1, g]),
        )

    for g in range(x_ref.shape[0] // b):
        for copy in copies(g):
            copy.start()
    degree = lax.broadcasted_iota(jnp.int32, (nb, cols), 0) + block * nb
    keep = lax.broadcasted_iota(jnp.int32, (width, cols), 0) < ranks[0, block]
    start = 0
    for out in outs:

        def some(g, carry, out=out, start=start):
            for copy in copies(start // b + g):
                copy.wait()
            for j in range(b):
                slot = g * b + j
                wave = waves[first + start + slot]
                live = jnp.where(degree >= wave, x_ref[start + slot], 0).astype(x_ref.dtype)
                total = dot(a_ref[start + slot], live, 0)
                out[slot] = jnp.where(keep, total, 0.0).astype(out.dtype)
            return carry

        lax.fori_loop(0, out.shape[0] // b, some, 0)
        start += out.shape[0]


def compress_slots(first, counts, waves, ranks, spectral, compress, late):
    b = min(group(count) for count in (first, *counts) if count)
    nb, cols = spectral.shape[1:]
    width = compress.shape[2]
    count = sum(counts)
    shapes = [(n, width, cols) for n in counts]
    return pl.pallas_call(
        ordered(functools.partial(compress_kernel, first, b), 4, len(late)),
        out_shape=[jax.ShapeDtypeStruct(s, jnp.bfloat16) for s in shapes],
        grid=(1,),
        in_specs=[SMEM, SMEM, HBM, HBM] + [ANY] * len(late),
        out_specs=[pl.BlockSpec(s, lambda i: (0, 0, 0)) for s in shapes],
        scratch_shapes=[
            pltpu.VMEM((count, nb, cols), spectral.dtype),
            pltpu.VMEM((count, nb, width), compress.dtype),
            pltpu.SemaphoreType.DMA((2, count // b)),
        ],
        compiler_params=pltpu.CompilerParams(vmem_limit_bytes=VMEM_LIMIT),
        cost_estimate=pl.CostEstimate(flops=0, bytes_accessed=0, transcendentals=0),
        name="compress_slots",
    )(waves, ranks, spectral, compress, *late)


def section_task(section, first, ranks, own, peer, vector, partner):
    count, width, cols = vector.shape
    b = math.gcd(first, count)
    weight = (None, b, None, width, width)
    part = (b, width, cols)

    def kernel(i, ranks, own_ref, peer_ref, v_ref, u_ref, *outs):
        block = lax.axis_index("deg")
        keep = lax.broadcasted_iota(jnp.int32, (width, cols), 0) < ranks[section, block]
        for j in range(b):
            total = dot_pair(own_ref[j], peer_ref[j], v_ref[j], u_ref[j])
            total = jnp.where(keep, total, 0.0).astype(vector.dtype)
            outs[0][j] = total

    def weights(i):
        return (section - 1, first // b + i, 0, 0, 0)

    def parts(i):
        return (i, 0, 0)

    outs = [(jax.ShapeDtypeStruct(vector.shape, vector.dtype), part, parts)]
    ins = [(own, weight, weights), (peer, weight, weights)]
    ins += [(vector, part, parts), (partner, part, parts)]
    return kernel, ins, outs, count // b


def expand_task(first, expand, got, both, pieces):
    _, count, width, cols = both.shape
    b = group(math.gcd(first, count), 4)
    rows = expand.shape[2] // 2
    piece = rows // pieces
    block = (b, None, rows, width)

    def kernel(i, ranks, kept_ref, got_ref, both_ref, *outs):
        zone = lax.axis_index("zonal")
        mine = lax.axis_index("deg") % 2
        rows_ref = outs[-1]
        for j in range(b):
            rows_ref[...] = dot_pair(
                kept_ref[j], got_ref[j], both_ref[mine, j], both_ref[1 - mine, j]
            )
            for offset, out in enumerate(outs[:-1]):
                at = pl.multiple_of((zone ^ offset) * piece, piece)
                out[j] = rows_ref[pl.ds(at, piece), :].astype(out.dtype)

    def weights(i):
        return (first // b + i, 0, lax.axis_index("deg") % 2, 0)

    def parts(i):
        return (i, 0, 0)

    def pairs(i):
        return (0, i, 0, 0)

    shape = jax.ShapeDtypeStruct((count, piece, cols), jnp.bfloat16)
    outs = [(shape, (b, piece, cols), parts)] * pieces
    ins = [(expand, block, weights), (got, block, weights), (both, (2, b, width, cols), pairs)]
    return kernel, ins, outs, count // b


def fused(tasks, ranks, rows, cols, late, flops, held=()):
    starts = [sum(t[3] for t in tasks[:n]) for n in range(len(tasks))]
    ins, in_specs, outs, out_specs = [], [], [], []

    def spec(block, place_of, start, steps):
        def index(i):
            return place_of(jnp.clip(i - start, 0, steps - 1))

        return pl.BlockSpec(block, index)

    for (_, task_ins, task_outs, steps), start in zip(tasks, starts):
        for array, block, place_of in task_ins:
            ins.append(array)
            in_specs.append(spec(block, place_of, start, steps))
        for shape, block, place_of in task_outs:
            outs.append(shape)
            out_specs.append(spec(block, place_of, start, steps))

    def kernel(ranks, *refs):
        i = pl.program_id(0)
        sources = refs[: len(ins)]
        targets = refs[len(ins) + len(late) + len(held) : -1 - len(held)]
        for (run, task_ins, task_outs, steps), start in zip(tasks, starts):
            here, sources = sources[: len(task_ins)], sources[len(task_ins) :]
            there, targets = targets[: len(task_outs)], targets[len(task_outs) :]
            if len(task_outs) == 4:
                there = (*there, refs[-1])
            if len(tasks) == 1:
                run(i, ranks, *here, *there)
            else:

                @pl.when((i >= start) & (i < start + steps))
                def _():
                    run(i - start, ranks, *here, *there)

    return pl.pallas_call(
        kernel,
        out_shape=outs + [jax.ShapeDtypeStruct(h.shape, h.dtype) for h in held],
        grid=(sum(t[3] for t in tasks),),
        in_specs=[SMEM] + in_specs + [ANY] * (len(late) + len(held)),
        out_specs=out_specs + [ANY] * len(held),
        input_output_aliases={
            1 + len(ins) + len(late) + n: len(outs) + n for n in range(len(held))
        },
        scratch_shapes=[pltpu.VMEM((rows, cols), jnp.float32)],
        compiler_params=pltpu.CompilerParams(vmem_limit_bytes=VMEM_LIMIT),
        cost_estimate=pl.CostEstimate(flops=flops, bytes_accessed=0, transcendentals=0),
        name="butterfly_step",
    )(ranks, *ins, *late, *held)


def split_halves(holding, which_dim, my_bit):
    first_half = lax.index_in_dim(holding, 0, which_dim, keepdims=False)
    second_half = lax.index_in_dim(holding, 1, which_dim, keepdims=False)
    kept_half = jnp.where(my_bit == 0, first_half, second_half)
    given_half = jnp.where(my_bit == 0, second_half, first_half)
    return (kept_half, given_half)


def reduce_bands(expansion, vector, low_bits, deg_index):
    slots, rows = expansion.shape[:2]
    holding = jnp.einsum("mrk,mkc->mrc", expansion, vector, preferred_element_type=jnp.float32)
    holding = holding.reshape((slots,) + (2,) * low_bits + (rows >> low_bits, vector.shape[2]))
    for bit in range(low_bits - 1, -1, -1):
        kept_half, given_half = split_halves(holding, 1, deg_index >> bit & 1)
        holding = kept_half + from_partner(given_half, "deg", 1 << bit, "band_halves")
    return holding.astype(jnp.bfloat16)


def body(spectral, wavenumbers, compress, section_own, section_peer, expand, block_ranks):
    deg_count = lax.axis_size("deg")
    zones = lax.axis_size("zonal")
    deg_index = lax.axis_index("deg")
    zone = lax.axis_index("zonal")
    levels_total = deg_count.bit_length() - 1
    low_bits = levels_total - SECTIONS
    slots = spectral.shape[0]
    cols = spectral.shape[2]
    rows = expand.shape[2]
    band = rows >> low_bits
    piece = band // zones
    pairwise = low_bits == 1 and zones == 4 and piece % 16 == 0

    firsts = [sum(CHUNKS[:k]) for k in range(len(CHUNKS))]
    assert sum(CHUNKS) == slots
    late, sent, state = [], {}, {}

    def gate(waits):
        return late[-1:] + [array for w in waits for array in sent[w]]

    def send(name, array, axis, offset):
        sent[name] = [from_partner(array, axis, offset, name)]
        return sent[name][0]

    def gathered(k):
        part = reduce_bands(
            expand[firsts[k] : firsts[k] + CHUNKS[k], 0], state[k], low_bits, deg_index
        )
        part = lax.all_to_all(part, "zonal", split_axis=1, concat_axis=0, tiled=True)
        return part.reshape(zones, CHUNKS[k], piece, cols)

    def stepped(names, waits, hold):
        tasks = []
        for kind, k in names:
            if kind == "E":
                tasks.append(
                    expand_task(firsts[k], expand, sent["PG_0"][0], state[k], zones)
                )
            else:
                tasks.append(
                    section_task(
                        int(kind), firsts[k], block_ranks, section_own, section_peer,
                        state[k], sent[f"P{kind}_{k}"][0],
                    )
                )
        name = "+".join(kind + str(k) for kind, k in names)
        outs = [*fused(
            tasks, block_ranks, band, cols, gate(waits), COSTS.get(name, 0),
            [state[k] for k in hold],
        )]
        for k in hold[::-1]:
            state[k] = outs.pop()
        late.append(outs[0])
        for (kind, k), task in zip(names, tasks):
            made, outs = outs[: len(task[2])], outs[len(task[2]) :]
            if kind == "E":
                state[k] = made
                sent[f"P4_{k}"] = [
                    send(f"P4{offset}_{k}", part, "zonal", offset)
                    for offset, part in enumerate(made) if offset
                ]
            elif kind == "1":
                state[k] = made[0]
                send(f"P2_{k}", made[0], "deg", deg_count >> 2)
            elif pairwise:
                groups = [[i, i + 1] for i in range(0, deg_count, 2)]
                state[k] = lax.all_gather(made[0], "deg", axis_index_groups=groups)
            else:
                state[k] = made[0]

    for item in ORDER:
        names, _, waits = item.partition("<")
        names, _, hold = names.partition("^")
        hold = [int(k) for k in hold]
        waits = waits.split(",") if waits and pairwise else []
        with jax.named_scope("K" + names.replace("+", "_")):
            if names[0] == "C":
                ks = [int(k) for k in names[1:]]
                outs = compress_slots(
                    firsts[ks[0]], [CHUNKS[k] for k in ks], wavenumbers, block_ranks,
                    spectral, compress, gate(waits),
                )
                late.append(outs[-1])
                for k, out in zip(ks, outs):
                    state[k] = out
                    if not any(f"^{k}" in item for item in ORDER):
                        send(f"P1_{k}", out, "deg", deg_count >> 1)
            elif names[0] == "G":
                if pairwise:
                    send("PG_0", expand, "deg", 1)
            else:
                names = [(n[0], int(n[1])) for n in names.split("+")]
                for kind, k in names:
                    if kind == "E" and not pairwise:
                        state[k] = gathered(k)
                names = [n for n in names if pairwise or n[0] != "E"]
                if names:
                    stepped(names, waits, hold)
                    for k in hold:
                        send(f"P1_{k}", state[k], "deg", deg_count >> 1)

    if not pairwise:
        out = jnp.concatenate([state[k] for k in range(len(CHUNKS))], axis=1)
        return out.reshape(zones * slots, 1, 1, piece, cols)
    out = jnp.zeros((zones * slots, piece, cols), jnp.bfloat16)
    last = len(CHUNKS) - 1
    for k in [last, *range(last)]:
        at = zone * slots + firsts[k]
        out = lax.dynamic_update_slice(out, state[k][0], (at, 0, 0))
    for k in range(last + 1):
        for offset, part in enumerate(sent[f"P4_{k}"], 1):
            at = (zone ^ offset) * slots + firsts[k]
            out = lax.dynamic_update_slice(out, part, (at, 0, 0))
    return out.reshape(zones * slots, 1, 1, piece, cols)


def solution(mesh):
    in_specs = (
        P("zonal", "deg", None),
        P("zonal"),
        P("zonal", "deg", None),
        P(None, "zonal", "deg", None, None),
        P(None, "zonal", "deg", None, None),
        P("zonal", "deg", None, None),
        P(),
    )
    out_specs = P(None, "deg", "zonal", None, None)
    return jax.shard_map(body, mesh=mesh, in_specs=in_specs, out_specs=out_specs, check_vma=False)
```

time: 96.3 us -> 90 us (0.935)
  waiting for transfers between devices: 27.3 us -> 17.1 us
  starting transfers between devices: 28.3 us -> 32.2 us
  Pallas kernels: 28.4 us -> 25.6 us
  local copies, waits for them, and re-layouts: 2.77 us -> 5.09 us
    ppermute x21, waiting for transfers between devices: 27.3 us -> 17.1 us  [from_partner(): return lax.ppermute(array, axis, pairs)]
    ppermute x21, starting transfers between devices: 28.3 us -> 32.2 us  [from_partner(): return lax.ppermute(array, axis, pairs)]
    pallas_call x14 -> x13, Pallas kernels: 28.4 us -> 25.6 us  [the longest x9 16.5 us: fused(): pl.pallas_call(kernel, out_shape=outs + [jax.ShapeDtypeStruct(h.shape, h....]
    unnamed x8 -> x12, local copies, waits for them, and re-layouts: 1.35 us -> 3.67 us
  transfers between devices with their start and end apart: 21 -> 21, of which waited for: 6 -> 8; matrix products, arithmetic and copies ran while one was open for 1% -> 1% of each run, Pallas kernels for 30% -> 29%
where the time goes in v3:
time: 90 us; the launch traced here: 89.3 us
  starting transfers between devices  32.2 us (36%)
  Pallas kernels  25.6 us (28%)
  waiting for transfers between devices  17.1 us (19%)
  blocking collectives  9.1 us (10%)
  local copies, waits for them, and re-layouts  5.09 us (6%)
    ppermute x21, starting transfers between devices, from_partner(): return lax.ppermute(array, axis, pairs)  32.2 us
    ppermute x21, waiting for transfers between devices, from_partner(): return lax.ppermute(array, axis, pairs)  17.1 us
    pallas_call x9, Pallas kernels, fused(): pl.pallas_call(kernel, out_shape=outs + [jax.ShapeDtypeStruct(h.shape, h....  16.5 us
    pallas_call x4, Pallas kernels, compress_slots(): pl.pallas_call(ordered(functools.partial(compress_kernel, first, b), 4, l...  9.13 us
    all_gather x4, blocking collectives, stepped(): state[k] = lax.all_gather(made[0], 'deg', axis_index_groups=groups)  9.1 us
    unnamed x12, local copies, waits for them, and re-layouts  3.67 us
  transfers between devices with their start and end apart: 21, of which 8 were waited for; matrix products, arithmetic and copies ran while one was open for 1% of the time, Pallas kernels for 29%

profile of v3, /device:TPU:0, one launch (start us, length us, event | category | flops | bytes accessed | tf_op | source)
XLA Modules:
  0.0 89.3 jit_solution(13793961392574831143)
XLA Ops:
  1.8 2.3 %compress_slots.4.refs_4_.refs_2_ = bf16[8,128,128]{2,1,0:T(8,128)(2,1)S(1)} custom-call(s32[32]{0:T(128)S(1)} %copy-done.3, s32[3,8]{1,0:T(4,128)S(1)} %copy-done.1, bf16[32,320,128]{2,1,0:T(8,128)(2,1)} %refs_2_.7, bf16[32,320,128]{2,1,0:T(8,128)(2,1)} %refs_3_.10), custom_call_target="tpu_custom_call" | custom-call | tf_op jit(solution)/shard_map/KC0/compress_slots/pallas_call | solution.py:105
  4.1 3.7 %collective-permute-start.1 = (bf16[8,128,128]{2,1,0:T(8,128)(2,1)S(1)}, bf16[8,128,128]{2,1,0:T(8,128)(2,1)S(1)}, u32[]{:S(2)}, u32[]{:S(2)}) collective-permute-start(bf16[8,128,128]{2,1,0:T(8,128)(2,1)S(1)} %compress_slots.4.refs_4_.refs_2_), channel_id=1, source_target_pairs={{0,4},{1,5},{2,6},{3,7},{4,0},{5,1},{6,2},{7,3},{8,12},{9,13},{10,... | collective-permute-start | bytes 786440 | tf_op jit(solution)/shard_map/KC0/P1_0/ppermute | solution.py:39
  7.7 2.3 %compress_slots.5.refs_4_.refs_5_ = bf16[8,128,128]{2,1,0:T(8,128)(2,1)S(1)} custom-call(s32[32]{0:T(128)S(1)} %copy-done.3, s32[3,8]{1,0:T(4,128)S(1)} %copy-done.1, bf16[32,320,128]{2,1,0:T(8,128)(2,1)} %refs_2_.7, bf16[32,320,128]{2,1,0:T(8,128)(2,1)} %refs_3_.10, bf16[8,128,128]{2,1,0:T(8,128)(2,1)S(1)} %compress_slots.4.refs_4_.refs_2_), custom_call_target="tpu_custom_call" | custom-call | tf_op jit(solution)/shard_map/KC2/compress_slots/pallas_call | solution.py:105
  10.0 2.3 %copy-done.4 = bf16[32,1,640,128]{3,2,1,0:T(8,128)(2,1)} copy-done((bf16[32,1,640,128]{3,2,1,0:T(8,128)(2,1)}, bf16[32,1,640,128]{3,2,1,0:T(8,128)(2,1)S(1)}, u32[]{:S(2)}) %copy-start.4) | copy-done | bytes 5242904
  12.4 2.3 %compress_slots.6.refs_4_.refs_5_ = bf16[8,128,128]{2,1,0:T(8,128)(2,1)S(1)} custom-call(s32[32]{0:T(128)S(1)} %copy-done.3, s32[3,8]{1,0:T(4,128)S(1)} %copy-done.1, bf16[32,320,128]{2,1,0:T(8,128)(2,1)} %refs_2_.7, bf16[32,320,128]{2,1,0:T(8,128)(2,1)} %refs_3_.10, bf16[8,128,128]{2,1,0:T(8,128)(2,1)S(1)} %compress_slots.5.refs_4_.refs_5_, ...), custom_call_target="tpu_custom_call" | custom-call | tf_op jit(solution)/shard_map/KC3/compress_slots/pallas_call | solution.py:105
  14.7 2.3 %compress_slots.7.refs_4_.refs_2_ = bf16[8,128,128]{2,1,0:T(8,128)(2,1)S(1)} custom-call(s32[32]{0:T(128)S(1)} %copy-done.3, s32[3,8]{1,0:T(4,128)S(1)} %copy-done.1, bf16[32,320,128]{2,1,0:T(8,128)(2,1)} %refs_2_.7, bf16[32,320,128]{2,1,0:T(8,128)(2,1)} %refs_3_.10, bf16[8,128,128]{2,1,0:T(8,128)(2,1)S(1)} %compress_slots.6.refs_4_.refs_5_), custom_call_target="tpu_custom_call" | custom-call | tf_op jit(solution)/shard_map/KC1/compress_slots/pallas_call | solution.py:105
  16.9 2.9 %collective-permute-start.3 = (bf16[8,128,128]{2,1,0:T(8,128)(2,1)S(1)}, bf16[8,128,128]{2,1,0:T(8,128)(2,1)S(1)}, u32[]{:S(2)}, u32[]{:S(2)}) collective-permute-start(bf16[8,128,128]{2,1,0:T(8,128)(2,1)S(1)} %compress_slots.7.refs_4_.refs_2_), channel_id=1, source_target_pairs={{0,4},{1,5},{2,6},{3,7},{4,0},{5,1},{6,2},{7,3},{8,12},{9,13},{10,... | collective-permute-start | bytes 786440 | tf_op jit(solution)/shard_map/KC1/P1_1/ppermute | solution.py:39
  20.3 1.3 %butterfly_step.9.refs_4_.refs_2_ = bf16[8,128,128]{2,1,0:T(8,128)(2,1)S(1)} custom-call(s32[3,8]{1,0:T(4,128)S(1)} %copy-done.1, bf16[2,32,1,128,128]{4,3,2,1,0:T(8,128)(2,1)} %refs_3_.13, bf16[2,32,1,128,128]{4,3,2,1,0:T(8,128)(2,1)} %refs_4_.5, bf16[8,128,128]{2,1,0:T(8,128)(2,1)S(1)} %compress_slots.4.refs_4_.refs_2_, ...), custom_call_target="tpu_custom_call" | custom-call | tf_op jit(solution)/shard_map/K10/butterfly_step/pallas_call | solution.py:217
  22.9 3.0 %collective-permute-start.4 = (bf16[8,128,128]{2,1,0:T(8,128)(2,1)S(1)}, bf16[8,128,128]{2,1,0:T(8,128)(2,1)S(1)}, u32[]{:S(2)}, u32[]{:S(2)}) collective-permute-start(bf16[8,128,128]{2,1,0:T(8,128)(2,1)S(1)} %compress_slots.5.refs_4_.refs_5_), channel_id=1, source_target_pairs={{0,4},{1,5},{2,6},{3,7},{4,0},{5,1},{6,2},{7,3},{8,12},{9,13},{10,... | collective-permute-start | bytes 786440 | tf_op jit(solution)/shard_map/KC2/P1_2/ppermute | solution.py:39
  25.8 7.1 %collective-permute-done.3.refs_3_ = bf16[8,128,128]{2,1,0:T(8,128)(2,1)S(1)} collective-permute-done((bf16[8,128,128]{2,1,0:T(8,128)(2,1)S(1)}, bf16[8,128,128]{2,1,0:T(8,128)(2,1)S(1)}, u32[]{:S(2)}, u32[]{:S(2)}) %collective-permute-start.3) | collective-permute-done | bytes 262176 | tf_op jit(solution)/shard_map/KC1/P1_1/ppermute | solution.py:39
  33.0 1.3 %butterfly_step.10.refs_4_.refs_2_ = bf16[8,128,128]{2,1,0:T(8,128)(2,1)S(1)} custom-call(s32[3,8]{1,0:T(4,128)S(1)} %copy-done.1, bf16[2,32,1,128,128]{4,3,2,1,0:T(8,128)(2,1)} %refs_3_.13, bf16[2,32,1,128,128]{4,3,2,1,0:T(8,128)(2,1)} %refs_4_.5, bf16[8,128,128]{2,1,0:T(8,128)(2,1)S(1)} %compress_slots.7.refs_4_.refs_2_, ...), custom_call_target="tpu_custom_call" | custom-call | tf_op jit(solution)/shard_map/K11/butterfly_step/pallas_call | solution.py:217
  34.9 3.6 %collective-permute-start.7 = (bf16[8,128,128]{2,1,0:T(8,128)(2,1)S(1)}, bf16[8,128,128]{2,1,0:T(8,128)(2,1)S(1)}, u32[]{:S(2)}, u32[]{:S(2)}) collective-permute-start(bf16[8,128,128]{2,1,0:T(8,128)(2,1)S(1)} %compress_slots.6.refs_4_.refs_5_), channel_id=1, source_target_pairs={{0,4},{1,5},{2,6},{3,7},{4,0},{5,1},{6,2},{7,3},{8,12},{9,13},{10,... | collective-permute-start | bytes 786440 | tf_op jit(solution)/shard_map/KC3/P1_3/ppermute | solution.py:39
  38.6 1.3 %butterfly_step.11.refs_7_ = bf16[8,128,128]{2,1,0:T(8,128)(2,1)S(1)} custom-call(s32[3,8]{1,0:T(4,128)S(1)} %copy-done.1, bf16[2,32,1,128,128]{4,3,2,1,0:T(8,128)(2,1)} %refs_3_.13, bf16[2,32,1,128,128]{4,3,2,1,0:T(8,128)(2,1)} %refs_4_.5, bf16[8,128,128]{2,1,0:T(8,128)(2,1)S(1)} %butterfly_step.9.refs_4_.refs_2_, ...), custom_call_target="tpu_custom_call" | custom-call | tf_op jit(solution)/shard_map/K20/butterfly_step/pallas_call | solution.py:217
  39.9 2.3 %all-gather = bf16[16,128,128]{2,1,0:T(8,128)(2,1)} all-gather(bf16[8,128,128]{2,1,0:T(8,128)(2,1)S(1)} %butterfly_step.11.refs_7_), channel_id=2, replica_groups={{0,1},{2,3},{4,5},{6,7},{8,9},{10,11},{12,13},{14,15},{16,17},{18,19},{..., dimensions={0}, use_global_device_ids=true | all-gather | bytes 786432 | tf_op jit(solution)/shard_map/K20/all_gather | solution.py:318
  42.2 1.9 %collective-permute-done.4.refs_6_ = bf16[8,128,128]{2,1,0:T(8,128)(2,1)S(1)} collective-permute-done((bf16[8,128,128]{2,1,0:T(8,128)(2,1)S(1)}, bf16[8,128,128]{2,1,0:T(8,128)(2,1)S(1)}, u32[]{:S(2)}, u32[]{:S(2)}) %collective-permute-start.4) | collective-permute-done | bytes 262176 | tf_op jit(solution)/shard_map/KC2/P1_2/ppermute | solution.py:39
  44.1 2.6 %butterfly_step.12 = (bf16[8,80,128]{2,1,0:T(8,128)(2,1)S(1)}, bf16[8,80,128]{2,1,0:T(8,128)(2,1)S(1)}, bf16[8,80,128]{2,1,0:T(8,128)(2,1)S(1)}, bf16[8,80,128]{2,1,0:T(8,128)(2,1)S(1)}, bf16[8,128,128]{2,1,0:T(8,128)(2,1)S(1)}) custom-call(s32[3,8]{1,0:T(4,128)S(1)} %copy-done.1, bf16[32,1,640,128]{3,2,1,0:T(8,128)(2,1)} %refs_0_.25, ...), custom_call_target="tpu_custom_call" | custom-call | tf_op jit(solution)/shard_map/KE0_12/butterfly_step/pallas_call | solution.py:217
  47.5 1.5 %collective-permute-start.10 = (bf16[8,80,128]{2,1,0:T(8,128)(2,1)S(1)}, bf16[8,80,128]{2,1,0:T(8,128)(2,1)S(1)}, u32[]{:S(2)}, u32[]{:S(2)}) collective-permute-start(bf16[8,80,128]{2,1,0:T(8,128)(2,1)S(1)} %get-tuple-element.29), channel_id=1, source_target_pairs={{0,16},{8,24},{16,0},{24,8},{1,17},{9,25},{17,1},{25,9},{2,18},{10... | collective-permute-start | bytes 491528 | tf_op jit(solution)/shard_map/KE0_12/P42_0/ppermute | solution.py:39
  49.0 1.4 %collective-permute-start.11 = (bf16[8,80,128]{2,1,0:T(8,128)(2,1)S(1)}, bf16[8,80,128]{2,1,0:T(8,128)(2,1)S(1)}, u32[]{:S(2)}, u32[]{:S(2)}) collective-permute-start(bf16[8,80,128]{2,1,0:T(8,128)(2,1)S(1)} %get-tuple-element.30), channel_id=1, source_target_pairs={{0,24},{8,16},{16,8},{24,0},{1,25},{9,17},{17,9},{25,1},{2,26},{10... | collective-permute-start | bytes 491528 | tf_op jit(solution)/shard_map/KE0_12/P43_0/ppermute | solution.py:39
  50.4 1.3 %butterfly_step.13.refs_7_ = bf16[8,128,128]{2,1,0:T(8,128)(2,1)S(1)} custom-call(s32[3,8]{1,0:T(4,128)S(1)} %copy-done.1, bf16[2,32,1,128,128]{4,3,2,1,0:T(8,128)(2,1)} %refs_3_.13, bf16[2,32,1,128,128]{4,3,2,1,0:T(8,128)(2,1)} %refs_4_.5, bf16[8,128,128]{2,1,0:T(8,128)(2,1)S(1)} %butterfly_step.10.refs_4_.refs_2_, ...), custom_call_target="tpu_custom_call" | custom-call | tf_op jit(solution)/shard_map/K21/butterfly_step/pallas_call | solution.py:217
  51.8 2.3 %all-gather.1 = bf16[16,128,128]{2,1,0:T(8,128)(2,1)} all-gather(bf16[8,128,128]{2,1,0:T(8,128)(2,1)S(1)} %butterfly_step.13.refs_7_), channel_id=3, replica_groups={{0,1},{2,3},{4,5},{6,7},{8,9},{10,11},{12,13},{14,15},{16,17},{18,19},{..., dimensions={0}, use_global_device_ids=true | all-gather | bytes 786432 | tf_op jit(solution)/shard_map/K21/all_gather | solution.py:318
  54.8 2.6 %butterfly_step.14 = (bf16[8,80,128]{2,1,0:T(8,128)(2,1)S(1)}, bf16[8,80,128]{2,1,0:T(8,128)(2,1)S(1)}, bf16[8,80,128]{2,1,0:T(8,128)(2,1)S(1)}, bf16[8,80,128]{2,1,0:T(8,128)(2,1)S(1)}, bf16[8,128,128]{2,1,0:T(8,128)(2,1)S(1)}) custom-call(s32[3,8]{1,0:T(4,128)S(1)} %copy-done.1, bf16[32,1,640,128]{3,2,1,0:T(8,128)(2,1)} %refs_0_.25, ...), custom_call_target="tpu_custom_call" | custom-call | tf_op jit(solution)/shard_map/KE1_13/butterfly_step/pallas_call | solution.py:217
  60.8 1.3 %butterfly_step.15.refs_7_ = bf16[8,128,128]{2,1,0:T(8,128)(2,1)S(1)} custom-call(s32[3,8]{1,0:T(4,128)S(1)} %copy-done.2, bf16[2,32,1,128,128]{4,3,2,1,0:T(8,128)(2,1)} %refs_3_.13, bf16[2,32,1,128,128]{4,3,2,1,0:T(8,128)(2,1)} %refs_4_.5, bf16[8,128,128]{2,1,0:T(8,128)(2,1)S(1)} %get-tuple-element.24.refs_2_, ...), custom_call_target="tpu_custom_call" | custom-call | tf_op jit(solution)/shard_map/K22/butterfly_step/pallas_call | solution.py:217
  62.1 1.6 %collective-permute-start.13 = (bf16[8,80,128]{2,1,0:T(8,128)(2,1)S(1)}, bf16[8,80,128]{2,1,0:T(8,128)(2,1)S(1)}, u32[]{:S(2)}, u32[]{:S(2)}) collective-permute-start(bf16[8,80,128]{2,1,0:T(8,128)(2,1)S(1)} %get-tuple-element.34), channel_id=1, source_target_pairs={{0,16},{8,24},{16,0},{24,8},{1,17},{9,25},{17,1},{25,9},{2,18},{10... | collective-permute-start | bytes 491528 | tf_op jit(solution)/shard_map/KE1_13/P42_1/ppermute | solution.py:39
  64.5 2.3 %all-gather.2 = bf16[16,128,128]{2,1,0:T(8,128)(2,1)} all-gather(bf16[8,128,128]{2,1,0:T(8,128)(2,1)S(1)} %butterfly_step.15.refs_7_), channel_id=4, replica_groups={{0,1},{2,3},{4,5},{6,7},{8,9},{10,11},{12,13},{14,15},{16,17},{18,19},{..., dimensions={0}, use_global_device_ids=true | all-gather | bytes 786432 | tf_op jit(solution)/shard_map/K22/all_gather | solution.py:318
  66.9 2.6 %butterfly_step.16 = (bf16[8,80,128]{2,1,0:T(8,128)(2,1)S(1)}, bf16[8,80,128]{2,1,0:T(8,128)(2,1)S(1)}, bf16[8,80,128]{2,1,0:T(8,128)(2,1)S(1)}, bf16[8,80,128]{2,1,0:T(8,128)(2,1)S(1)}, bf16[8,128,128]{2,1,0:T(8,128)(2,1)S(1)}) custom-call(s32[3,8]{1,0:T(4,128)S(1)} %copy-done.2, bf16[32,1,640,128]{3,2,1,0:T(8,128)(2,1)} %refs_0_.25, ...), custom_call_target="tpu_custom_call" | custom-call | tf_op jit(solution)/shard_map/KE2_23/butterfly_step/pallas_call | solution.py:217
  70.7 1.6 %collective-permute-start.16 = (bf16[8,80,128]{2,1,0:T(8,128)(2,1)S(1)}, bf16[8,80,128]{2,1,0:T(8,128)(2,1)S(1)}, u32[]{:S(2)}, u32[]{:S(2)}) collective-permute-start(bf16[8,80,128]{2,1,0:T(8,128)(2,1)S(1)} %get-tuple-element.38), channel_id=1, source_target_pairs={{0,16},{8,24},{16,0},{24,8},{1,17},{9,25},{17,1},{25,9},{2,18},{10... | collective-permute-start | bytes 491528 | tf_op jit(solution)/shard_map/KE2_23/P42_2/ppermute | solution.py:39
  72.3 2.2 %all-gather.3 = bf16[16,128,128]{2,1,0:T(8,128)(2,1)S(1)} all-gather(bf16[8,128,128]{2,1,0:T(8,128)(2,1)S(1)} %get-tuple-element.31), channel_id=5, replica_groups={{0,1},{2,3},{4,5},{6,7},{8,9},{10,11},{12,13},{14,15},{16,17},{18,19},{..., dimensions={0}, use_global_device_ids=true | all-gather | bytes 786432 | tf_op jit(solution)/shard_map/KE2_23/all_gather | solution.py:318
  75.2 2.0 %butterfly_step.17 = (bf16[8,80,128]{2,1,0:T(8,128)(2,1)S(1)}, bf16[8,80,128]{2,1,0:T(8,128)(2,1)S(1)}, bf16[8,80,128]{2,1,0:T(8,128)(2,1)S(1)}, bf16[8,80,128]{2,1,0:T(8,128)(2,1)S(1)}) custom-call(s32[3,8]{1,0:T(4,128)S(1)} %copy-done.2, bf16[32,1,640,128]{3,2,1,0:T(8,128)(2,1)} %refs_0_.25, bf16[32,1,640,128]{3,2,1,0:T(8,128)(2,1)} %copy-done.4, ...), custom_call_target="tpu_custom_call" | custom-call | tf_op jit(solution)/shard_map/KE3/butterfly_step/pallas_call | solution.py:217
  78.4 1.6 %collective-permute-start.19 = (bf16[8,80,128]{2,1,0:T(8,128)(2,1)S(1)}, bf16[8,80,128]{2,1,0:T(8,128)(2,1)S(1)}, u32[]{:S(2)}, u32[]{:S(2)}) collective-permute-start(bf16[8,80,128]{2,1,0:T(8,128)(2,1)S(1)} %get-tuple-element.41), channel_id=1, source_target_pairs={{0,16},{8,24},{16,0},{24,8},{1,17},{9,25},{17,1},{25,9},{2,18},{10... | collective-permute-start | bytes 491528 | tf_op jit(solution)/shard_map/KE3/P42_3/ppermute | solution.py:39
  82.4 2.5 %collective-permute-done.18 = bf16[8,80,128]{2,1,0:T(8,128)(2,1)S(1)} collective-permute-done((bf16[8,80,128]{2,1,0:T(8,128)(2,1)S(1)}, bf16[8,80,128]{2,1,0:T(8,128)(2,1)S(1)}, u32[]{:S(2)}, u32[]{:S(2)}) %collective-permute-start.18) | collective-permute-done | bytes 163872 | tf_op jit(solution)/shard_map/KE3/P41_3/ppermute | solution.py:39
  84.9 2.2 %collective-permute-done.19 = bf16[8,80,128]{2,1,0:T(8,128)(2,1)S(1)} collective-permute-done((bf16[8,80,128]{2,1,0:T(8,128)(2,1)S(1)}, bf16[8,80,128]{2,1,0:T(8,128)(2,1)S(1)}, u32[]{:S(2)}, u32[]{:S(2)}) %collective-permute-start.19) | collective-permute-done | bytes 163872 | tf_op jit(solution)/shard_map/KE3/P42_3/ppermute | solution.py:39
  87.1 1.5 %collective-permute-done.20 = bf16[8,80,128]{2,1,0:T(8,128)(2,1)S(1)} collective-permute-done((bf16[8,80,128]{2,1,0:T(8,128)(2,1)S(1)}, bf16[8,80,128]{2,1,0:T(8,128)(2,1)S(1)}, u32[]{:S(2)}, u32[]{:S(2)}) %collective-permute-start.20) | collective-permute-done | bytes 163872 | tf_op jit(solution)/shard_map/KE3/P43_3/ppermute | solution.py:39
  (56 shorter events, 16.0 us)
Async XLA Ops:
  0.0 10.0 %collective-permute-start = (bf16[32,1,640,128]{3,2,1,0:T(8,128)(2,1)}, bf16[32,1,640,128]{3,2,1,0:T(8,128)(2,1)S(1)}, u32[]{:S(2)}, u32[]{:S(2)}) collective-permute-start(bf16[32,1,640,128]{3,2,1,0:T(8,128)(2,1)} %refs_0_.25), channel_id=1, source_target_pairs={{0,1},{1,0},{2,3},{3,2},{4,5},{5,4},{6,7},{7,6},{8,9},{9,8},{10,11... | collective-permute-start | bytes 15728648 | tf_op jit(solution)/shard_map/KG0/PG_0/ppermute | solution.py:39
  0.5 0.7 copy-start.1
  1.1 0.7 copy-start.3
  4.1 16.2 %collective-permute-start.1 = (bf16[8,128,128]{2,1,0:T(8,128)(2,1)S(1)}, bf16[8,128,128]{2,1,0:T(8,128)(2,1)S(1)}, u32[]{:S(2)}, u32[]{:S(2)}) collective-permute-start(bf16[8,128,128]{2,1,0:T(8,128)(2,1)S(1)} %compress_slots.4.refs_4_.refs_2_), channel_id=1, source_target_pairs={{0,4},{1,5},{2,6},{3,7},{4,0},{5,1},{6,2},{7,3},{8,12},{9,13},{10,... | collective-permute-start | bytes 786440 | tf_op jit(solution)/shard_map/KC0/P1_0/ppermute | solution.py:39
  10.0 2.3 %copy-start.4 = (bf16[32,1,640,128]{3,2,1,0:T(8,128)(2,1)}, bf16[32,1,640,128]{3,2,1,0:T(8,128)(2,1)S(1)}, u32[]{:S(2)}) copy-start(bf16[32,1,640,128]{3,2,1,0:T(8,128)(2,1)S(1)} %collective-permute-done.refs_5_.refs_1_) | copy-start | bytes 15728644
  16.9 16.0 %collective-permute-start.3 = (bf16[8,128,128]{2,1,0:T(8,128)(2,1)S(1)}, bf16[8,128,128]{2,1,0:T(8,128)(2,1)S(1)}, u32[]{:S(2)}, u32[]{:S(2)}) collective-permute-start(bf16[8,128,128]{2,1,0:T(8,128)(2,1)S(1)} %compress_slots.7.refs_4_.refs_2_), channel_id=1, source_target_pairs={{0,4},{1,5},{2,6},{3,7},{4,0},{5,1},{6,2},{7,3},{8,12},{9,13},{10,... | collective-permute-start | bytes 786440 | tf_op jit(solution)/shard_map/KC1/P1_1/ppermute | solution.py:39
  21.7 16.9 %collective-permute-start.2 = (bf16[8,128,128]{2,1,0:T(8,128)(2,1)S(1)}, bf16[8,128,128]{2,1,0:T(8,128)(2,1)S(1)}, u32[]{:S(2)}, u32[]{:S(2)}) collective-permute-start(bf16[8,128,128]{2,1,0:T(8,128)(2,1)S(1)} %butterfly_step.9.refs_4_.refs_2_), channel_id=1, source_target_pairs={{0,2},{1,3},{2,0},{3,1},{4,6},{5,7},{6,4},{7,5},{8,10},{9,11},{10,... | collective-permute-start | bytes 786440 | tf_op jit(solution)/shard_map/K10/P2_0/ppermute | solution.py:39
  22.9 21.2 %collective-permute-start.4 = (bf16[8,128,128]{2,1,0:T(8,128)(2,1)S(1)}, bf16[8,128,128]{2,1,0:T(8,128)(2,1)S(1)}, u32[]{:S(2)}, u32[]{:S(2)}) collective-permute-start(bf16[8,128,128]{2,1,0:T(8,128)(2,1)S(1)} %compress_slots.5.refs_4_.refs_5_), channel_id=1, source_target_pairs={{0,4},{1,5},{2,6},{3,7},{4,0},{5,1},{6,2},{7,3},{8,12},{9,13},{10,... | collective-permute-start | bytes 786440 | tf_op jit(solution)/shard_map/KC2/P1_2/ppermute | solution.py:39
  34.3 16.1 %collective-permute-start.6 = (bf16[8,128,128]{2,1,0:T(8,128)(2,1)S(1)}, bf16[8,128,128]{2,1,0:T(8,128)(2,1)S(1)}, u32[]{:S(2)}, u32[]{:S(2)}) collective-permute-start(bf16[8,128,128]{2,1,0:T(8,128)(2,1)S(1)} %butterfly_step.10.refs_4_.refs_2_), channel_id=1, source_target_pairs={{0,2},{1,3},{2,0},{3,1},{4,6},{5,7},{6,4},{7,5},{8,10},{9,11},{10,... | collective-permute-start | bytes 786440 | tf_op jit(solution)/shard_map/K11/P2_1/ppermute | solution.py:39
  34.9 19.8 %collective-permute-start.7 = (bf16[8,128,128]{2,1,0:T(8,128)(2,1)S(1)}, bf16[8,128,128]{2,1,0:T(8,128)(2,1)S(1)}, u32[]{:S(2)}, u32[]{:S(2)}) collective-permute-start(bf16[8,128,128]{2,1,0:T(8,128)(2,1)S(1)} %compress_slots.6.refs_4_.refs_5_), channel_id=1, source_target_pairs={{0,4},{1,5},{2,6},{3,7},{4,0},{5,1},{6,2},{7,3},{8,12},{9,13},{10,... | collective-permute-start | bytes 786440 | tf_op jit(solution)/shard_map/KC3/P1_3/ppermute | solution.py:39
  46.7 12.9 %collective-permute-start.5 = (bf16[8,128,128]{2,1,0:T(8,128)(2,1)S(1)}, bf16[8,128,128]{2,1,0:T(8,128)(2,1)S(1)}, u32[]{:S(2)}, u32[]{:S(2)}) collective-permute-start(bf16[8,128,128]{2,1,0:T(8,128)(2,1)S(1)} %get-tuple-element.24.refs_2_), channel_id=1, source_target_pairs={{0,2},{1,3},{2,0},{3,1},{4,6},{5,7},{6,4},{7,5},{8,10},{9,11},{10,... | collective-permute-start | bytes 786440 | tf_op jit(solution)/shard_map/KE0_12/P2_2/ppermute | solution.py:39
  47.5 14.7 %collective-permute-start.10 = (bf16[8,80,128]{2,1,0:T(8,128)(2,1)S(1)}, bf16[8,80,128]{2,1,0:T(8,128)(2,1)S(1)}, u32[]{:S(2)}, u32[]{:S(2)}) collective-permute-start(bf16[8,80,128]{2,1,0:T(8,128)(2,1)S(1)} %get-tuple-element.29), channel_id=1, source_target_pairs={{0,16},{8,24},{16,0},{24,8},{1,17},{9,25},{17,1},{25,9},{2,18},{10... | collective-permute-start | bytes 491528 | tf_op jit(solution)/shard_map/KE0_12/P42_0/ppermute | solution.py:39
  49.0 14.7 %collective-permute-start.11 = (bf16[8,80,128]{2,1,0:T(8,128)(2,1)S(1)}, bf16[8,80,128]{2,1,0:T(8,128)(2,1)S(1)}, u32[]{:S(2)}, u32[]{:S(2)}) collective-permute-start(bf16[8,80,128]{2,1,0:T(8,128)(2,1)S(1)} %get-tuple-element.30), channel_id=1, source_target_pairs={{0,24},{8,16},{16,8},{24,0},{1,25},{9,17},{17,9},{25,1},{2,26},{10... | collective-permute-start | bytes 491528 | tf_op jit(solution)/shard_map/KE0_12/P43_0/ppermute | solution.py:39
  54.8 6.0 %copy-start.2 = (s32[3,8]{1,0:T(4,128)S(1)}, s32[3,8]{1,0:T(4,128)}, u32[]{:S(2)}) copy-start(s32[3,8]{1,0:T(4,128)} %ranks.17) | copy-start | bytes 292
  57.4 9.5 %collective-permute-start.8 = (bf16[8,128,128]{2,1,0:T(8,128)(2,1)S(1)}, bf16[8,128,128]{2,1,0:T(8,128)(2,1)S(1)}, u32[]{:S(2)}, u32[]{:S(2)}) collective-permute-start(bf16[8,128,128]{2,1,0:T(8,128)(2,1)S(1)} %get-tuple-element.27.refs_5_), channel_id=1, source_target_pairs={{0,2},{1,3},{2,0},{3,1},{4,6},{5,7},{6,4},{7,5},{8,10},{9,11},{10,... | collective-permute-start | bytes 786440 | tf_op jit(solution)/shard_map/KE1_13/P2_3/ppermute | solution.py:39
  58.7 8.1 %collective-permute-start.9 = (bf16[8,80,128]{2,1,0:T(8,128)(2,1)S(1)}, bf16[8,80,128]{2,1,0:T(8,128)(2,1)S(1)}, u32[]{:S(2)}, u32[]{:S(2)}) collective-permute-start(bf16[8,80,128]{2,1,0:T(8,128)(2,1)S(1)} %get-tuple-element.28), channel_id=1, source_target_pairs={{0,8},{8,0},{16,24},{24,16},{1,9},{9,1},{17,25},{25,17},{2,10},{10... | collective-permute-start | bytes 491528 | tf_op jit(solution)/shard_map/KE0_12/P41_0/ppermute | solution.py:39
  59.6 14.8 %collective-permute-start.12 = (bf16[8,80,128]{2,1,0:T(8,128)(2,1)S(1)}, bf16[8,80,128]{2,1,0:T(8,128)(2,1)S(1)}, u32[]{:S(2)}, u32[]{:S(2)}) collective-permute-start(bf16[8,80,128]{2,1,0:T(8,128)(2,1)S(1)} %get-tuple-element.33), channel_id=1, source_target_pairs={{0,8},{8,0},{16,24},{24,16},{1,9},{9,1},{17,25},{25,17},{2,10},{10... | collective-permute-start | bytes 491528 | tf_op jit(solution)/shard_map/KE1_13/P41_1/ppermute | solution.py:39
  62.1 4.7 %copy-start = (bf16[8,128,128]{2,1,0:T(8,128)(2,1)}, bf16[8,128,128]{2,1,0:T(8,128)(2,1)S(1)}, u32[]{:S(2)}) copy-start(bf16[8,128,128]{2,1,0:T(8,128)(2,1)S(1)} %butterfly_step.15.refs_7_) | copy-start | bytes 786436
  62.1 13.1 %collective-permute-start.13 = (bf16[8,80,128]{2,1,0:T(8,128)(2,1)S(1)}, bf16[8,80,128]{2,1,0:T(8,128)(2,1)S(1)}, u32[]{:S(2)}, u32[]{:S(2)}) collective-permute-start(bf16[8,80,128]{2,1,0:T(8,128)(2,1)S(1)} %get-tuple-element.34), channel_id=1, source_target_pairs={{0,16},{8,24},{16,0},{24,8},{1,17},{9,25},{17,1},{25,9},{2,18},{10... | collective-permute-start | bytes 491528 | tf_op jit(solution)/shard_map/KE1_13/P42_1/ppermute | solution.py:39
  63.7 11.5 %collective-permute-start.14 = (bf16[8,80,128]{2,1,0:T(8,128)(2,1)S(1)}, bf16[8,80,128]{2,1,0:T(8,128)(2,1)S(1)}, u32[]{:S(2)}, u32[]{:S(2)}) collective-permute-start(bf16[8,80,128]{2,1,0:T(8,128)(2,1)S(1)} %get-tuple-element.35), channel_id=1, source_target_pairs={{0,24},{8,16},{16,8},{24,0},{1,25},{9,17},{17,9},{25,1},{2,26},{10... | collective-permute-start | bytes 491528 | tf_op jit(solution)/shard_map/KE1_13/P43_1/ppermute | solution.py:39
  69.5 11.2 %collective-permute-start.15 = (bf16[8,80,128]{2,1,0:T(8,128)(2,1)S(1)}, bf16[8,80,128]{2,1,0:T(8,128)(2,1)S(1)}, u32[]{:S(2)}, u32[]{:S(2)}) collective-permute-start(bf16[8,80,128]{2,1,0:T(8,128)(2,1)S(1)} %get-tuple-element.37), channel_id=1, source_target_pairs={{0,8},{8,0},{16,24},{24,16},{1,9},{9,1},{17,25},{25,17},{2,10},{10... | collective-permute-start | bytes 491528 | tf_op jit(solution)/shard_map/KE2_23/P41_2/ppermute | solution.py:39
  70.7 10.8 %collective-permute-start.16 = (bf16[8,80,128]{2,1,0:T(8,128)(2,1)S(1)}, bf16[8,80,128]{2,1,0:T(8,128)(2,1)S(1)}, u32[]{:S(2)}, u32[]{:S(2)}) collective-permute-start(bf16[8,80,128]{2,1,0:T(8,128)(2,1)S(1)} %get-tuple-element.38), channel_id=1, source_target_pairs={{0,16},{8,24},{16,0},{24,8},{1,17},{9,25},{17,1},{25,9},{2,18},{10... | collective-permute-start | bytes 491528 | tf_op jit(solution)/shard_map/KE2_23/P42_2/ppermute | solution.py:39
  74.5 7.9 %collective-permute-start.17 = (bf16[8,80,128]{2,1,0:T(8,128)(2,1)S(1)}, bf16[8,80,128]{2,1,0:T(8,128)(2,1)S(1)}, u32[]{:S(2)}, u32[]{:S(2)}) collective-permute-start(bf16[8,80,128]{2,1,0:T(8,128)(2,1)S(1)} %get-tuple-element.39), channel_id=1, source_target_pairs={{0,24},{8,16},{16,8},{24,0},{1,25},{9,17},{17,9},{25,1},{2,26},{10... | collective-permute-start | bytes 491528 | tf_op jit(solution)/shard_map/KE2_23/P43_2/ppermute | solution.py:39
  77.2 7.7 %collective-permute-start.18 = (bf16[8,80,128]{2,1,0:T(8,128)(2,1)S(1)}, bf16[8,80,128]{2,1,0:T(8,128)(2,1)S(1)}, u32[]{:S(2)}, u32[]{:S(2)}) collective-permute-start(bf16[8,80,128]{2,1,0:T(8,128)(2,1)S(1)} %get-tuple-element.40), channel_id=1, source_target_pairs={{0,8},{8,0},{16,24},{24,16},{1,9},{9,1},{17,25},{25,17},{2,10},{10... | collective-permute-start | bytes 491528 | tf_op jit(solution)/shard_map/KE3/P41_3/ppermute | solution.py:39
  78.4 8.7 %collective-permute-start.19 = (bf16[8,80,128]{2,1,0:T(8,128)(2,1)S(1)}, bf16[8,80,128]{2,1,0:T(8,128)(2,1)S(1)}, u32[]{:S(2)}, u32[]{:S(2)}) collective-permute-start(bf16[8,80,128]{2,1,0:T(8,128)(2,1)S(1)} %get-tuple-element.41), channel_id=1, source_target_pairs={{0,16},{8,24},{16,0},{24,8},{1,17},{9,25},{17,1},{25,9},{2,18},{10... | collective-permute-start | bytes 491528 | tf_op jit(solution)/shard_map/KE3/P42_3/ppermute | solution.py:39
  80.7 7.9 %collective-permute-start.20 = (bf16[8,80,128]{2,1,0:T(8,128)(2,1)S(1)}, bf16[8,80,128]{2,1,0:T(8,128)(2,1)S(1)}, u32[]{:S(2)}, u32[]{:S(2)}) collective-permute-start(bf16[8,80,128]{2,1,0:T(8,128)(2,1)S(1)} %get-tuple-element.42), channel_id=1, source_target_pairs={{0,24},{8,16},{16,8},{24,0},{1,25},{9,17},{17,9},{25,1},{2,26},{10... | collective-permute-start | bytes 491528 | tf_op jit(solution)/shard_map/KE3/P43_3/ppermute | solution.py:39
  87.1 1.5 %copy-start.5 = (bf16[128,1,1,80,128]{4,3,2,1,0:T(8,128)(2,1)}, bf16[128,1,1,80,128]{4,3,2,1,0:T(8,128)(2,1)S(1)}, u32[]{:S(2)}) copy-start(bf16[128,1,1,80,128]{4,3,2,1,0:T(8,128)(2,1)S(1)} %bitcast_dynamic-update-slice_fusion.1) | copy-start | bytes 7864324

commit v4 on v3

--- a/solution.py
+++ b/solution.py
@@ -19,7 +19,8 @@
     "10",
     "11",
     "20",
-    "E0+12",
+    "E0",
+    "12",
     "21",
     "E1+13",
     "22",
@@ -60,11 +61,10 @@
     return max(b for b in range(1, most + 1) if count % b == 0)
 
 
-def compress_kernel(first, b, waves, ranks, x_hbm, a_hbm, *refs):
-    outs, (x_ref, a_ref, sems) = refs[:-3], refs[-3:]
+def compress_kernel(first, b, waves_hbm, x_hbm, a_hbm, *refs):
+    outs, (x_ref, a_ref, waves, sems, small) = refs[:-5], refs[-5:]
     block = lax.axis_index("deg")
     nb, cols = x_ref.shape[1:]
-    width = a_ref.shape[2]
 
     def copies(g):
         here, there = pl.ds(g * b, b), pl.ds(first + g * b, b)
@@ -73,11 +73,13 @@
             pltpu.make_async_copy(a_hbm.at[there], a_ref.at[here], sems.at[1, g]),
         )
 
+    scalars = pltpu.make_async_copy(waves_hbm, waves, small.at[0])
+    scalars.start()
     for g in range(x_ref.shape[0] // b):
         for copy in copies(g):
             copy.start()
+    scalars.wait()
     degree = lax.broadcasted_iota(jnp.int32, (nb, cols), 0) + block * nb
-    keep = lax.broadcasted_iota(jnp.int32, (width, cols), 0) < ranks[0, block]
     start = 0
     for out in outs:
 
@@ -89,34 +91,36 @@
                 wave = waves[first + start + slot]
                 live = jnp.where(degree >= wave, x_ref[start + slot], 0).astype(x_ref.dtype)
                 total = dot(a_ref[start + slot], live, 0)
-                out[slot] = jnp.where(keep, total, 0.0).astype(out.dtype)
+                out[slot] = total.astype(out.dtype)
             return carry
 
         lax.fori_loop(0, out.shape[0] // b, some, 0)
         start += out.shape[0]
 
 
-def compress_slots(first, counts, waves, ranks, spectral, compress, late):
+def compress_slots(first, counts, waves, spectral, compress, late):
     b = min(group(count) for count in (first, *counts) if count)
     nb, cols = spectral.shape[1:]
     width = compress.shape[2]
     count = sum(counts)
     shapes = [(n, width, cols) for n in counts]
     return pl.pallas_call(
-        ordered(functools.partial(compress_kernel, first, b), 4, len(late)),
+        ordered(functools.partial(compress_kernel, first, b), 3, len(late)),
         out_shape=[jax.ShapeDtypeStruct(s, jnp.bfloat16) for s in shapes],
         grid=(1,),
-        in_specs=[SMEM, SMEM, HBM, HBM] + [ANY] * len(late),
+        in_specs=[HBM] * 3 + [ANY] * len(late),
         out_specs=[pl.BlockSpec(s, lambda i: (0, 0, 0)) for s in shapes],
         scratch_shapes=[
             pltpu.VMEM((count, nb, cols), spectral.dtype),
             pltpu.VMEM((count, nb, width), compress.dtype),
+            pltpu.SMEM(waves.shape, waves.dtype),
             pltpu.SemaphoreType.DMA((2, count // b)),
+            pltpu.SemaphoreType.DMA((1,)),
         ],
         compiler_params=pltpu.CompilerParams(vmem_limit_bytes=VMEM_LIMIT),
         cost_estimate=pl.CostEstimate(flops=0, bytes_accessed=0, transcendentals=0),
         name="compress_slots",
-    )(waves, ranks, spectral, compress, *late)
+    )(waves, spectral, compress, *late)
 
 
 def section_task(section, first, ranks, own, peer, vector, partner):
@@ -127,9 +131,17 @@
 
     def kernel(i, ranks, own_ref, peer_ref, v_ref, u_ref, *outs):
         block = lax.axis_index("deg")
-        keep = lax.broadcasted_iota(jnp.int32, (width, cols), 0) < ranks[section, block]
+        row = lax.broadcasted_iota(jnp.int32, (width, cols), 0)
+        keep = row < ranks[section, block]
+        if section == 1:
+            partner_block = block ^ (lax.axis_size("deg") >> 1)
+            keep_v, keep_u = row < ranks[0, block], row < ranks[0, partner_block]
         for j in range(b):
-            total = dot_pair(own_ref[j], peer_ref[j], v_ref[j], u_ref[j])
+            v, u = v_ref[j], u_ref[j]
+            if section == 1:
+                v = jnp.where(keep_v, v, 0).astype(v.dtype)
+                u = jnp.where(keep_u, u, 0).astype(u.dtype)
+            total = dot_pair(own_ref[j], peer_ref[j], v, u)
             total = jnp.where(keep, total, 0.0).astype(vector.dtype)
             outs[0][j] = total
 
@@ -157,12 +169,13 @@
         mine = lax.axis_index("deg") % 2
         rows_ref = outs[-1]
         for j in range(b):
-            rows_ref[...] = dot_pair(
+            total = dot_pair(
                 kept_ref[j], got_ref[j], both_ref[mine, j], both_ref[1 - mine, j]
             )
+            rows_ref[...] = total.astype(rows_ref.dtype)
             for offset, out in enumerate(outs[:-1]):
                 at = pl.multiple_of((zone ^ offset) * piece, piece)
-                out[j] = rows_ref[pl.ds(at, piece), :].astype(out.dtype)
+                out[j] = rows_ref[pl.ds(at, piece), :]
 
     def weights(i):
         return (first // b + i, 0, lax.axis_index("deg") % 2, 0)
@@ -223,7 +236,7 @@
         input_output_aliases={
             1 + len(ins) + len(late) + n: len(outs) + n for n in range(len(held))
         },
-        scratch_shapes=[pltpu.VMEM((rows, cols), jnp.float32)],
+        scratch_shapes=[pltpu.VMEM((rows, cols), jnp.bfloat16)],
         compiler_params=pltpu.CompilerParams(vmem_limit_bytes=VMEM_LIMIT),
         cost_estimate=pl.CostEstimate(flops=flops, bytes_accessed=0, transcendentals=0),
         name="butterfly_step",
@@ -328,7 +341,7 @@
             if names[0] == "C":
                 ks = [int(k) for k in names[1:]]
                 outs = compress_slots(
-                    firsts[ks[0]], [CHUNKS[k] for k in ks], wavenumbers, block_ranks,
+                    firsts[ks[0]], [CHUNKS[k] for k in ks], wavenumbers,
                     spectral, compress, gate(waits),
                 )
                 late.append(outs[-1])

time: 90 us -> 88.3 us (0.981)
  Pallas kernels: 25.6 us -> 24 us
  starting transfers between devices: 32.2 us -> 33.4 us
    pallas_call x4, Pallas kernels: 9.13 us -> 6.89 us  [compress_slots(): pl.pallas_call(ordered(functools.partial(compress_kernel, first, b), 3, l...]
    ppermute x21, starting transfers between devices: 32.2 us -> 33.4 us  [from_partner(): return lax.ppermute(array, axis, pairs)]
    unnamed x12 -> x10, local copies, waits for them, and re-layouts: 3.67 us -> 3 us
    pallas_call x9 -> x10, Pallas kernels: 16.5 us -> 17.1 us  [fused(): pl.pallas_call(kernel, out_shape=outs + [jax.ShapeDtypeStruct(h.shape, h....]
  transfers between devices with their start and end apart: 21 -> 21, of which waited for: 8 -> 7; matrix products, arithmetic and copies ran while one was open for 1% -> 1% of each run, Pallas kernels for 29% -> 27%
where the time goes in v4:
time: 88.3 us; the launch traced here: 87.5 us
  starting transfers between devices  33.4 us (38%)
  Pallas kernels  24 us (27%)
  waiting for transfers between devices  16.4 us (19%)
  blocking collectives  8.97 us (10%)
  local copies, waits for them, and re-layouts  4.43 us (5%)
    ppermute x21, starting transfers between devices, from_partner(): return lax.ppermute(array, axis, pairs)  33.4 us
    pallas_call x10, Pallas kernels, fused(): pl.pallas_call(kernel, out_shape=outs + [jax.ShapeDtypeStruct(h.shape, h....  17.1 us
    ppermute x21, waiting for transfers between devices, from_partner(): return lax.ppermute(array, axis, pairs)  16.4 us
    all_gather x4, blocking collectives, stepped(): state[k] = lax.all_gather(made[0], 'deg', axis_index_groups=groups)  8.97 us
    pallas_call x4, Pallas kernels, compress_slots(): pl.pallas_call(ordered(functools.partial(compress_kernel, first, b), 3, l...  6.89 us
    unnamed x10, local copies, waits for them, and re-layouts  3 us
  transfers between devices with their start and end apart: 21, of which 7 were waited for; matrix products, arithmetic and copies ran while one was open for 1% of the time, Pallas kernels for 27%

profile of v4, /device:TPU:0, one launch (start us, length us, event | category | flops | bytes accessed | tf_op | source)
XLA Modules:
  0.0 87.5 jit_solution(17838287154957512799)
XLA Ops:
  1.1 1.7 %compress_slots.4.refs_3_.refs_2_ = bf16[8,128,128]{2,1,0:T(8,128)(2,1)S(1)} custom-call(s32[32]{0:T(128)S(1)} %copy-done.2, bf16[32,320,128]{2,1,0:T(8,128)(2,1)} %refs_1_.13, bf16[32,320,128]{2,1,0:T(8,128)(2,1)} %refs_2_.7), custom_call_target="tpu_custom_call" | custom-call | tf_op jit(solution)/shard_map/KC0/compress_slots/pallas_call | solution.py:107
  2.8 3.7 %collective-permute-start.2 = (bf16[8,128,128]{2,1,0:T(8,128)(2,1)S(1)}, bf16[8,128,128]{2,1,0:T(8,128)(2,1)S(1)}, u32[]{:S(2)}, u32[]{:S(2)}) collective-permute-start(bf16[8,128,128]{2,1,0:T(8,128)(2,1)S(1)} %compress_slots.4.refs_3_.refs_2_), channel_id=1, source_target_pairs={{0,4},{1,5},{2,6},{3,7},{4,0},{5,1},{6,2},{7,3},{8,12},{9,13},{10,... | collective-permute-start | bytes 786440 | tf_op jit(solution)/shard_map/KC0/P1_0/ppermute | solution.py:40
  6.5 1.7 %compress_slots.5.refs_3_.refs_2_ = bf16[8,128,128]{2,1,0:T(8,128)(2,1)S(1)} custom-call(s32[32]{0:T(128)S(1)} %copy-done.2, bf16[32,320,128]{2,1,0:T(8,128)(2,1)} %refs_1_.13, bf16[32,320,128]{2,1,0:T(8,128)(2,1)} %refs_2_.7, bf16[8,128,128]{2,1,0:T(8,128)(2,1)S(1)} %compress_slots.4.refs_3_.refs_2_), custom_call_target="tpu_custom_call" | custom-call | tf_op jit(solution)/shard_map/KC2/compress_slots/pallas_call | solution.py:107
  9.0 2.3 %copy-done.3 = bf16[32,1,640,128]{3,2,1,0:T(8,128)(2,1)} copy-done((bf16[32,1,640,128]{3,2,1,0:T(8,128)(2,1)}, bf16[32,1,640,128]{3,2,1,0:T(8,128)(2,1)S(1)}, u32[]{:S(2)}) %copy-start.3) | copy-done | bytes 5242904
  11.3 1.7 %compress_slots.6.refs_3_.refs_5_ = bf16[8,128,128]{2,1,0:T(8,128)(2,1)S(1)} custom-call(s32[32]{0:T(128)S(1)} %copy-done.2, bf16[32,320,128]{2,1,0:T(8,128)(2,1)} %refs_1_.13, bf16[32,320,128]{2,1,0:T(8,128)(2,1)} %refs_2_.7, bf16[8,128,128]{2,1,0:T(8,128)(2,1)S(1)} %compress_slots.5.refs_3_.refs_2_, bf16[32,1,640,128]{3,2,1,0:T(8,128)(2,1)} %copy-done.3), custom_call_target="tpu_custom_call" | custom-call | tf_op jit(solution)/shard_map/KC3/compress_slots/pallas_call | solution.py:107
  13.0 1.7 %compress_slots.7.refs_4_.refs_2_ = bf16[8,128,128]{2,1,0:T(8,128)(2,1)S(1)} custom-call(s32[32]{0:T(128)S(1)} %copy-done.2, bf16[32,320,128]{2,1,0:T(8,128)(2,1)} %refs_1_.13, bf16[32,320,128]{2,1,0:T(8,128)(2,1)} %refs_2_.7, bf16[8,128,128]{2,1,0:T(8,128)(2,1)S(1)} %compress_slots.6.refs_3_.refs_5_), custom_call_target="tpu_custom_call" | custom-call | tf_op jit(solution)/shard_map/KC1/compress_slots/pallas_call | solution.py:107
  14.8 4.0 %collective-permute-start.4 = (bf16[8,128,128]{2,1,0:T(8,128)(2,1)S(1)}, bf16[8,128,128]{2,1,0:T(8,128)(2,1)S(1)}, u32[]{:S(2)}, u32[]{:S(2)}) collective-permute-start(bf16[8,128,128]{2,1,0:T(8,128)(2,1)S(1)} %compress_slots.7.refs_4_.refs_2_), channel_id=1, source_target_pairs={{0,4},{1,5},{2,6},{3,7},{4,0},{5,1},{6,2},{7,3},{8,12},{9,13},{10,... | collective-permute-start | bytes 786440 | tf_op jit(solution)/shard_map/KC1/P1_1/ppermute | solution.py:40
  19.1 1.3 %butterfly_step.10.refs_4_.refs_2_ = bf16[8,128,128]{2,1,0:T(8,128)(2,1)S(1)} custom-call(s32[3,8]{1,0:T(4,128)S(1)} %copy-done.1, bf16[2,32,1,128,128]{4,3,2,1,0:T(8,128)(2,1)} %refs_3_.3, bf16[2,32,1,128,128]{4,3,2,1,0:T(8,128)(2,1)} %refs_4_.3, bf16[8,128,128]{2,1,0:T(8,128)(2,1)S(1)} %compress_slots.4.refs_3_.refs_2_, ...), custom_call_target="tpu_custom_call" | custom-call | tf_op jit(solution)/shard_map/K10/butterfly_step/pallas_call | solution.py:230
  21.8 2.8 %collective-permute-start.1 = (bf16[8,128,128]{2,1,0:T(8,128)(2,1)S(1)}, bf16[8,128,128]{2,1,0:T(8,128)(2,1)S(1)}, u32[]{:S(2)}, u32[]{:S(2)}) collective-permute-start(bf16[8,128,128]{2,1,0:T(8,128)(2,1)S(1)} %compress_slots.5.refs_3_.refs_2_), channel_id=1, source_target_pairs={{0,4},{1,5},{2,6},{3,7},{4,0},{5,1},{6,2},{7,3},{8,12},{9,13},{10,... | collective-permute-start | bytes 786440 | tf_op jit(solution)/shard_map/KC2/P1_2/ppermute | solution.py:40
  24.6 7.1 %collective-permute-done.4.refs_3_ = bf16[8,128,128]{2,1,0:T(8,128)(2,1)S(1)} collective-permute-done((bf16[8,128,128]{2,1,0:T(8,128)(2,1)S(1)}, bf16[8,128,128]{2,1,0:T(8,128)(2,1)S(1)}, u32[]{:S(2)}, u32[]{:S(2)}) %collective-permute-start.4) | collective-permute-done | bytes 262176 | tf_op jit(solution)/shard_map/KC1/P1_1/ppermute | solution.py:40
  33.9 3.6 %collective-permute-start.7 = (bf16[8,128,128]{2,1,0:T(8,128)(2,1)S(1)}, bf16[8,128,128]{2,1,0:T(8,128)(2,1)S(1)}, u32[]{:S(2)}, u32[]{:S(2)}) collective-permute-start(bf16[8,128,128]{2,1,0:T(8,128)(2,1)S(1)} %compress_slots.6.refs_3_.refs_5_), channel_id=1, source_target_pairs={{0,4},{1,5},{2,6},{3,7},{4,0},{5,1},{6,2},{7,3},{8,12},{9,13},{10,... | collective-permute-start | bytes 786440 | tf_op jit(solution)/shard_map/KC3/P1_3/ppermute | solution.py:40
  38.8 2.2 %all-gather = bf16[16,128,128]{2,1,0:T(8,128)(2,1)S(1)} all-gather(bf16[8,128,128]{2,1,0:T(8,128)(2,1)S(1)} %butterfly_step.12.refs_3_), channel_id=2, replica_groups={{0,1},{2,3},{4,5},{6,7},{8,9},{10,11},{12,13},{14,15},{16,17},{18,19},{..., dimensions={0}, use_global_device_ids=true | all-gather | bytes 786432 | tf_op jit(solution)/shard_map/K20/all_gather | solution.py:331
  41.0 1.9 %butterfly_step.13 = (bf16[8,80,128]{2,1,0:T(8,128)(2,1)S(1)}, bf16[8,80,128]{2,1,0:T(8,128)(2,1)S(1)}, bf16[8,80,128]{2,1,0:T(8,128)(2,1)S(1)}, bf16[8,80,128]{2,1,0:T(8,128)(2,1)S(1)}) custom-call(s32[3,8]{1,0:T(4,128)S(1)} %copy-done.1, bf16[32,1,640,128]{3,2,1,0:T(8,128)(2,1)} %refs_0_.27, bf16[32,1,640,128]{3,2,1,0:T(8,128)(2,1)} %copy-done.3, ...), custom_call_target="tpu_custom_call" | custom-call | tf_op jit(solution)/shard_map/KE0/butterfly_step/pallas_call | solution.py:230
  42.9 1.4 %butterfly_step.14.refs_4_.refs_2_ = bf16[8,128,128]{2,1,0:T(8,128)(2,1)S(1)} custom-call(s32[3,8]{1,0:T(4,128)S(1)} %copy-done.1, bf16[2,32,1,128,128]{4,3,2,1,0:T(8,128)(2,1)} %refs_3_.3, bf16[2,32,1,128,128]{4,3,2,1,0:T(8,128)(2,1)} %refs_4_.3, bf16[8,128,128]{2,1,0:T(8,128)(2,1)S(1)} %compress_slots.5.refs_3_.refs_2_, ...), custom_call_target="tpu_custom_call" | custom-call | tf_op jit(solution)/shard_map/K12/butterfly_step/pallas_call | solution.py:230
  45.1 1.5 %collective-permute-start.10 = (bf16[8,80,128]{2,1,0:T(8,128)(2,1)S(1)}, bf16[8,80,128]{2,1,0:T(8,128)(2,1)S(1)}, u32[]{:S(2)}, u32[]{:S(2)}) collective-permute-start(bf16[8,80,128]{2,1,0:T(8,128)(2,1)S(1)} %get-tuple-element.27), channel_id=1, source_target_pairs={{0,16},{8,24},{16,0},{24,8},{1,17},{9,25},{17,1},{25,9},{2,18},{10... | collective-permute-start | bytes 491528 | tf_op jit(solution)/shard_map/KE0/P42_0/ppermute | solution.py:40
  46.7 1.4 %collective-permute-start.11 = (bf16[8,80,128]{2,1,0:T(8,128)(2,1)S(1)}, bf16[8,80,128]{2,1,0:T(8,128)(2,1)S(1)}, u32[]{:S(2)}, u32[]{:S(2)}) collective-permute-start(bf16[8,80,128]{2,1,0:T(8,128)(2,1)S(1)} %get-tuple-element.28), channel_id=1, source_target_pairs={{0,24},{8,16},{16,8},{24,0},{1,25},{9,17},{17,9},{25,1},{2,26},{10... | collective-permute-start | bytes 491528 | tf_op jit(solution)/shard_map/KE0/P43_0/ppermute | solution.py:40
  49.4 2.3 %all-gather.1 = bf16[16,128,128]{2,1,0:T(8,128)(2,1)} all-gather(bf16[8,128,128]{2,1,0:T(8,128)(2,1)S(1)} %butterfly_step.15.refs_7_), channel_id=3, replica_groups={{0,1},{2,3},{4,5},{6,7},{8,9},{10,11},{12,13},{14,15},{16,17},{18,19},{..., dimensions={0}, use_global_device_ids=true | all-gather | bytes 786432 | tf_op jit(solution)/shard_map/K21/all_gather | solution.py:331
  51.7 1.9 %collective-permute-done.7.refs_6_ = bf16[8,128,128]{2,1,0:T(8,128)(2,1)S(1)} collective-permute-done((bf16[8,128,128]{2,1,0:T(8,128)(2,1)S(1)}, bf16[8,128,128]{2,1,0:T(8,128)(2,1)S(1)}, u32[]{:S(2)}, u32[]{:S(2)}) %collective-permute-start.7) | collective-permute-done | bytes 262176 | tf_op jit(solution)/shard_map/KC3/P1_3/ppermute | solution.py:40
  53.7 2.6 %butterfly_step.16 = (bf16[8,80,128]{2,1,0:T(8,128)(2,1)S(1)}, bf16[8,80,128]{2,1,0:T(8,128)(2,1)S(1)}, bf16[8,80,128]{2,1,0:T(8,128)(2,1)S(1)}, bf16[8,80,128]{2,1,0:T(8,128)(2,1)S(1)}, bf16[8,128,128]{2,1,0:T(8,128)(2,1)S(1)}) custom-call(s32[3,8]{1,0:T(4,128)S(1)} %copy-done.1, bf16[32,1,640,128]{3,2,1,0:T(8,128)(2,1)} %refs_0_.27, ...), custom_call_target="tpu_custom_call" | custom-call | tf_op jit(solution)/shard_map/KE1_13/butterfly_step/pallas_call | solution.py:230
  57.0 1.5 %collective-permute-start.9 = (bf16[8,80,128]{2,1,0:T(8,128)(2,1)S(1)}, bf16[8,80,128]{2,1,0:T(8,128)(2,1)S(1)}, u32[]{:S(2)}, u32[]{:S(2)}) collective-permute-start(bf16[8,80,128]{2,1,0:T(8,128)(2,1)S(1)} %get-tuple-element.26), channel_id=1, source_target_pairs={{0,8},{8,0},{16,24},{24,16},{1,9},{9,1},{17,25},{25,17},{2,10},{10... | collective-permute-start | bytes 491528 | tf_op jit(solution)/shard_map/KE0/P41_0/ppermute | solution.py:40
  60.4 1.6 %collective-permute-start.13 = (bf16[8,80,128]{2,1,0:T(8,128)(2,1)S(1)}, bf16[8,80,128]{2,1,0:T(8,128)(2,1)S(1)}, u32[]{:S(2)}, u32[]{:S(2)}) collective-permute-start(bf16[8,80,128]{2,1,0:T(8,128)(2,1)S(1)} %get-tuple-element.32), channel_id=1, source_target_pairs={{0,16},{8,24},{16,0},{24,8},{1,17},{9,25},{17,1},{25,9},{2,18},{10... | collective-permute-start | bytes 491528 | tf_op jit(solution)/shard_map/KE1_13/P42_1/ppermute | solution.py:40
  62.0 1.4 %collective-permute-start.14 = (bf16[8,80,128]{2,1,0:T(8,128)(2,1)S(1)}, bf16[8,80,128]{2,1,0:T(8,128)(2,1)S(1)}, u32[]{:S(2)}, u32[]{:S(2)}) collective-permute-start(bf16[8,80,128]{2,1,0:T(8,128)(2,1)S(1)} %get-tuple-element.33), channel_id=1, source_target_pairs={{0,24},{8,16},{16,8},{24,0},{1,25},{9,17},{17,9},{25,1},{2,26},{10... | collective-permute-start | bytes 491528 | tf_op jit(solution)/shard_map/KE1_13/P43_1/ppermute | solution.py:40
  63.4 2.3 %all-gather.2 = bf16[16,128,128]{2,1,0:T(8,128)(2,1)} all-gather(bf16[8,128,128]{2,1,0:T(8,128)(2,1)S(1)} %butterfly_step.17.refs_7_), channel_id=4, replica_groups={{0,1},{2,3},{4,5},{6,7},{8,9},{10,11},{12,13},{14,15},{16,17},{18,19},{..., dimensions={0}, use_global_device_ids=true | all-gather | bytes 786432 | tf_op jit(solution)/shard_map/K22/all_gather | solution.py:331
  65.7 2.6 %butterfly_step.18 = (bf16[8,80,128]{2,1,0:T(8,128)(2,1)S(1)}, bf16[8,80,128]{2,1,0:T(8,128)(2,1)S(1)}, bf16[8,80,128]{2,1,0:T(8,128)(2,1)S(1)}, bf16[8,80,128]{2,1,0:T(8,128)(2,1)S(1)}, bf16[8,128,128]{2,1,0:T(8,128)(2,1)S(1)}) custom-call(s32[3,8]{1,0:T(4,128)S(1)} %copy-done.1, bf16[32,1,640,128]{3,2,1,0:T(8,128)(2,1)} %refs_0_.27, ...), custom_call_target="tpu_custom_call" | custom-call | tf_op jit(solution)/shard_map/KE2_23/butterfly_step/pallas_call | solution.py:230
  69.0 1.6 %collective-permute-start.16 = (bf16[8,80,128]{2,1,0:T(8,128)(2,1)S(1)}, bf16[8,80,128]{2,1,0:T(8,128)(2,1)S(1)}, u32[]{:S(2)}, u32[]{:S(2)}) collective-permute-start(bf16[8,80,128]{2,1,0:T(8,128)(2,1)S(1)} %get-tuple-element.36), channel_id=1, source_target_pairs={{0,16},{8,24},{16,0},{24,8},{1,17},{9,25},{17,1},{25,9},{2,18},{10... | collective-permute-start | bytes 491528 | tf_op jit(solution)/shard_map/KE2_23/P42_2/ppermute | solution.py:40
  70.5 2.2 %all-gather.3 = bf16[16,128,128]{2,1,0:T(8,128)(2,1)S(1)} all-gather(bf16[8,128,128]{2,1,0:T(8,128)(2,1)S(1)} %get-tuple-element.29), channel_id=5, replica_groups={{0,1},{2,3},{4,5},{6,7},{8,9},{10,11},{12,13},{14,15},{16,17},{18,19},{..., dimensions={0}, use_global_device_ids=true | all-gather | bytes 786432 | tf_op jit(solution)/shard_map/KE2_23/all_gather | solution.py:331
  72.7 1.4 %collective-permute-start.17 = (bf16[8,80,128]{2,1,0:T(8,128)(2,1)S(1)}, bf16[8,80,128]{2,1,0:T(8,128)(2,1)S(1)}, u32[]{:S(2)}, u32[]{:S(2)}) collective-permute-start(bf16[8,80,128]{2,1,0:T(8,128)(2,1)S(1)} %get-tuple-element.37), channel_id=1, source_target_pairs={{0,24},{8,16},{16,8},{24,0},{1,25},{9,17},{17,9},{25,1},{2,26},{10... | collective-permute-start | bytes 491528 | tf_op jit(solution)/shard_map/KE2_23/P43_2/ppermute | solution.py:40
  74.1 1.9 %butterfly_step.19 = (bf16[8,80,128]{2,1,0:T(8,128)(2,1)S(1)}, bf16[8,80,128]{2,1,0:T(8,128)(2,1)S(1)}, bf16[8,80,128]{2,1,0:T(8,128)(2,1)S(1)}, bf16[8,80,128]{2,1,0:T(8,128)(2,1)S(1)}) custom-call(s32[3,8]{1,0:T(4,128)S(1)} %copy-done.1, bf16[32,1,640,128]{3,2,1,0:T(8,128)(2,1)} %refs_0_.27, bf16[32,1,640,128]{3,2,1,0:T(8,128)(2,1)} %copy-done.3, ...), custom_call_target="tpu_custom_call" | custom-call | tf_op jit(solution)/shard_map/KE3/butterfly_step/pallas_call | solution.py:230
  76.7 1.6 %collective-permute-start.19 = (bf16[8,80,128]{2,1,0:T(8,128)(2,1)S(1)}, bf16[8,80,128]{2,1,0:T(8,128)(2,1)S(1)}, u32[]{:S(2)}, u32[]{:S(2)}) collective-permute-start(bf16[8,80,128]{2,1,0:T(8,128)(2,1)S(1)} %get-tuple-element.39), channel_id=1, source_target_pairs={{0,16},{8,24},{16,0},{24,8},{1,17},{9,25},{17,1},{25,9},{2,18},{10... | collective-permute-start | bytes 491528 | tf_op jit(solution)/shard_map/KE3/P42_3/ppermute | solution.py:40
  79.0 1.4 %collective-permute-start.20 = (bf16[8,80,128]{2,1,0:T(8,128)(2,1)S(1)}, bf16[8,80,128]{2,1,0:T(8,128)(2,1)S(1)}, u32[]{:S(2)}, u32[]{:S(2)}) collective-permute-start(bf16[8,80,128]{2,1,0:T(8,128)(2,1)S(1)} %get-tuple-element.40), channel_id=1, source_target_pairs={{0,24},{8,16},{16,8},{24,0},{1,25},{9,17},{17,9},{25,1},{2,26},{10... | collective-permute-start | bytes 491528 | tf_op jit(solution)/shard_map/KE3/P43_3/ppermute | solution.py:40
  80.5 2.7 %collective-permute-done.18 = bf16[8,80,128]{2,1,0:T(8,128)(2,1)S(1)} collective-permute-done((bf16[8,80,128]{2,1,0:T(8,128)(2,1)S(1)}, bf16[8,80,128]{2,1,0:T(8,128)(2,1)S(1)}, u32[]{:S(2)}, u32[]{:S(2)}) %collective-permute-start.18) | collective-permute-done | bytes 163872 | tf_op jit(solution)/shard_map/KE3/P41_3/ppermute | solution.py:40
  84.2 2.6 %collective-permute-done.20 = bf16[8,80,128]{2,1,0:T(8,128)(2,1)S(1)} collective-permute-done((bf16[8,80,128]{2,1,0:T(8,128)(2,1)S(1)}, bf16[8,80,128]{2,1,0:T(8,128)(2,1)S(1)}, u32[]{:S(2)}, u32[]{:S(2)}) %collective-permute-start.20) | collective-permute-done | bytes 163872 | tf_op jit(solution)/shard_map/KE3/P43_3/ppermute | solution.py:40
  (55 shorter events, 15.3 us)
Async XLA Ops:
  0.0 8.9 %collective-permute-start = (bf16[32,1,640,128]{3,2,1,0:T(8,128)(2,1)}, bf16[32,1,640,128]{3,2,1,0:T(8,128)(2,1)S(1)}, u32[]{:S(2)}, u32[]{:S(2)}) collective-permute-start(bf16[32,1,640,128]{3,2,1,0:T(8,128)(2,1)} %refs_0_.27), channel_id=1, source_target_pairs={{0,1},{1,0},{2,3},{3,2},{4,5},{5,4},{6,7},{7,6},{8,9},{9,8},{10,11... | collective-permute-start | bytes 15728648 | tf_op jit(solution)/shard_map/KG0/PG_0/ppermute | solution.py:40
  0.5 0.7 copy-start.2
  2.8 16.2 %collective-permute-start.2 = (bf16[8,128,128]{2,1,0:T(8,128)(2,1)S(1)}, bf16[8,128,128]{2,1,0:T(8,128)(2,1)S(1)}, u32[]{:S(2)}, u32[]{:S(2)}) collective-permute-start(bf16[8,128,128]{2,1,0:T(8,128)(2,1)S(1)} %compress_slots.4.refs_3_.refs_2_), channel_id=1, source_target_pairs={{0,4},{1,5},{2,6},{3,7},{4,0},{5,1},{6,2},{7,3},{8,12},{9,13},{10,... | collective-permute-start | bytes 786440 | tf_op jit(solution)/shard_map/KC0/P1_0/ppermute | solution.py:40
  8.9 2.3 %copy-start.3 = (bf16[32,1,640,128]{3,2,1,0:T(8,128)(2,1)}, bf16[32,1,640,128]{3,2,1,0:T(8,128)(2,1)S(1)}, u32[]{:S(2)}) copy-start(bf16[32,1,640,128]{3,2,1,0:T(8,128)(2,1)S(1)} %collective-permute-done.refs_4_.refs_1_) | copy-start | bytes 15728644
  13.0 6.1 %copy-start.1 = (s32[3,8]{1,0:T(4,128)S(1)}, s32[3,8]{1,0:T(4,128)}, u32[]{:S(2)}) copy-start(s32[3,8]{1,0:T(4,128)} %ranks.19) | copy-start | bytes 292
  14.8 17.0 %collective-permute-start.4 = (bf16[8,128,128]{2,1,0:T(8,128)(2,1)S(1)}, bf16[8,128,128]{2,1,0:T(8,128)(2,1)S(1)}, u32[]{:S(2)}, u32[]{:S(2)}) collective-permute-start(bf16[8,128,128]{2,1,0:T(8,128)(2,1)S(1)} %compress_slots.7.refs_4_.refs_2_), channel_id=1, source_target_pairs={{0,4},{1,5},{2,6},{3,7},{4,0},{5,1},{6,2},{7,3},{8,12},{9,13},{10,... | collective-permute-start | bytes 786440 | tf_op jit(solution)/shard_map/KC1/P1_1/ppermute | solution.py:40
  20.4 17.0 %collective-permute-start.3 = (bf16[8,128,128]{2,1,0:T(8,128)(2,1)S(1)}, bf16[8,128,128]{2,1,0:T(8,128)(2,1)S(1)}, u32[]{:S(2)}, u32[]{:S(2)}) collective-permute-start(bf16[8,128,128]{2,1,0:T(8,128)(2,1)S(1)} %butterfly_step.10.refs_4_.refs_2_), channel_id=1, source_target_pairs={{0,2},{1,3},{2,0},{3,1},{4,6},{5,7},{6,4},{7,5},{8,10},{9,11},{10,... | collective-permute-start | bytes 786440 | tf_op jit(solution)/shard_map/K10/P2_0/ppermute | solution.py:40
  21.8 21.1 %collective-permute-start.1 = (bf16[8,128,128]{2,1,0:T(8,128)(2,1)S(1)}, bf16[8,128,128]{2,1,0:T(8,128)(2,1)S(1)}, u32[]{:S(2)}, u32[]{:S(2)}) collective-permute-start(bf16[8,128,128]{2,1,0:T(8,128)(2,1)S(1)} %compress_slots.5.refs_3_.refs_2_), channel_id=1, source_target_pairs={{0,4},{1,5},{2,6},{3,7},{4,0},{5,1},{6,2},{7,3},{8,12},{9,13},{10,... | collective-permute-start | bytes 786440 | tf_op jit(solution)/shard_map/KC2/P1_2/ppermute | solution.py:40
  33.1 15.0 %collective-permute-start.6 = (bf16[8,128,128]{2,1,0:T(8,128)(2,1)S(1)}, bf16[8,128,128]{2,1,0:T(8,128)(2,1)S(1)}, u32[]{:S(2)}, u32[]{:S(2)}) collective-permute-start(bf16[8,128,128]{2,1,0:T(8,128)(2,1)S(1)} %butterfly_step.11.refs_4_.refs_2_), channel_id=1, source_target_pairs={{0,2},{1,3},{2,0},{3,1},{4,6},{5,7},{6,4},{7,5},{8,10},{9,11},{10,... | collective-permute-start | bytes 786440 | tf_op jit(solution)/shard_map/K11/P2_1/ppermute | solution.py:40
  33.9 19.8 %collective-permute-start.7 = (bf16[8,128,128]{2,1,0:T(8,128)(2,1)S(1)}, bf16[8,128,128]{2,1,0:T(8,128)(2,1)S(1)}, u32[]{:S(2)}, u32[]{:S(2)}) collective-permute-start(bf16[8,128,128]{2,1,0:T(8,128)(2,1)S(1)} %compress_slots.6.refs_3_.refs_5_), channel_id=1, source_target_pairs={{0,4},{1,5},{2,6},{3,7},{4,0},{5,1},{6,2},{7,3},{8,12},{9,13},{10,... | collective-permute-start | bytes 786440 | tf_op jit(solution)/shard_map/KC3/P1_3/ppermute | solution.py:40
  44.3 14.2 %collective-permute-start.5 = (bf16[8,128,128]{2,1,0:T(8,128)(2,1)S(1)}, bf16[8,128,128]{2,1,0:T(8,128)(2,1)S(1)}, u32[]{:S(2)}, u32[]{:S(2)}) collective-permute-start(bf16[8,128,128]{2,1,0:T(8,128)(2,1)S(1)} %butterfly_step.14.refs_4_.refs_2_), channel_id=1, source_target_pairs={{0,2},{1,3},{2,0},{3,1},{4,6},{5,7},{6,4},{7,5},{8,10},{9,11},{10,... | collective-permute-start | bytes 786440 | tf_op jit(solution)/shard_map/K12/P2_2/ppermute | solution.py:40
  45.1 15.2 %collective-permute-start.10 = (bf16[8,80,128]{2,1,0:T(8,128)(2,1)S(1)}, bf16[8,80,128]{2,1,0:T(8,128)(2,1)S(1)}, u32[]{:S(2)}, u32[]{:S(2)}) collective-permute-start(bf16[8,80,128]{2,1,0:T(8,128)(2,1)S(1)} %get-tuple-element.27), channel_id=1, source_target_pairs={{0,16},{8,24},{16,0},{24,8},{1,17},{9,25},{17,1},{25,9},{2,18},{10... | collective-permute-start | bytes 491528 | tf_op jit(solution)/shard_map/KE0/P42_0/ppermute | solution.py:40
  46.7 15.3 %collective-permute-start.11 = (bf16[8,80,128]{2,1,0:T(8,128)(2,1)S(1)}, bf16[8,80,128]{2,1,0:T(8,128)(2,1)S(1)}, u32[]{:S(2)}, u32[]{:S(2)}) collective-permute-start(bf16[8,80,128]{2,1,0:T(8,128)(2,1)S(1)} %get-tuple-element.28), channel_id=1, source_target_pairs={{0,24},{8,16},{16,8},{24,0},{1,25},{9,17},{17,9},{25,1},{2,26},{10... | collective-permute-start | bytes 491528 | tf_op jit(solution)/shard_map/KE0/P43_0/ppermute | solution.py:40
  56.3 9.4 %collective-permute-start.8 = (bf16[8,128,128]{2,1,0:T(8,128)(2,1)S(1)}, bf16[8,128,128]{2,1,0:T(8,128)(2,1)S(1)}, u32[]{:S(2)}, u32[]{:S(2)}) collective-permute-start(bf16[8,128,128]{2,1,0:T(8,128)(2,1)S(1)} %get-tuple-element.25.refs_5_), channel_id=1, source_target_pairs={{0,2},{1,3},{2,0},{3,1},{4,6},{5,7},{6,4},{7,5},{8,10},{9,11},{10,... | collective-permute-start | bytes 786440 | tf_op jit(solution)/shard_map/KE1_13/P2_3/ppermute | solution.py:40
  57.0 8.7 %collective-permute-start.9 = (bf16[8,80,128]{2,1,0:T(8,128)(2,1)S(1)}, bf16[8,80,128]{2,1,0:T(8,128)(2,1)S(1)}, u32[]{:S(2)}, u32[]{:S(2)}) collective-permute-start(bf16[8,80,128]{2,1,0:T(8,128)(2,1)S(1)} %get-tuple-element.26), channel_id=1, source_target_pairs={{0,8},{8,0},{16,24},{24,16},{1,9},{9,1},{17,25},{25,17},{2,10},{10... | collective-permute-start | bytes 491528 | tf_op jit(solution)/shard_map/KE0/P41_0/ppermute | solution.py:40
  58.5 14.2 %collective-permute-start.12 = (bf16[8,80,128]{2,1,0:T(8,128)(2,1)S(1)}, bf16[8,80,128]{2,1,0:T(8,128)(2,1)S(1)}, u32[]{:S(2)}, u32[]{:S(2)}) collective-permute-start(bf16[8,80,128]{2,1,0:T(8,128)(2,1)S(1)} %get-tuple-element.31), channel_id=1, source_target_pairs={{0,8},{8,0},{16,24},{24,16},{1,9},{9,1},{17,25},{25,17},{2,10},{10... | collective-permute-start | bytes 491528 | tf_op jit(solution)/shard_map/KE1_13/P41_1/ppermute | solution.py:40
  60.4 5.4 %copy-start = (bf16[8,128,128]{2,1,0:T(8,128)(2,1)}, bf16[8,128,128]{2,1,0:T(8,128)(2,1)S(1)}, u32[]{:S(2)}) copy-start(bf16[8,128,128]{2,1,0:T(8,128)(2,1)S(1)} %butterfly_step.17.refs_7_) | copy-start | bytes 786436
  60.4 13.7 %collective-permute-start.13 = (bf16[8,80,128]{2,1,0:T(8,128)(2,1)S(1)}, bf16[8,80,128]{2,1,0:T(8,128)(2,1)S(1)}, u32[]{:S(2)}, u32[]{:S(2)}) collective-permute-start(bf16[8,80,128]{2,1,0:T(8,128)(2,1)S(1)} %get-tuple-element.32), channel_id=1, source_target_pairs={{0,16},{8,24},{16,0},{24,8},{1,17},{9,25},{17,1},{25,9},{2,18},{10... | collective-permute-start | bytes 491528 | tf_op jit(solution)/shard_map/KE1_13/P42_1/ppermute | solution.py:40
  62.0 12.1 %collective-permute-start.14 = (bf16[8,80,128]{2,1,0:T(8,128)(2,1)S(1)}, bf16[8,80,128]{2,1,0:T(8,128)(2,1)S(1)}, u32[]{:S(2)}, u32[]{:S(2)}) collective-permute-start(bf16[8,80,128]{2,1,0:T(8,128)(2,1)S(1)} %get-tuple-element.33), channel_id=1, source_target_pairs={{0,24},{8,16},{16,8},{24,0},{1,25},{9,17},{17,9},{25,1},{2,26},{10... | collective-permute-start | bytes 491528 | tf_op jit(solution)/shard_map/KE1_13/P43_1/ppermute | solution.py:40
  68.4 10.6 %collective-permute-start.15 = (bf16[8,80,128]{2,1,0:T(8,128)(2,1)S(1)}, bf16[8,80,128]{2,1,0:T(8,128)(2,1)S(1)}, u32[]{:S(2)}, u32[]{:S(2)}) collective-permute-start(bf16[8,80,128]{2,1,0:T(8,128)(2,1)S(1)} %get-tuple-element.35), channel_id=1, source_target_pairs={{0,8},{8,0},{16,24},{24,16},{1,9},{9,1},{17,25},{25,17},{2,10},{10... | collective-permute-start | bytes 491528 | tf_op jit(solution)/shard_map/KE2_23/P41_2/ppermute | solution.py:40
  69.0 11.4 %collective-permute-start.16 = (bf16[8,80,128]{2,1,0:T(8,128)(2,1)S(1)}, bf16[8,80,128]{2,1,0:T(8,128)(2,1)S(1)}, u32[]{:S(2)}, u32[]{:S(2)}) collective-permute-start(bf16[8,80,128]{2,1,0:T(8,128)(2,1)S(1)} %get-tuple-element.36), channel_id=1, source_target_pairs={{0,16},{8,24},{16,0},{24,8},{1,17},{9,25},{17,1},{25,9},{2,18},{10... | collective-permute-start | bytes 491528 | tf_op jit(solution)/shard_map/KE2_23/P42_2/ppermute | solution.py:40
  72.7 7.7 %collective-permute-start.17 = (bf16[8,80,128]{2,1,0:T(8,128)(2,1)S(1)}, bf16[8,80,128]{2,1,0:T(8,128)(2,1)S(1)}, u32[]{:S(2)}, u32[]{:S(2)}) collective-permute-start(bf16[8,80,128]{2,1,0:T(8,128)(2,1)S(1)} %get-tuple-element.37), channel_id=1, source_target_pairs={{0,24},{8,16},{16,8},{24,0},{1,25},{9,17},{17,9},{25,1},{2,26},{10... | collective-permute-start | bytes 491528 | tf_op jit(solution)/shard_map/KE2_23/P43_2/ppermute | solution.py:40
  76.0 7.2 %collective-permute-start.18 = (bf16[8,80,128]{2,1,0:T(8,128)(2,1)S(1)}, bf16[8,80,128]{2,1,0:T(8,128)(2,1)S(1)}, u32[]{:S(2)}, u32[]{:S(2)}) collective-permute-start(bf16[8,80,128]{2,1,0:T(8,128)(2,1)S(1)} %get-tuple-element.38), channel_id=1, source_target_pairs={{0,8},{8,0},{16,24},{24,16},{1,9},{9,1},{17,25},{25,17},{2,10},{10... | collective-permute-start | bytes 491528 | tf_op jit(solution)/shard_map/KE3/P41_3/ppermute | solution.py:40
  76.7 7.5 %collective-permute-start.19 = (bf16[8,80,128]{2,1,0:T(8,128)(2,1)S(1)}, bf16[8,80,128]{2,1,0:T(8,128)(2,1)S(1)}, u32[]{:S(2)}, u32[]{:S(2)}) collective-permute-start(bf16[8,80,128]{2,1,0:T(8,128)(2,1)S(1)} %get-tuple-element.39), channel_id=1, source_target_pairs={{0,16},{8,24},{16,0},{24,8},{1,17},{9,25},{17,1},{25,9},{2,18},{10... | collective-permute-start | bytes 491528 | tf_op jit(solution)/shard_map/KE3/P42_3/ppermute | solution.py:40
  79.0 7.9 %collective-permute-start.20 = (bf16[8,80,128]{2,1,0:T(8,128)(2,1)S(1)}, bf16[8,80,128]{2,1,0:T(8,128)(2,1)S(1)}, u32[]{:S(2)}, u32[]{:S(2)}) collective-permute-start(bf16[8,80,128]{2,1,0:T(8,128)(2,1)S(1)} %get-tuple-element.40), channel_id=1, source_target_pairs={{0,24},{8,16},{16,8},{24,0},{1,25},{9,17},{17,9},{25,1},{2,26},{10... | collective-permute-start | bytes 491528 | tf_op jit(solution)/shard_map/KE3/P43_3/ppermute | solution.py:40
  84.2 2.7 %copy-start.4 = (bf16[128,1,1,80,128]{4,3,2,1,0:T(8,128)(2,1)}, bf16[128,1,1,80,128]{4,3,2,1,0:T(8,128)(2,1)S(1)}, u32[]{:S(2)}) copy-start(bf16[128,1,1,80,128]{4,3,2,1,0:T(8,128)(2,1)S(1)} %bitcast_dynamic-update-slice_fusion.1) | copy-start | bytes 7864324

commit v5 on v4

--- a/solution.py
+++ b/solution.py
@@ -23,8 +23,8 @@
     "12",
     "21",
     "E1+13",
-    "22",
-    "E2+23<P4_0",
+    "22<P4_0",
+    "E2+23",
     "E3<P4_1",
 )
 COSTS = {}

time: 88.3 us -> 87.7 us (level)
  starting transfers between devices: 33.4 us -> 32.4 us
    ppermute x21, starting transfers between devices: 33.4 us -> 32.4 us  [from_partner(): return lax.ppermute(array, axis, pairs)]
    unnamed x10 -> x8, local copies, waits for them, and re-layouts: 3 us -> 3 us
  transfers between devices with their start and end apart: 21 -> 21, of which waited for: 7 -> 8; matrix products, arithmetic and copies ran while one was open for 1% -> 1% of each run, Pallas kernels for 27% -> 28%
where the time goes in v5:
time: 87.7 us; the launch traced here: 87 us
  starting transfers between devices  32.4 us (37%)
  Pallas kernels  24 us (27%)
  waiting for transfers between devices  16.9 us (19%)
  blocking collectives  8.98 us (10%)
  local copies, waits for them, and re-layouts  4.42 us (5%)
    ppermute x21, starting transfers between devices, from_partner(): return lax.ppermute(array, axis, pairs)  32.4 us
    pallas_call x10, Pallas kernels, fused(): pl.pallas_call(kernel, out_shape=outs + [jax.ShapeDtypeStruct(h.shape, h....  17.1 us
    ppermute x21, waiting for transfers between devices, from_partner(): return lax.ppermute(array, axis, pairs)  16.9 us
    all_gather x4, blocking collectives, stepped(): state[k] = lax.all_gather(made[0], 'deg', axis_index_groups=groups)  8.98 us
    pallas_call x4, Pallas kernels, compress_slots(): pl.pallas_call(ordered(functools.partial(compress_kernel, first, b), 3, l...  6.89 us
    unnamed x8, local copies, waits for them, and re-layouts  3 us
  transfers between devices with their start and end apart: 21, of which 8 were waited for; matrix products, arithmetic and copies ran while one was open for 1% of the time, Pallas kernels for 28%

profile of v5, /device:TPU:0, one launch (start us, length us, event | category | flops | bytes accessed | tf_op | source)
XLA Modules:
  0.0 87.0 jit_solution(16324370449156506832)
XLA Ops:
  1.1 1.7 %compress_slots.4.refs_3_.refs_2_ = bf16[8,128,128]{2,1,0:T(8,128)(2,1)S(1)} custom-call(s32[32]{0:T(128)S(1)} %copy-done.1, bf16[32,320,128]{2,1,0:T(8,128)(2,1)} %refs_1_.13, bf16[32,320,128]{2,1,0:T(8,128)(2,1)} %refs_2_.7), custom_call_target="tpu_custom_call" | custom-call | tf_op jit(solution)/shard_map/KC0/compress_slots/pallas_call | solution.py:107
  2.8 3.7 %collective-permute-start.2 = (bf16[8,128,128]{2,1,0:T(8,128)(2,1)S(1)}, bf16[8,128,128]{2,1,0:T(8,128)(2,1)S(1)}, u32[]{:S(2)}, u32[]{:S(2)}) collective-permute-start(bf16[8,128,128]{2,1,0:T(8,128)(2,1)S(1)} %compress_slots.4.refs_3_.refs_2_), channel_id=1, source_target_pairs={{0,4},{1,5},{2,6},{3,7},{4,0},{5,1},{6,2},{7,3},{8,12},{9,13},{10,... | collective-permute-start | bytes 786440 | tf_op jit(solution)/shard_map/KC0/P1_0/ppermute | solution.py:40
  6.5 1.7 %compress_slots.5.refs_3_.refs_2_ = bf16[8,128,128]{2,1,0:T(8,128)(2,1)S(1)} custom-call(s32[32]{0:T(128)S(1)} %copy-done.1, bf16[32,320,128]{2,1,0:T(8,128)(2,1)} %refs_1_.13, bf16[32,320,128]{2,1,0:T(8,128)(2,1)} %refs_2_.7, bf16[8,128,128]{2,1,0:T(8,128)(2,1)S(1)} %compress_slots.4.refs_3_.refs_2_), custom_call_target="tpu_custom_call" | custom-call | tf_op jit(solution)/shard_map/KC2/compress_slots/pallas_call | solution.py:107
  9.0 2.3 %copy-done.2 = bf16[32,1,640,128]{3,2,1,0:T(8,128)(2,1)} copy-done((bf16[32,1,640,128]{3,2,1,0:T(8,128)(2,1)}, bf16[32,1,640,128]{3,2,1,0:T(8,128)(2,1)S(1)}, u32[]{:S(2)}) %copy-start.2) | copy-done | bytes 5242904
  11.3 1.7 %compress_slots.6.refs_3_.refs_5_ = bf16[8,128,128]{2,1,0:T(8,128)(2,1)S(1)} custom-call(s32[32]{0:T(128)S(1)} %copy-done.1, bf16[32,320,128]{2,1,0:T(8,128)(2,1)} %refs_1_.13, bf16[32,320,128]{2,1,0:T(8,128)(2,1)} %refs_2_.7, bf16[8,128,128]{2,1,0:T(8,128)(2,1)S(1)} %compress_slots.5.refs_3_.refs_2_, bf16[32,1,640,128]{3,2,1,0:T(8,128)(2,1)} %copy-done.2), custom_call_target="tpu_custom_call" | custom-call | tf_op jit(solution)/shard_map/KC3/compress_slots/pallas_call | solution.py:107
  13.0 1.7 %compress_slots.7.refs_4_.refs_2_ = bf16[8,128,128]{2,1,0:T(8,128)(2,1)S(1)} custom-call(s32[32]{0:T(128)S(1)} %copy-done.1, bf16[32,320,128]{2,1,0:T(8,128)(2,1)} %refs_1_.13, bf16[32,320,128]{2,1,0:T(8,128)(2,1)} %refs_2_.7, bf16[8,128,128]{2,1,0:T(8,128)(2,1)S(1)} %compress_slots.6.refs_3_.refs_5_), custom_call_target="tpu_custom_call" | custom-call | tf_op jit(solution)/shard_map/KC1/compress_slots/pallas_call | solution.py:107
  14.8 4.0 %collective-permute-start.4 = (bf16[8,128,128]{2,1,0:T(8,128)(2,1)S(1)}, bf16[8,128,128]{2,1,0:T(8,128)(2,1)S(1)}, u32[]{:S(2)}, u32[]{:S(2)}) collective-permute-start(bf16[8,128,128]{2,1,0:T(8,128)(2,1)S(1)} %compress_slots.7.refs_4_.refs_2_), channel_id=1, source_target_pairs={{0,4},{1,5},{2,6},{3,7},{4,0},{5,1},{6,2},{7,3},{8,12},{9,13},{10,... | collective-permute-start | bytes 786440 | tf_op jit(solution)/shard_map/KC1/P1_1/ppermute | solution.py:40
  19.1 1.3 %butterfly_step.10.refs_4_.refs_2_ = bf16[8,128,128]{2,1,0:T(8,128)(2,1)S(1)} custom-call(s32[3,8]{1,0:T(4,128)S(1)} %copy-done, bf16[2,32,1,128,128]{4,3,2,1,0:T(8,128)(2,1)} %refs_3_.3, bf16[2,32,1,128,128]{4,3,2,1,0:T(8,128)(2,1)} %refs_4_.3, bf16[8,128,128]{2,1,0:T(8,128)(2,1)S(1)} %compress_slots.4.refs_3_.refs_2_, ...), custom_call_target="tpu_custom_call" | custom-call | tf_op jit(solution)/shard_map/K10/butterfly_step/pallas_call | solution.py:230
  21.8 2.8 %collective-permute-start.1 = (bf16[8,128,128]{2,1,0:T(8,128)(2,1)S(1)}, bf16[8,128,128]{2,1,0:T(8,128)(2,1)S(1)}, u32[]{:S(2)}, u32[]{:S(2)}) collective-permute-start(bf16[8,128,128]{2,1,0:T(8,128)(2,1)S(1)} %compress_slots.5.refs_3_.refs_2_), channel_id=1, source_target_pairs={{0,4},{1,5},{2,6},{3,7},{4,0},{5,1},{6,2},{7,3},{8,12},{9,13},{10,... | collective-permute-start | bytes 786440 | tf_op jit(solution)/shard_map/KC2/P1_2/ppermute | solution.py:40
  24.6 7.1 %collective-permute-done.4.refs_3_ = bf16[8,128,128]{2,1,0:T(8,128)(2,1)S(1)} collective-permute-done((bf16[8,128,128]{2,1,0:T(8,128)(2,1)S(1)}, bf16[8,128,128]{2,1,0:T(8,128)(2,1)S(1)}, u32[]{:S(2)}, u32[]{:S(2)}) %collective-permute-start.4) | collective-permute-done | bytes 262176 | tf_op jit(solution)/shard_map/KC1/P1_1/ppermute | solution.py:40
  31.8 1.3 %butterfly_step.11.refs_4_.refs_2_ = bf16[8,128,128]{2,1,0:T(8,128)(2,1)S(1)} custom-call(s32[3,8]{1,0:T(4,128)S(1)} %copy-done, bf16[2,32,1,128,128]{4,3,2,1,0:T(8,128)(2,1)} %refs_3_.3, bf16[2,32,1,128,128]{4,3,2,1,0:T(8,128)(2,1)} %refs_4_.3, bf16[8,128,128]{2,1,0:T(8,128)(2,1)S(1)} %compress_slots.7.refs_4_.refs_2_, ...), custom_call_target="tpu_custom_call" | custom-call | tf_op jit(solution)/shard_map/K11/butterfly_step/pallas_call | solution.py:230
  33.9 3.6 %collective-permute-start.7 = (bf16[8,128,128]{2,1,0:T(8,128)(2,1)S(1)}, bf16[8,128,128]{2,1,0:T(8,128)(2,1)S(1)}, u32[]{:S(2)}, u32[]{:S(2)}) collective-permute-start(bf16[8,128,128]{2,1,0:T(8,128)(2,1)S(1)} %compress_slots.6.refs_3_.refs_5_), channel_id=1, source_target_pairs={{0,4},{1,5},{2,6},{3,7},{4,0},{5,1},{6,2},{7,3},{8,12},{9,13},{10,... | collective-permute-start | bytes 786440 | tf_op jit(solution)/shard_map/KC3/P1_3/ppermute | solution.py:40
  38.8 2.2 %all-gather = bf16[16,128,128]{2,1,0:T(8,128)(2,1)S(1)} all-gather(bf16[8,128,128]{2,1,0:T(8,128)(2,1)S(1)} %butterfly_step.12.refs_3_), channel_id=2, replica_groups={{0,1},{2,3},{4,5},{6,7},{8,9},{10,11},{12,13},{14,15},{16,17},{18,19},{..., dimensions={0}, use_global_device_ids=true | all-gather | bytes 786432 | tf_op jit(solution)/shard_map/K20/all_gather | solution.py:331
  41.0 1.9 %butterfly_step.13 = (bf16[8,80,128]{2,1,0:T(8,128)(2,1)S(1)}, bf16[8,80,128]{2,1,0:T(8,128)(2,1)S(1)}, bf16[8,80,128]{2,1,0:T(8,128)(2,1)S(1)}, bf16[8,80,128]{2,1,0:T(8,128)(2,1)S(1)}) custom-call(s32[3,8]{1,0:T(4,128)S(1)} %copy-done, bf16[32,1,640,128]{3,2,1,0:T(8,128)(2,1)} %refs_0_.27, bf16[32,1,640,128]{3,2,1,0:T(8,128)(2,1)} %copy-done.2, ...), custom_call_target="tpu_custom_call" | custom-call | tf_op jit(solution)/shard_map/KE0/butterfly_step/pallas_call | solution.py:230
  42.9 1.4 %butterfly_step.14.refs_4_.refs_2_ = bf16[8,128,128]{2,1,0:T(8,128)(2,1)S(1)} custom-call(s32[3,8]{1,0:T(4,128)S(1)} %copy-done, bf16[2,32,1,128,128]{4,3,2,1,0:T(8,128)(2,1)} %refs_3_.3, bf16[2,32,1,128,128]{4,3,2,1,0:T(8,128)(2,1)} %refs_4_.3, bf16[8,128,128]{2,1,0:T(8,128)(2,1)S(1)} %compress_slots.5.refs_3_.refs_2_, ...), custom_call_target="tpu_custom_call" | custom-call | tf_op jit(solution)/shard_map/K12/butterfly_step/pallas_call | solution.py:230
  45.1 2.5 %collective-permute-start.10 = (bf16[8,80,128]{2,1,0:T(8,128)(2,1)S(1)}, bf16[8,80,128]{2,1,0:T(8,128)(2,1)S(1)}, u32[]{:S(2)}, u32[]{:S(2)}) collective-permute-start(bf16[8,80,128]{2,1,0:T(8,128)(2,1)S(1)} %get-tuple-element.27), channel_id=1, source_target_pairs={{0,24},{8,16},{16,8},{24,0},{1,25},{9,17},{17,9},{25,1},{2,26},{10... | collective-permute-start | bytes 491528 | tf_op jit(solution)/shard_map/KE0/P43_0/ppermute | solution.py:40
  50.0 2.3 %all-gather.1 = bf16[16,128,128]{2,1,0:T(8,128)(2,1)} all-gather(bf16[8,128,128]{2,1,0:T(8,128)(2,1)S(1)} %butterfly_step.15.refs_7_), channel_id=3, replica_groups={{0,1},{2,3},{4,5},{6,7},{8,9},{10,11},{12,13},{14,15},{16,17},{18,19},{..., dimensions={0}, use_global_device_ids=true | all-gather | bytes 786432 | tf_op jit(solution)/shard_map/K21/all_gather | solution.py:331
  52.3 1.4 %collective-permute-done.7.refs_6_ = bf16[8,128,128]{2,1,0:T(8,128)(2,1)S(1)} collective-permute-done((bf16[8,128,128]{2,1,0:T(8,128)(2,1)S(1)}, bf16[8,128,128]{2,1,0:T(8,128)(2,1)S(1)}, u32[]{:S(2)}, u32[]{:S(2)}) %collective-permute-start.7) | collective-permute-done | bytes 262176 | tf_op jit(solution)/shard_map/KC3/P1_3/ppermute | solution.py:40
  53.7 2.6 %butterfly_step.16 = (bf16[8,80,128]{2,1,0:T(8,128)(2,1)S(1)}, bf16[8,80,128]{2,1,0:T(8,128)(2,1)S(1)}, bf16[8,80,128]{2,1,0:T(8,128)(2,1)S(1)}, bf16[8,80,128]{2,1,0:T(8,128)(2,1)S(1)}, bf16[8,128,128]{2,1,0:T(8,128)(2,1)S(1)}) custom-call(s32[3,8]{1,0:T(4,128)S(1)} %copy-done, bf16[32,1,640,128]{3,2,1,0:T(8,128)(2,1)} %refs_0_.27, ...), custom_call_target="tpu_custom_call" | custom-call | tf_op jit(solution)/shard_map/KE1_13/butterfly_step/pallas_call | solution.py:230
  57.0 1.5 %collective-permute-start.12 = (bf16[8,80,128]{2,1,0:T(8,128)(2,1)S(1)}, bf16[8,80,128]{2,1,0:T(8,128)(2,1)S(1)}, u32[]{:S(2)}, u32[]{:S(2)}) collective-permute-start(bf16[8,80,128]{2,1,0:T(8,128)(2,1)S(1)} %get-tuple-element.31), channel_id=1, source_target_pairs={{0,8},{8,0},{16,24},{24,16},{1,9},{9,1},{17,25},{25,17},{2,10},{10... | collective-permute-start | bytes 491528 | tf_op jit(solution)/shard_map/KE1_13/P41_1/ppermute | solution.py:40
  58.5 1.6 %collective-permute-start.13 = (bf16[8,80,128]{2,1,0:T(8,128)(2,1)S(1)}, bf16[8,80,128]{2,1,0:T(8,128)(2,1)S(1)}, u32[]{:S(2)}, u32[]{:S(2)}) collective-permute-start(bf16[8,80,128]{2,1,0:T(8,128)(2,1)S(1)} %get-tuple-element.32), channel_id=1, source_target_pairs={{0,16},{8,24},{16,0},{24,8},{1,17},{9,25},{17,1},{25,9},{2,18},{10... | collective-permute-start | bytes 491528 | tf_op jit(solution)/shard_map/KE1_13/P42_1/ppermute | solution.py:40
  61.8 2.3 %all-gather.2 = bf16[16,128,128]{2,1,0:T(8,128)(2,1)} all-gather(bf16[8,128,128]{2,1,0:T(8,128)(2,1)S(1)} %butterfly_step.17.refs_7_), channel_id=4, replica_groups={{0,1},{2,3},{4,5},{6,7},{8,9},{10,11},{12,13},{14,15},{16,17},{18,19},{..., dimensions={0}, use_global_device_ids=true | all-gather | bytes 786432 | tf_op jit(solution)/shard_map/K22/all_gather | solution.py:331
  64.2 2.6 %butterfly_step.18 = (bf16[8,80,128]{2,1,0:T(8,128)(2,1)S(1)}, bf16[8,80,128]{2,1,0:T(8,128)(2,1)S(1)}, bf16[8,80,128]{2,1,0:T(8,128)(2,1)S(1)}, bf16[8,80,128]{2,1,0:T(8,128)(2,1)S(1)}, bf16[8,128,128]{2,1,0:T(8,128)(2,1)S(1)}) custom-call(s32[3,8]{1,0:T(4,128)S(1)} %copy-done, bf16[32,1,640,128]{3,2,1,0:T(8,128)(2,1)} %refs_0_.27, ...), custom_call_target="tpu_custom_call" | custom-call | tf_op jit(solution)/shard_map/KE2_23/butterfly_step/pallas_call | solution.py:230
  66.8 1.6 %collective-permute-start.15 = (bf16[8,80,128]{2,1,0:T(8,128)(2,1)S(1)}, bf16[8,80,128]{2,1,0:T(8,128)(2,1)S(1)}, u32[]{:S(2)}, u32[]{:S(2)}) collective-permute-start(bf16[8,80,128]{2,1,0:T(8,128)(2,1)S(1)} %get-tuple-element.35), channel_id=1, source_target_pairs={{0,8},{8,0},{16,24},{24,16},{1,9},{9,1},{17,25},{25,17},{2,10},{10... | collective-permute-start | bytes 491528 | tf_op jit(solution)/shard_map/KE2_23/P41_2/ppermute | solution.py:40
  68.3 1.6 %collective-permute-start.16 = (bf16[8,80,128]{2,1,0:T(8,128)(2,1)S(1)}, bf16[8,80,128]{2,1,0:T(8,128)(2,1)S(1)}, u32[]{:S(2)}, u32[]{:S(2)}) collective-permute-start(bf16[8,80,128]{2,1,0:T(8,128)(2,1)S(1)} %get-tuple-element.36), channel_id=1, source_target_pairs={{0,16},{8,24},{16,0},{24,8},{1,17},{9,25},{17,1},{25,9},{2,18},{10... | collective-permute-start | bytes 491528 | tf_op jit(solution)/shard_map/KE2_23/P42_2/ppermute | solution.py:40
  69.9 2.2 %all-gather.3 = bf16[16,128,128]{2,1,0:T(8,128)(2,1)S(1)} all-gather(bf16[8,128,128]{2,1,0:T(8,128)(2,1)S(1)} %get-tuple-element.29), channel_id=5, replica_groups={{0,1},{2,3},{4,5},{6,7},{8,9},{10,11},{12,13},{14,15},{16,17},{18,19},{..., dimensions={0}, use_global_device_ids=true | all-gather | bytes 786432 | tf_op jit(solution)/shard_map/KE2_23/all_gather | solution.py:331
  72.5 1.9 %butterfly_step.19 = (bf16[8,80,128]{2,1,0:T(8,128)(2,1)S(1)}, bf16[8,80,128]{2,1,0:T(8,128)(2,1)S(1)}, bf16[8,80,128]{2,1,0:T(8,128)(2,1)S(1)}, bf16[8,80,128]{2,1,0:T(8,128)(2,1)S(1)}) custom-call(s32[3,8]{1,0:T(4,128)S(1)} %copy-done, bf16[32,1,640,128]{3,2,1,0:T(8,128)(2,1)} %refs_0_.27, bf16[32,1,640,128]{3,2,1,0:T(8,128)(2,1)} %copy-done.2, ...), custom_call_target="tpu_custom_call" | custom-call | tf_op jit(solution)/shard_map/KE3/butterfly_step/pallas_call | solution.py:230
  74.5 1.6 %collective-permute-start.18 = (bf16[8,80,128]{2,1,0:T(8,128)(2,1)S(1)}, bf16[8,80,128]{2,1,0:T(8,128)(2,1)S(1)}, u32[]{:S(2)}, u32[]{:S(2)}) collective-permute-start(bf16[8,80,128]{2,1,0:T(8,128)(2,1)S(1)} %get-tuple-element.38), channel_id=1, source_target_pairs={{0,8},{8,0},{16,24},{24,16},{1,9},{9,1},{17,25},{25,17},{2,10},{10... | collective-permute-start | bytes 491528 | tf_op jit(solution)/shard_map/KE3/P41_3/ppermute | solution.py:40
  76.0 1.7 %collective-permute-start.19 = (bf16[8,80,128]{2,1,0:T(8,128)(2,1)S(1)}, bf16[8,80,128]{2,1,0:T(8,128)(2,1)S(1)}, u32[]{:S(2)}, u32[]{:S(2)}) collective-permute-start(bf16[8,80,128]{2,1,0:T(8,128)(2,1)S(1)} %get-tuple-element.39), channel_id=1, source_target_pairs={{0,16},{8,24},{16,0},{24,8},{1,17},{9,25},{17,1},{25,9},{2,18},{10... | collective-permute-start | bytes 491528 | tf_op jit(solution)/shard_map/KE3/P42_3/ppermute | solution.py:40
  80.1 2.4 %collective-permute-done.18 = bf16[8,80,128]{2,1,0:T(8,128)(2,1)S(1)} collective-permute-done((bf16[8,80,128]{2,1,0:T(8,128)(2,1)S(1)}, bf16[8,80,128]{2,1,0:T(8,128)(2,1)S(1)}, u32[]{:S(2)}, u32[]{:S(2)}) %collective-permute-start.18) | collective-permute-done | bytes 163872 | tf_op jit(solution)/shard_map/KE3/P41_3/ppermute | solution.py:40
  82.5 2.2 %collective-permute-done.19 = bf16[8,80,128]{2,1,0:T(8,128)(2,1)S(1)} collective-permute-done((bf16[8,80,128]{2,1,0:T(8,128)(2,1)S(1)}, bf16[8,80,128]{2,1,0:T(8,128)(2,1)S(1)}, u32[]{:S(2)}, u32[]{:S(2)}) %collective-permute-start.19) | collective-permute-done | bytes 163872 | tf_op jit(solution)/shard_map/KE3/P42_3/ppermute | solution.py:40
  84.8 1.5 %collective-permute-done.20 = bf16[8,80,128]{2,1,0:T(8,128)(2,1)S(1)} collective-permute-done((bf16[8,80,128]{2,1,0:T(8,128)(2,1)S(1)}, bf16[8,80,128]{2,1,0:T(8,128)(2,1)S(1)}, u32[]{:S(2)}, u32[]{:S(2)}) %collective-permute-start.20) | collective-permute-done | bytes 163872 | tf_op jit(solution)/shard_map/KE3/P43_3/ppermute | solution.py:40
  (53 shorter events, 14.7 us)
Async XLA Ops:
  0.0 8.9 %collective-permute-start = (bf16[32,1,640,128]{3,2,1,0:T(8,128)(2,1)}, bf16[32,1,640,128]{3,2,1,0:T(8,128)(2,1)S(1)}, u32[]{:S(2)}, u32[]{:S(2)}) collective-permute-start(bf16[32,1,640,128]{3,2,1,0:T(8,128)(2,1)} %refs_0_.27), channel_id=1, source_target_pairs={{0,1},{1,0},{2,3},{3,2},{4,5},{5,4},{6,7},{7,6},{8,9},{9,8},{10,11... | collective-permute-start | bytes 15728648 | tf_op jit(solution)/shard_map/KG0/PG_0/ppermute | solution.py:40
  0.5 0.7 copy-start.1
  2.8 16.2 %collective-permute-start.2 = (bf16[8,128,128]{2,1,0:T(8,128)(2,1)S(1)}, bf16[8,128,128]{2,1,0:T(8,128)(2,1)S(1)}, u32[]{:S(2)}, u32[]{:S(2)}) collective-permute-start(bf16[8,128,128]{2,1,0:T(8,128)(2,1)S(1)} %compress_slots.4.refs_3_.refs_2_), channel_id=1, source_target_pairs={{0,4},{1,5},{2,6},{3,7},{4,0},{5,1},{6,2},{7,3},{8,12},{9,13},{10,... | collective-permute-start | bytes 786440 | tf_op jit(solution)/shard_map/KC0/P1_0/ppermute | solution.py:40
  8.9 2.3 %copy-start.2 = (bf16[32,1,640,128]{3,2,1,0:T(8,128)(2,1)}, bf16[32,1,640,128]{3,2,1,0:T(8,128)(2,1)S(1)}, u32[]{:S(2)}) copy-start(bf16[32,1,640,128]{3,2,1,0:T(8,128)(2,1)S(1)} %collective-permute-done.refs_4_.refs_1_) | copy-start | bytes 15728644
  13.0 6.1 %copy-start = (s32[3,8]{1,0:T(4,128)S(1)}, s32[3,8]{1,0:T(4,128)}, u32[]{:S(2)}) copy-start(s32[3,8]{1,0:T(4,128)} %ranks.19) | copy-start | bytes 292
  14.8 17.0 %collective-permute-start.4 = (bf16[8,128,128]{2,1,0:T(8,128)(2,1)S(1)}, bf16[8,128,128]{2,1,0:T(8,128)(2,1)S(1)}, u32[]{:S(2)}, u32[]{:S(2)}) collective-permute-start(bf16[8,128,128]{2,1,0:T(8,128)(2,1)S(1)} %compress_slots.7.refs_4_.refs_2_), channel_id=1, source_target_pairs={{0,4},{1,5},{2,6},{3,7},{4,0},{5,1},{6,2},{7,3},{8,12},{9,13},{10,... | collective-permute-start | bytes 786440 | tf_op jit(solution)/shard_map/KC1/P1_1/ppermute | solution.py:40
  20.4 17.0 %collective-permute-start.3 = (bf16[8,128,128]{2,1,0:T(8,128)(2,1)S(1)}, bf16[8,128,128]{2,1,0:T(8,128)(2,1)S(1)}, u32[]{:S(2)}, u32[]{:S(2)}) collective-permute-start(bf16[8,128,128]{2,1,0:T(8,128)(2,1)S(1)} %butterfly_step.10.refs_4_.refs_2_), channel_id=1, source_target_pairs={{0,2},{1,3},{2,0},{3,1},{4,6},{5,7},{6,4},{7,5},{8,10},{9,11},{10,... | collective-permute-start | bytes 786440 | tf_op jit(solution)/shard_map/K10/P2_0/ppermute | solution.py:40
  21.8 21.1 %collective-permute-start.1 = (bf16[8,128,128]{2,1,0:T(8,128)(2,1)S(1)}, bf16[8,128,128]{2,1,0:T(8,128)(2,1)S(1)}, u32[]{:S(2)}, u32[]{:S(2)}) collective-permute-start(bf16[8,128,128]{2,1,0:T(8,128)(2,1)S(1)} %compress_slots.5.refs_3_.refs_2_), channel_id=1, source_target_pairs={{0,4},{1,5},{2,6},{3,7},{4,0},{5,1},{6,2},{7,3},{8,12},{9,13},{10,... | collective-permute-start | bytes 786440 | tf_op jit(solution)/shard_map/KC2/P1_2/ppermute | solution.py:40
  33.1 15.0 %collective-permute-start.6 = (bf16[8,128,128]{2,1,0:T(8,128)(2,1)S(1)}, bf16[8,128,128]{2,1,0:T(8,128)(2,1)S(1)}, u32[]{:S(2)}, u32[]{:S(2)}) collective-permute-start(bf16[8,128,128]{2,1,0:T(8,128)(2,1)S(1)} %butterfly_step.11.refs_4_.refs_2_), channel_id=1, source_target_pairs={{0,2},{1,3},{2,0},{3,1},{4,6},{5,7},{6,4},{7,5},{8,10},{9,11},{10,... | collective-permute-start | bytes 786440 | tf_op jit(solution)/shard_map/K11/P2_1/ppermute | solution.py:40
  33.9 19.8 %collective-permute-start.7 = (bf16[8,128,128]{2,1,0:T(8,128)(2,1)S(1)}, bf16[8,128,128]{2,1,0:T(8,128)(2,1)S(1)}, u32[]{:S(2)}, u32[]{:S(2)}) collective-permute-start(bf16[8,128,128]{2,1,0:T(8,128)(2,1)S(1)} %compress_slots.6.refs_3_.refs_5_), channel_id=1, source_target_pairs={{0,4},{1,5},{2,6},{3,7},{4,0},{5,1},{6,2},{7,3},{8,12},{9,13},{10,... | collective-permute-start | bytes 786440 | tf_op jit(solution)/shard_map/KC3/P1_3/ppermute | solution.py:40
  44.3 16.2 %collective-permute-start.5 = (bf16[8,128,128]{2,1,0:T(8,128)(2,1)S(1)}, bf16[8,128,128]{2,1,0:T(8,128)(2,1)S(1)}, u32[]{:S(2)}, u32[]{:S(2)}) collective-permute-start(bf16[8,128,128]{2,1,0:T(8,128)(2,1)S(1)} %butterfly_step.14.refs_4_.refs_2_), channel_id=1, source_target_pairs={{0,2},{1,3},{2,0},{3,1},{4,6},{5,7},{6,4},{7,5},{8,10},{9,11},{10,... | collective-permute-start | bytes 786440 | tf_op jit(solution)/shard_map/K12/P2_2/ppermute | solution.py:40
  45.1 11.9 %collective-permute-start.10 = (bf16[8,80,128]{2,1,0:T(8,128)(2,1)S(1)}, bf16[8,80,128]{2,1,0:T(8,128)(2,1)S(1)}, u32[]{:S(2)}, u32[]{:S(2)}) collective-permute-start(bf16[8,80,128]{2,1,0:T(8,128)(2,1)S(1)} %get-tuple-element.27), channel_id=1, source_target_pairs={{0,24},{8,16},{16,8},{24,0},{1,25},{9,17},{17,9},{25,1},{2,26},{10... | collective-permute-start | bytes 491528 | tf_op jit(solution)/shard_map/KE0/P43_0/ppermute | solution.py:40
  47.6 10.9 %collective-permute-start.8 = (bf16[8,80,128]{2,1,0:T(8,128)(2,1)S(1)}, bf16[8,80,128]{2,1,0:T(8,128)(2,1)S(1)}, u32[]{:S(2)}, u32[]{:S(2)}) collective-permute-start(bf16[8,80,128]{2,1,0:T(8,128)(2,1)S(1)} %get-tuple-element.25), channel_id=1, source_target_pairs={{0,8},{8,0},{16,24},{24,16},{1,9},{9,1},{17,25},{25,17},{2,10},{10... | collective-permute-start | bytes 491528 | tf_op jit(solution)/shard_map/KE0/P41_0/ppermute | solution.py:40
  48.1 12.0 %collective-permute-start.9 = (bf16[8,80,128]{2,1,0:T(8,128)(2,1)S(1)}, bf16[8,80,128]{2,1,0:T(8,128)(2,1)S(1)}, u32[]{:S(2)}, u32[]{:S(2)}) collective-permute-start(bf16[8,80,128]{2,1,0:T(8,128)(2,1)S(1)} %get-tuple-element.26), channel_id=1, source_target_pairs={{0,16},{8,24},{16,0},{24,8},{1,17},{9,25},{17,1},{25,9},{2,18},{10... | collective-permute-start | bytes 491528 | tf_op jit(solution)/shard_map/KE0/P42_0/ppermute | solution.py:40
  56.3 7.9 %collective-permute-start.11 = (bf16[8,128,128]{2,1,0:T(8,128)(2,1)S(1)}, bf16[8,128,128]{2,1,0:T(8,128)(2,1)S(1)}, u32[]{:S(2)}, u32[]{:S(2)}) collective-permute-start(bf16[8,128,128]{2,1,0:T(8,128)(2,1)S(1)} %get-tuple-element.28.refs_5_), channel_id=1, source_target_pairs={{0,2},{1,3},{2,0},{3,1},{4,6},{5,7},{6,4},{7,5},{8,10},{9,11},{10,... | collective-permute-start | bytes 786440 | tf_op jit(solution)/shard_map/KE1_13/P2_3/ppermute | solution.py:40
  57.0 15.1 %collective-permute-start.12 = (bf16[8,80,128]{2,1,0:T(8,128)(2,1)S(1)}, bf16[8,80,128]{2,1,0:T(8,128)(2,1)S(1)}, u32[]{:S(2)}, u32[]{:S(2)}) collective-permute-start(bf16[8,80,128]{2,1,0:T(8,128)(2,1)S(1)} %get-tuple-element.31), channel_id=1, source_target_pairs={{0,8},{8,0},{16,24},{24,16},{1,9},{9,1},{17,25},{25,17},{2,10},{10... | collective-permute-start | bytes 491528 | tf_op jit(solution)/shard_map/KE1_13/P41_1/ppermute | solution.py:40
  58.5 14.0 %collective-permute-start.13 = (bf16[8,80,128]{2,1,0:T(8,128)(2,1)S(1)}, bf16[8,80,128]{2,1,0:T(8,128)(2,1)S(1)}, u32[]{:S(2)}, u32[]{:S(2)}) collective-permute-start(bf16[8,80,128]{2,1,0:T(8,128)(2,1)S(1)} %get-tuple-element.32), channel_id=1, source_target_pairs={{0,16},{8,24},{16,0},{24,8},{1,17},{9,25},{17,1},{25,9},{2,18},{10... | collective-permute-start | bytes 491528 | tf_op jit(solution)/shard_map/KE1_13/P42_1/ppermute | solution.py:40
  60.1 12.4 %collective-permute-start.14 = (bf16[8,80,128]{2,1,0:T(8,128)(2,1)S(1)}, bf16[8,80,128]{2,1,0:T(8,128)(2,1)S(1)}, u32[]{:S(2)}, u32[]{:S(2)}) collective-permute-start(bf16[8,80,128]{2,1,0:T(8,128)(2,1)S(1)} %get-tuple-element.33), channel_id=1, source_target_pairs={{0,24},{8,16},{16,8},{24,0},{1,25},{9,17},{17,9},{25,1},{2,26},{10... | collective-permute-start | bytes 491528 | tf_op jit(solution)/shard_map/KE1_13/P43_1/ppermute | solution.py:40
  66.8 11.6 %collective-permute-start.15 = (bf16[8,80,128]{2,1,0:T(8,128)(2,1)S(1)}, bf16[8,80,128]{2,1,0:T(8,128)(2,1)S(1)}, u32[]{:S(2)}, u32[]{:S(2)}) collective-permute-start(bf16[8,80,128]{2,1,0:T(8,128)(2,1)S(1)} %get-tuple-element.35), channel_id=1, source_target_pairs={{0,8},{8,0},{16,24},{24,16},{1,9},{9,1},{17,25},{25,17},{2,10},{10... | collective-permute-start | bytes 491528 | tf_op jit(solution)/shard_map/KE2_23/P41_2/ppermute | solution.py:40
  68.3 10.5 %collective-permute-start.16 = (bf16[8,80,128]{2,1,0:T(8,128)(2,1)S(1)}, bf16[8,80,128]{2,1,0:T(8,128)(2,1)S(1)}, u32[]{:S(2)}, u32[]{:S(2)}) collective-permute-start(bf16[8,80,128]{2,1,0:T(8,128)(2,1)S(1)} %get-tuple-element.36), channel_id=1, source_target_pairs={{0,16},{8,24},{16,0},{24,8},{1,17},{9,25},{17,1},{25,9},{2,18},{10... | collective-permute-start | bytes 491528 | tf_op jit(solution)/shard_map/KE2_23/P42_2/ppermute | solution.py:40
  72.1 7.9 %collective-permute-start.17 = (bf16[8,80,128]{2,1,0:T(8,128)(2,1)S(1)}, bf16[8,80,128]{2,1,0:T(8,128)(2,1)S(1)}, u32[]{:S(2)}, u32[]{:S(2)}) collective-permute-start(bf16[8,80,128]{2,1,0:T(8,128)(2,1)S(1)} %get-tuple-element.37), channel_id=1, source_target_pairs={{0,24},{8,16},{16,8},{24,0},{1,25},{9,17},{17,9},{25,1},{2,26},{10... | collective-permute-start | bytes 491528 | tf_op jit(solution)/shard_map/KE2_23/P43_2/ppermute | solution.py:40
  74.5 8.1 %collective-permute-start.18 = (bf16[8,80,128]{2,1,0:T(8,128)(2,1)S(1)}, bf16[8,80,128]{2,1,0:T(8,128)(2,1)S(1)}, u32[]{:S(2)}, u32[]{:S(2)}) collective-permute-start(bf16[8,80,128]{2,1,0:T(8,128)(2,1)S(1)} %get-tuple-element.38), channel_id=1, source_target_pairs={{0,8},{8,0},{16,24},{24,16},{1,9},{9,1},{17,25},{25,17},{2,10},{10... | collective-permute-start | bytes 491528 | tf_op jit(solution)/shard_map/KE3/P41_3/ppermute | solution.py:40
  76.0 8.7 %collective-permute-start.19 = (bf16[8,80,128]{2,1,0:T(8,128)(2,1)S(1)}, bf16[8,80,128]{2,1,0:T(8,128)(2,1)S(1)}, u32[]{:S(2)}, u32[]{:S(2)}) collective-permute-start(bf16[8,80,128]{2,1,0:T(8,128)(2,1)S(1)} %get-tuple-element.39), channel_id=1, source_target_pairs={{0,16},{8,24},{16,0},{24,8},{1,17},{9,25},{17,1},{25,9},{2,18},{10... | collective-permute-start | bytes 491528 | tf_op jit(solution)/shard_map/KE3/P42_3/ppermute | solution.py:40
  78.4 7.9 %collective-permute-start.20 = (bf16[8,80,128]{2,1,0:T(8,128)(2,1)S(1)}, bf16[8,80,128]{2,1,0:T(8,128)(2,1)S(1)}, u32[]{:S(2)}, u32[]{:S(2)}) collective-permute-start(bf16[8,80,128]{2,1,0:T(8,128)(2,1)S(1)} %get-tuple-element.40), channel_id=1, source_target_pairs={{0,24},{8,16},{16,8},{24,0},{1,25},{9,17},{17,9},{25,1},{2,26},{10... | collective-permute-start | bytes 491528 | tf_op jit(solution)/shard_map/KE3/P43_3/ppermute | solution.py:40
  84.8 1.5 %copy-start.3 = (bf16[128,1,1,80,128]{4,3,2,1,0:T(8,128)(2,1)}, bf16[128,1,1,80,128]{4,3,2,1,0:T(8,128)(2,1)S(1)}, u32[]{:S(2)}) copy-start(bf16[128,1,1,80,128]{4,3,2,1,0:T(8,128)(2,1)S(1)} %bitcast_dynamic-update-slice_fusion.1) | copy-start | bytes 7864324
